TPU v7x, 512 devices: a whole 4x4x16 slice. The times are simulated.
512 devices in a mesh: step: 32 (over z, core), seq: 16 (over y, x).
Axes of the slice: x: 4, y: 4, z: 16, core: 2. Of those that a mesh axis runs over, the one named last changes fastest.
Arguments:
- start_latent: float32 [1024, 64], P('seq')
- timesteps: int32 [33], replicated, may hold values from 213 to 949, as said below
- modulation: bfloat16 [32, 3072], P('step'), may hold values from -3 to 3
- w_in: bfloat16 [64, 1536], replicated, may hold values from -0.75 to 0.75
- w_qkv: bfloat16 [1536, 3072], P('step')
- w_o: bfloat16 [1024, 1536], P('step'), may hold values from -0.1875 to 0.1875
- w_out: bfloat16 [1536, 64], replicated, may hold values from -0.15625 to 0.15625
Outputs:
- window_latents: float32 [32, 1024, 64], P('step', 'seq')
- errors: float32 [32], P('step')
Inputs may be any that keep to these rules, and one draw needn't show every extreme that they name: timesteps starts at 949 and falls by 6 to 23 from each entry to the next.
All inputs are finite; a program needn't handle non-finite values.
Results may differ from a plain program's by a relative error of at most 0.0017.
Values may be sent and summed in bfloat16 or wider, within the bound.
No kernel may reach another device: no remote copies, remote signals or barrier semaphores. Data moves between devices by JAX's collectives and lax.ppermute only.
A program may use at most 64 MiB of HBM per device.

v0:
```python
import math

import jax
import jax.numpy as jnp
from jax import lax
from jax.sharding import PartitionSpec as P

D = 1536
HEADS = 8
HEAD_DIM = 128
SWEEPS = 2
INNER = 1024


def alpha_bar(steps_in):
    angle = (steps_in.astype(jnp.float32) / 1000.0 + 0.008) / 1.008 * (math.pi / 2)
    return jnp.cos(angle) ** 2


def layer_norm(values):
    center = values - jnp.mean(values, axis=-1, keepdims=True)
    spread = jnp.mean(center * center, axis=-1, keepdims=True)
    return center * lax.rsqrt(spread + 1e-06)


def fold_block(carry, piece, query):
    top, total, acc = carry
    key_piece, value_piece = piece
    count = key_piece.shape[0]
    head_count = query.shape[1]
    head_size = query.shape[2]
    key_heads = key_piece.reshape(count, head_count, head_size)
    value_heads = value_piece.reshape(count, head_count, head_size)
    scores = jnp.einsum("qhd,khd->qhk", query, key_heads, preferred_element_type=jnp.float32)
    scores = scores * (1.0 / math.sqrt(HEAD_DIM))
    new_top = jnp.maximum(top, jnp.max(scores, axis=-1))
    weights = jnp.exp(scores - new_top[:, :, None])
    total = jnp.sum(weights, axis=-1)
    update = jnp.einsum(
        "qhk,khd->qhd",
        weights.astype(jnp.bfloat16),
        value_heads,
        preferred_element_type=jnp.float32,
    )
    acc = update
    return (new_top, total, acc)


def empty_carry(rows, head_count):
    return (
        jnp.full((rows, head_count), -1e30, jnp.float32),
        jnp.zeros((rows, head_count), jnp.float32),
        jnp.zeros((rows, head_count, HEAD_DIM), jnp.float32),
    )


def predict(latent, mod_row, w_in, whole_qkv, whole_o, w_out):
    rows = latent.shape[0]
    embed = jnp.dot(latent.astype(jnp.bfloat16), w_in, preferred_element_type=jnp.float32)
    shift = mod_row[:D].astype(jnp.float32)
    gain = mod_row[D:].astype(jnp.float32)
    hidden = (layer_norm(embed) * (1.0 + gain) + shift).astype(jnp.bfloat16)
    qkv = jnp.dot(hidden, whole_qkv, preferred_element_type=jnp.float32).astype(jnp.bfloat16)
    query_flat = qkv[:, :INNER]
    query = query_flat.reshape(rows, HEADS, HEAD_DIM)
    keys = qkv[:, INNER : 2 * INNER]
    values = qkv[:, 2 * INNER :]
    all_keys, all_values = (
        lax.all_gather(keys, "seq", axis=0, tiled=True),
        lax.all_gather(values, "seq", axis=0, tiled=True),
    )
    top, total, acc = fold_block(empty_carry(rows, HEADS), (all_keys, all_values), query)
    heads = (acc / total[:, :, None]).astype(jnp.bfloat16).reshape(rows, INNER)
    attended = jnp.dot(heads, whole_o, preferred_element_type=jnp.float32)
    resid = (embed + attended).astype(jnp.bfloat16)
    return jnp.dot(resid, w_out, preferred_element_type=jnp.float32)


def body(start_latent, timesteps, modulation, w_in, w_qkv, w_o, w_out):
    whole_qkv, whole_o = (
        lax.all_gather(w_qkv, "step", axis=0, tiled=True),
        lax.all_gather(w_o, "step", axis=0, tiled=True),
    )
    index = lax.axis_index("step")
    pair = lax.dynamic_slice_in_dim(timesteps, index, 2)
    abar = alpha_bar(pair)
    keep = jnp.sqrt(abar[1] / abar[0])
    noise = jnp.sqrt(1.0 - abar[1]) - keep * jnp.sqrt(1.0 - abar[0])
    is_first = index == 0
    mod_row = modulation[0]
    latent = start_latent
    previous = latent
    for sweep in range(SWEEPS):
        eps = predict(latent, mod_row, w_in, whole_qkv, whole_o, w_out)
        drift = (keep - 1.0) * latent + noise * eps
        term = drift + jnp.where(is_first, latent, jnp.zeros_like(latent))
        every = lax.all_gather(term[None], "step", axis=0, tiled=True)
        below = jnp.arange(every.shape[0]) < index
        prefix = jnp.sum(jnp.where(below[:, None, None], every, 0.0), axis=0)
        fresh = jnp.where(is_first, latent, prefix)
        previous, latent = (latent, fresh)
    change = latent - previous
    squared = lax.psum(jnp.sum(change * change), "seq")
    entries = latent.shape[0] * lax.axis_size("seq") * latent.shape[1]
    errors = jnp.sqrt(squared / entries + 1e-06).reshape(1)
    return (latent[None], errors)


def solution(mesh):
    return jax.shard_map(
        body,
        mesh=mesh,
        in_specs=(P("seq", None), P(), P("step", None), P(), P("step", None), P("step", None), P()),
        out_specs=(P("step", "seq", None), P("step")),
        check_vma=False,
    )
```

profile of v0, /device:TPU:1, one launch (start us, length us, event | category | flops | bytes accessed | tf_op | source)
XLA Modules:
  0.0 539.6 jit_solution(5159006024612734211)
XLA Ops:
  7.2 0.0 copy-start
  7.2 0.0 all-gather.9.cloned.1.call-start
  7.2 0.7 all-gather.9.cloned.1.call-update
  7.9 0.0 all-gather.13.cloned.1.call-start
  8.0 0.7 add_reduce_fusion
  8.7 0.0 copy-done
  8.7 1.0 fusion.85
  9.8 0.2 multiply_reduce_fusion.1
  10.0 86.7 %all-gather.9.cloned.1.call-done = bf16[1536,3072]{1,0:T(8,128)(2,1)} async-done(((bf16[48,3072]{1,0:T(8,128)(2,1)}), bf16[1536,3072]{1,0:T(8,128)(2,1)}) %all-gather.9.cloned.1.call-update) | async-done | bytes 9437200 | tf_op jit(solution)/shard_map/all_gather | solution.py:81
  96.7 0.0 copy-start.7
  96.7 5.5 %convolution_convert_fusion.1 = bf16[64,3072]{1,0:T(8,128)(2,1)S(1)} fusion(bf16[1536,3072]{1,0:T(8,128)(2,1)} %all-gather.9.cloned.1.call-done, f32[64,1536]{1,0:T(8,128)S(1)} %get-tuple-element.15, f32[1536]{0:T(1024)S(1)} %get-tuple-element.3, f32[1536]{0:T(1024)S(1)} %get-tuple-element.2, f32[64]{0:T(128)S(1)} %add_rsqrt_fusion.1, ...), kind=kOutput, calls=%fused_computation.1 | convolution fusion | flops 604667904 | bytes 10236416 | tf_op jit(solution)/shard_map/dot_general | solution.py:63
  102.2 0.7 slice_bitcast_fusion.1
  103.0 0.0 all-gather.13.cloned.1.call-update
  103.0 0.0 all-gather.11.cloned.1.call-start
  103.1 0.7 all-gather.11.cloned.1.call-update
  103.7 0.0 all-gather.15.cloned.1.call-start
  103.8 0.5 all-gather.15.cloned.1.call-update
  104.3 0.0 all-gather.19.cloned.1.call-start
  104.4 0.0 copy-done.7
  104.4 0.1 cosine_multiply_fusion
  104.5 0.6 fusion.84
  107.9 49.8 %all-gather.13.cloned.1.call-done = bf16[1024,1024]{1,0:T(8,128)(2,1)} async-done(((bf16[64,1024]{1,0:T(8,128)(2,1)}), bf16[1024,1024]{1,0:T(8,128)(2,1)}) %all-gather.13.cloned.1.call-update) | async-done | bytes 2097168 | tf_op jit(solution)/shard_map/all_gather | solution.py:69
  157.7 2.5 bitcast_reduce_fusion.1
  160.2 0.5 fusion.16
  160.8 0.0 copy-start.3
  160.8 0.0 copy-start.6
  160.8 59.7 %all-gather.11.cloned.1.call-done = bf16[1024,1024]{1,0:T(8,128)(2,1)} async-done(((bf16[64,1024]{1,0:T(8,128)(2,1)}), bf16[1024,1024]{1,0:T(8,128)(2,1)}) %all-gather.11.cloned.1.call-update) | async-done | bytes 2097168 | tf_op jit(solution)/shard_map/all_gather | solution.py:70
  220.5 2.4 fusion.43
  222.9 73.3 %all-gather.15.cloned.1.call-done = bf16[1024,1536]{1,0:T(8,128)(2,1)} async-done(((bf16[32,1536]{1,0:T(8,128)(2,1)}), bf16[1024,1536]{1,0:T(8,128)(2,1)}) %all-gather.15.cloned.1.call-update) | async-done | bytes 3145744 | tf_op jit(solution)/shard_map/all_gather | solution.py:82
  296.2 0.0 copy-done.3
  296.2 0.0 copy-done.6
  296.2 2.7 fusion.48
  298.9 32.4 %all-gather = f32[2048,64]{1,0:T(8,128)S(1)} all-gather(f32[64,64]{1,0:T(8,128)S(1)} %fusion.48), channel_id=2, replica_groups=mesh['step'=32,'seq'=16] {'step'}, dimensions={0}, use_global_device_ids=true | all-gather | bytes 540672 | tf_op jit(solution)/shard_map/all_gather | solution.py:97
  331.3 0.2 select_reduce_fusion.1
  331.5 0.0 copy-start.4
  331.5 0.6 copy-done.4
  332.1 0.3 fusion.86
  332.4 0.0 copy-start.2
  332.4 0.2 multiply_reduce_fusion
  332.6 5.5 %convolution_convert_fusion = bf16[64,3072]{1,0:T(8,128)(2,1)S(1)} fusion(bf16[1536,3072]{1,0:T(8,128)(2,1)} %all-gather.9.cloned.1.call-done, f32[64,1536]{1,0:T(8,128)S(1)} %get-tuple-element.19, f32[64]{0:T(128)S(1)} %add_rsqrt_fusion, f32[64]{0:T(128)S(1)} %broadcast_multiply_fusion, f32[1536]{0:T(1024)S(1)} %get-tuple-element.3, ...), kind=kOutput, calls=%fused_computation | convolution fusion | flops 604667904 | bytes 10236416 | tf_op jit(solution)/shard_map/dot_general | solution.py:63
  338.1 0.0 copy-done.2
  338.1 0.7 slice_bitcast_fusion
  338.9 0.0 all-gather.19.cloned.1.call-update
  338.9 0.0 all-gather.17.cloned.1.call-start
  338.9 0.5 all-gather.17.cloned.1.call-update
  339.5 54.1 %all-gather.19.cloned.1.call-done = bf16[1024,1024]{1,0:T(8,128)(2,1)} async-done(((bf16[64,1024]{1,0:T(8,128)(2,1)}), bf16[1024,1024]{1,0:T(8,128)(2,1)}) %all-gather.19.cloned.1.call-update) | async-done | bytes 2097168 | tf_op jit(solution)/shard_map/all_gather | solution.py:69
  393.6 3.7 bitcast_reduce_fusion
  397.4 2.1 fusion.18
  399.5 0.0 copy-start.1
  399.5 56.8 %all-gather.17.cloned.1.call-done = bf16[1024,1024]{1,0:T(8,128)(2,1)} async-done(((bf16[64,1024]{1,0:T(8,128)(2,1)}), bf16[1024,1024]{1,0:T(8,128)(2,1)}) %all-gather.17.cloned.1.call-update) | async-done | bytes 2097168 | tf_op jit(solution)/shard_map/all_gather | solution.py:70
  456.2 3.7 fusion.40
  459.9 0.0 copy-done.1
  459.9 2.4 fusion.51
  462.3 0.0 copy-start.5
  462.3 35.6 %all-gather.1 = f32[2048,64]{1,0:T(8,128)S(1)} all-gather(f32[64,64]{1,0:T(8,128)} %fusion.51), channel_id=3, replica_groups=mesh['step'=32,'seq'=16] {'step'}, dimensions={0}, use_global_device_ids=true | all-gather | bytes 540672 | tf_op jit(solution)/shard_map/all_gather | solution.py:97
  497.9 0.2 select_reduce_fusion
  498.1 0.0 copy-done.5
  498.1 1.2 multiply_reduce_fusion.2
  499.3 31.6 %psum.7 = f32[]{:T(128)} all-reduce(f32[]{:T(128)} %get-tuple-element.10), channel_id=1, replica_groups=mesh['step'=32,'seq'=16] {'seq'}, use_global_device_ids=true, to_apply=%region_11.12 | all-reduce | flops 1 | bytes 8 | tf_op jit(solution)/shard_map/psum | solution.py:103
  (8 shorter events, 0.0 us)
Async XLA Ops:
  7.2 1.5 copy-start
  7.2 89.5 %all-gather.9.cloned.1.call-start = ((), (), s32[]{:S(2)}) async-start(), calls=%async_computation | async-start | bytes 9732096 | tf_op jit(solution)/shard_map/all_gather | solution.py:81
  7.9 149.8 %all-gather.13.cloned.1.call-start = ((), (), s32[]{:S(2)}) async-start(), calls=%async_computation.2 | async-start | bytes 2228224 | tf_op jit(solution)/shard_map/all_gather | solution.py:69
  96.7 7.7 %copy-start.7 = (s32[33]{0:T(128)S(1)}, s32[33]{0:T(128)}, u32[]{:S(2)}) copy-start(s32[33]{0:T(128)} %param.8) | copy-start | bytes 400
  103.0 117.5 %all-gather.11.cloned.1.call-start = ((), (), s32[]{:S(2)}) async-start(), calls=%async_computation.1 | async-start | bytes 2228224 | tf_op jit(solution)/shard_map/all_gather | solution.py:70
  103.7 192.4 %all-gather.15.cloned.1.call-start = ((), (), s32[]{:S(2)}) async-start(), calls=%async_computation.3 | async-start | bytes 3244032 | tf_op jit(solution)/shard_map/all_gather | solution.py:82
  104.3 289.3 %all-gather.19.cloned.1.call-start = ((), (), s32[]{:S(2)}) async-start(), calls=%async_computation.5 | async-start | bytes 2228224 | tf_op jit(solution)/shard_map/all_gather | solution.py:69
  160.8 135.4 %copy-start.3 = (bf16[1536,64]{0,1:T(8,128)(2,1)S(1)}, bf16[1536,64]{0,1:T(8,128)(2,1)}, u32[]{:S(2)}) copy-start(bf16[1536,64]{0,1:T(8,128)(2,1)} %param.13) | copy-start | bytes 589828
  160.8 135.4 %copy-start.6 = (f32[64,64]{1,0:T(8,128)S(1)}, f32[64,64]{1,0:T(8,128)}, u32[]{:S(2)}) copy-start(f32[64,64]{1,0:T(8,128)} %param.7) | copy-start | bytes 49156
  331.5 0.6 copy-start.4
  332.4 5.8 %copy-start.2 = (f32[64,1536]{1,0:T(8,128)}, f32[64,1536]{1,0:T(8,128)S(1)}, u32[]{:S(2)}) copy-start(f32[64,1536]{1,0:T(8,128)S(1)} %get-tuple-element.19) | copy-start | bytes 1179652
  338.9 117.3 %all-gather.17.cloned.1.call-start = ((), (), s32[]{:S(2)}) async-start(), calls=%async_computation.4 | async-start | bytes 2228224 | tf_op jit(solution)/shard_map/all_gather | solution.py:70
  399.5 60.5 %copy-start.1 = (bf16[1024,1536]{1,0:T(8,128)(2,1)S(1)}, bf16[1024,1536]{1,0:T(8,128)(2,1)}, u32[]{:S(2)}) copy-start(bf16[1024,1536]{1,0:T(8,128)(2,1)} %all-gather.15.cloned.1.call-done) | copy-start | bytes 9437188
  462.3 35.7 %copy-start.5 = (f32[64,64]{1,0:T(8,128)S(1)}, f32[64,64]{1,0:T(8,128)}, u32[]{:S(2)}) copy-start(f32[64,64]{1,0:T(8,128)} %copy-done.4) | copy-start | bytes 49156
Sparse Core Ops, SparseCore 0:
  10.1 86.5 all-gather.8
  103.1 54.5 all-gather.12
  160.7 59.6 all-gather.10
  222.4 73.7 all-gather.14
  339.0 54.5 all-gather.18
  396.5 59.6 all-gather.16
where the time goes:
time: 544 us; the launch traced here: 540 us
  waiting for transfers between devices  383 us (70%)
  blocking collectives  99.6 us (18%)
  matrix products  29.9 us (5%)
  between operations  18.9 us (3%)
  other arithmetic  5.5 us (1%)
    all_gather x2, waiting for transfers between devices, predict(): lax.all_gather(values, 'seq', axis=0, tiled=True)  116 us
    all_gather x2, waiting for transfers between devices, predict(): lax.all_gather(keys, 'seq', axis=0, tiled=True)  104 us
    all_gather x1, waiting for transfers between devices, body(): lax.all_gather(w_qkv, 'step', axis=0, tiled=True)  86.7 us
    all_gather x1, waiting for transfers between devices, body(): lax.all_gather(w_o, 'step', axis=0, tiled=True)  73.3 us
    all_gather x2, blocking collectives, body(): every = lax.all_gather(term[None], 'step', axis=0, tiled=True)  67.9 us
    psum x1, blocking collectives, body(): squared = lax.psum(jnp.sum(change * change), 'seq')  31.6 us
    dot_general x2, matrix products, predict(): jnp.dot(hidden, whole_qkv, preferred_element_type=jnp.float32)  11.1 us
  transfers between devices with their start and end apart: 6, of which 6 were waited for; matrix products, arithmetic and copies ran while one was open for 3% of the time, Pallas kernels for 0%

commit v1 on v0

v1 whole, which is shorter than its diff:
```python
import math

import jax
import jax.numpy as jnp
from jax import lax
from jax.experimental import pallas as pl
from jax.experimental.pallas import tpu as pltpu
from jax.sharding import Mesh
from jax.sharding import PartitionSpec as P

D = 1536
HEADS = 8
HEAD_DIM = 128
C = 64
INNER = 1024
STEPS = 32
TOKENS = 1024
Z = 16
PEERS = 32
ROWS = 48
FLAT = ("core", "y", "x")
BF = jnp.bfloat16
F32 = jnp.float32
NT = (((1,), (1,)), ((), ()))
SCALE = 1.0 / (math.sqrt(HEAD_DIM) * math.log(2.0))


def place():
    return lax.axis_index("z"), lax.axis_index("core"), lax.axis_index("y") * 4 + lax.axis_index("x")


def lanes(shape):
    return lax.broadcasted_iota(jnp.int32, shape, len(shape) - 1)


def rows(shape):
    return lax.broadcasted_iota(jnp.int32, shape, 0)


def dot(a, b):
    return jnp.dot(a, b, preferred_element_type=F32)


def unpack(packed):
    low = lanes(packed.shape) < C
    return jnp.concatenate([jnp.where(low, packed, 0.0), jnp.where(low, pltpu.roll(packed, C, 1), 0.0)], axis=0)


def pack_high(values):
    half = values.shape[0] // 2
    low = lanes((half, 2 * C)) < C
    return jnp.where(low, pltpu.roll(values[:half], C, 1), values[half:])


def split_of(values, count):
    pieces = []
    for _ in range(count):
        piece = values.astype(BF)
        pieces.append(piece)
        values = values - piece.astype(F32)
    return pieces


def call(kernel, outs, args, scratch=(), smem=()):
    return pl.pallas_call(
        kernel,
        out_shape=outs,
        in_specs=[pl.BlockSpec(memory_space=pltpu.SMEM if at in smem else pltpu.VMEM) for at in range(len(args))],
        out_specs=jax.tree.map(lambda _: pl.BlockSpec(memory_space=pltpu.VMEM), outs),
        scratch_shapes=scratch,
        compiler_params=pltpu.CompilerParams(vmem_limit_bytes=40 * 1024 * 1024),
    )(*args)


def shape(dims, kind):
    return jax.ShapeDtypeStruct(dims, kind)


def send_weights(w_qkv, w_o, w_out, out):
    _, _, seq = place()
    odd = lax.rem(seq, 2) == 1

    def columns(base):
        start = pl.multiple_of(base + (seq // 2) * HEAD_DIM, HEAD_DIM)
        block = w_qkv[:, pl.ds(start, HEAD_DIM)].astype(F32)
        return jnp.where(odd, block[:, C:], block[:, :C])

    head = dot(w_o[...], w_out[...])
    head = jnp.concatenate([head, jnp.zeros((ROWS - head.shape[0], C), F32)], axis=0)
    first = jnp.concatenate([columns(0), columns(INNER)], axis=1).astype(BF)
    second = jnp.concatenate([columns(2 * INNER), head], axis=1).astype(BF)
    for to in range(Z):
        out[to, 0:ROWS, :] = first
        out[to, ROWS : 2 * ROWS, :] = second


def make_tables(own, peer, w_in, w_out, modulation, start, out, table, left, qk, vw):
    _, core, seq = place()
    for z in range(Z):
        for source, parity in ((own, core), (peer, 1 - core)):
            at = pl.ds(pl.multiple_of(z * 2 * ROWS + parity * ROWS, 16), ROWS)
            qk[at, :] = source[z, 0:ROWS, :]
            vw[at, :] = source[z, ROWS : 2 * ROWS, :]
    w = w_in[...].astype(F32)
    centred = w - jnp.mean(w, axis=1, keepdims=True)
    shift = modulation[:, 0:D].astype(F32)
    gain = modulation[:, D : 2 * D].astype(F32)
    left[0:C, :] = (centred * (1.0 + gain)).astype(BF)
    left[C : C + 16, :] = jnp.where(rows((16, D)) == 0, shift, 0.0).astype(BF)
    first = dot(left[...], qk[...])
    value = dot(left[...], vw[...])[:, :C]
    query, key = first[:, :C], first[:, C:]
    mine = own[seq, ROWS : ROWS + 32, C:].astype(F32)
    other = peer[seq, ROWS : ROWS + 32, C:].astype(F32)
    even = core == 0
    head = jnp.concatenate([jnp.where(even, mine, other), jnp.where(even, other, mine)], axis=0)
    best = lax.Precision.HIGHEST
    a = lax.dot_general(query, key, NT, precision=best, preferred_element_type=F32) * SCALE
    b = jnp.dot(value, head, precision=best, preferred_element_type=F32)
    bias = lax.dot_general(key[C : C + 8], query, NT, precision=best, preferred_element_type=F32) * SCALE
    bias = jnp.concatenate([bias, jnp.zeros((8, 128 - bias.shape[1]), F32)], axis=1)[0:1]
    main = jnp.concatenate([a[:, :C], b], axis=1)
    main = jnp.where(rows(main.shape) == C + 1, bias, main).astype(BF)
    x = start[pl.ds(pl.multiple_of(core * 32, 32), 32), :]
    x = jnp.concatenate([x[:16], x[16:]], axis=1).astype(BF)
    for to in range(PEERS):
        out[to, 0:80, :] = main
        out[to, 80:96, :] = x
    gram = lax.dot_general(centred, centred, NT, precision=best, preferred_element_type=F32) / D
    direct = dot(w_in[...], w_out[...])
    pad = jnp.zeros((C, C), F32)
    below = jnp.zeros((C, 2 * C), BF)
    gram = jnp.concatenate([gram, pad], axis=1)
    direct = jnp.concatenate([pad, direct], axis=1)
    for at, piece in enumerate(split_of(gram, 3) + split_of(direct, 2)):
        table[at, 0:C, :] = piece
        table[at, C : 2 * C, :] = below


def normalized(x, table):
    exact = x.astype(BF)
    y = dot(exact, table[0]) + dot(exact, table[1]) + dot(exact, table[2])
    spread = jnp.sum(x * y, axis=1, keepdims=True)
    return jnp.where(lanes(x.shape) == C, 1.0, x * lax.rsqrt(spread + 1e-06))


def attend(steps, heads, table, x, work):
    query_ref, key_ref, weight_ref, mixed_ref, direct_ref = work
    count = x.shape[0]
    span = HEADS * count
    mine = normalized(x, table)
    short = mine.astype(BF)
    lane = lanes((count, 128))
    exact = x.astype(BF)
    direct_ref[...] = dot(exact, table[3]) + dot(exact, table[4])
    results = []
    for step in steps:
        for head in range(HEADS):
            both = heads[step * HEADS + head]
            grown = dot(short, both)
            constant = jnp.sum(mine * both[C : C + 16].astype(F32)[1:2], axis=1, keepdims=True)
            grown = jnp.where(lane < C, grown, jnp.where(lane == C, constant, 0.0)).astype(BF)
            query_ref[step, head * count : (head + 1) * count, :] = grown
        scores = lax.dot_general(query_ref[step], key_ref[...], NT, preferred_element_type=F32)
        weight_ref[step] = jnp.exp2(scores - jnp.max(scores, axis=1, keepdims=True)).astype(BF)
        mixed = dot(weight_ref[step], key_ref[...])
        mixed_ref[step] = (mixed / mixed[:, C : C + 1]).astype(BF)
        eps = jnp.zeros((count, 128), F32)
        for head in range(HEADS):
            eps = eps + dot(mixed_ref[step, head * count : (head + 1) * count, :], heads[step * HEADS + head])
        results.append(pack_high(eps + direct_ref[...]))
    return results


def work_space():
    return (
        pltpu.VMEM((2, HEADS * 32, 128), BF),
        pltpu.VMEM((TOKENS, 128), BF),
        pltpu.VMEM((2, HEADS * 32, TOKENS), BF),
        pltpu.VMEM((2, HEADS * 32, 128), BF),
        pltpu.VMEM((32, 128), F32),
    )


def first_sweep(coef, got, start, table, heads, first_eps, out, *work):
    _, core, _ = place()
    for at in range(2 * HEADS):
        source = 2 * at
        both = got[source, 0:80, :].astype(F32) + got[source + 1, 0:80, :].astype(F32)
        heads[at, 0:80, :] = both.astype(BF)
        heads[at, 80:128, :] = jnp.zeros((48, 128), BF)
    x = start[pl.ds(pl.multiple_of(core * 32, 32), 32), :].astype(BF).astype(F32)
    x = jnp.concatenate([x, jnp.zeros_like(x)], axis=1)
    everything = got[:, 80:96, :].astype(F32).reshape(PEERS * 16, 128)
    work[1][...] = normalized(unpack(everything), table).astype(BF)
    eps = attend((0, 1), heads, table, x, work)
    first_eps[...] = eps[0]
    both = (coef[2] * eps[0] + coef[3] * eps[1]).astype(BF)
    for to in range(Z):
        out[to] = both


def packed_start(start, core):
    x = start[pl.ds(pl.multiple_of(core * 32, 32), 32), :]
    return jnp.concatenate([x[:16], x[16:]], axis=1)


def below(got, z):
    total = jnp.zeros((16, 128), F32)
    for at in range(Z):
        total = total + jnp.where(at < z, got[at].astype(F32), 0.0)
    return total


def first_prefix(coef, got, start, first_eps, latents, out):
    z, core, _ = place()
    x = packed_start(start, core)
    even = x + coef[4] * x + below(got, z)
    odd = even + coef[0] * x + coef[2] * first_eps[...]
    latents[0] = even
    latents[1] = odd
    for to in range(PEERS):
        out[to, 0:16, :] = even.astype(BF)
        out[to, 16:32, :] = odd.astype(BF)


def second_sweep(coef, got, latents, table, heads, term, out, *work):
    terms = []
    for step in range(2):
        everything = got[:, 16 * step : 16 * step + 16, :].astype(F32).reshape(PEERS * 16, 128)
        work[1][...] = normalized(unpack(everything), table).astype(BF)
        latent = latents[step]
        x = unpack(latent.astype(BF).astype(F32))
        eps = attend((step,), heads, table, x, work)[0]
        terms.append(coef[step] * latent + coef[2 + step] * eps)
    term[...] = terms[0]
    both = terms[0] + terms[1]
    for to in range(Z):
        out[to] = both


def second_prefix(got, start, latents, term, out):
    z, core, _ = place()
    even = packed_start(start, core) + below(got, z)
    fresh = (even, even + term[...])
    for step in range(2):
        change = fresh[step] - latents[step]
        squared = change * change
        squared = squared[:8] + squared[8:]
        for to in range(PEERS // 2):
            out[step * 16 + to, 0:16, :] = fresh[step]
            out[step * 16 + to, 16:24, :] = squared


def finish(got, window, errors):
    _, _, seq = place()
    for half in range(2):
        packed = got[half * 16 + seq, 0:16, :]
        window[0, half * 32 : half * 32 + 16, :] = packed[:, :C]
        window[0, half * 32 + 16 : half * 32 + 32, :] = packed[:, C:]
    total = got[0, 16:24, :]
    for at in range(1, PEERS):
        total = total + got[at, 16:24, :]
    total = jnp.sum(total, axis=(0, 1), keepdims=True)
    errors[...] = jnp.sqrt(total / (TOKENS * C) + 1e-06)


def alpha_bar(steps_in):
    angle = (steps_in.astype(jnp.float32) / 1000.0 + 0.008) / 1.008 * (math.pi / 2)
    return jnp.cos(angle) ** 2


def coefficients(timesteps):
    z = lax.axis_index("z")
    abar = alpha_bar(timesteps)
    keep = jnp.sqrt(abar[1:] / abar[:-1])
    noise = jnp.sqrt(1.0 - abar[1:]) - keep * jnp.sqrt(1.0 - abar[:-1])
    before = jnp.sum(jnp.where(jnp.arange(STEPS) < 2 * z, keep - 1.0, 0.0))
    pair = lax.dynamic_slice_in_dim(jnp.stack([keep - 1.0, noise]), 2 * z, 2, axis=1)
    return jnp.concatenate([pair.reshape(4), before[None], jnp.zeros((3,), F32)])


def body(start, timesteps, modulation, w_in, w_qkv, w_o, w_out):
    coef = coefficients(timesteps)
    sent = call(send_weights, shape((Z, 96, 128), BF), (w_qkv, w_o, w_out))
    own = lax.all_to_all(sent, "z", 0, 0, tiled=True)
    peer = lax.ppermute(own, "core", [(0, 1), (1, 0)])
    sent, table = call(
        make_tables,
        (shape((PEERS, 96, 128), BF), shape((5, 128, 128), BF)),
        (own, peer, w_in, w_out, modulation, start),
        scratch=(pltpu.VMEM((80, D), BF), pltpu.VMEM((D, 128), BF), pltpu.VMEM((D, 128), BF)),
    )
    got = lax.all_to_all(sent, FLAT, 0, 0, tiled=True)
    heads, first_eps, sent = call(
        first_sweep,
        (shape((2 * HEADS, 128, 128), BF), shape((16, 128), F32), shape((Z, 16, 128), BF)),
        (coef, got, start, table),
        scratch=work_space(),
        smem=(0,),
    )
    got = lax.all_to_all(sent, "z", 0, 0, tiled=True)
    latents, sent = call(
        first_prefix, (shape((2, 16, 128), F32), shape((PEERS, 32, 128), BF)), (coef, got, start, first_eps), smem=(0,)
    )
    got = lax.all_to_all(sent, FLAT, 0, 0, tiled=True)
    term, sent = call(
        second_sweep, (shape((16, 128), F32), shape((Z, 16, 128), F32)), (coef, got, latents, table, heads), work_space(), (0,)
    )
    got = lax.all_to_all(sent, "z", 0, 0, tiled=True)
    sent = call(second_prefix, shape((PEERS, 24, 128), F32), (got, start, latents, term))
    got = lax.all_to_all(sent, FLAT, 0, 0, tiled=True)
    window, errors = call(finish, (shape((1, 64, C), F32), shape((1, 1), F32)), (got,))
    return window, errors.reshape(1)


def solution(mesh):
    fine = Mesh(mesh.devices.reshape(Z, 2, 4, 4), ("z", "core", "y", "x"))
    step, seq = ("z", "core"), ("y", "x")
    return jax.shard_map(
        body,
        mesh=fine,
        in_specs=(P(seq, None), P(), P(step, None), P(), P(step, None), P(step, None), P()),
        out_specs=(P(step, seq, None), P(step)),
        check_vma=False,
    )
```

time: 544 us -> 140 us (0.26)
  waiting for transfers between devices: 383 us -> 12.8 us
  matrix products: 29.9 us -> 0 us
  between operations: 18.9 us -> 0.75 us
  starting transfers between devices: 0.24 us -> 16.2 us
  Pallas kernels: 0 us -> 10.3 us
    all_gather x6 -> x0, waiting for transfers between devices: 380 us -> none  [the longest x2 116 us: predict(): lax.all_gather(values, 'seq', axis=0, tiled=True)]
    all_to_all x0 -> x5, blocking collectives: none -> 96.1 us  [the longest x1 33.7 us: body(): own = lax.all_to_all(sent, 'z', 0, 0, tiled=True)]
    all_gather x2 -> x0, blocking collectives: 67.9 us -> none  [body(): every = lax.all_gather(term[None], 'step', axis=0, tiled=True)]
    psum x1 -> x0, blocking collectives: 31.6 us -> none  [body(): squared = lax.psum(jnp.sum(change * change), 'seq')]
    dot_general x10 -> x0, matrix products: 29.9 us -> none  [the longest x2 11.1 us: predict(): jnp.dot(hidden, whole_qkv, preferred_element_type=jnp.float32)]
    all_to_all x0 -> x1, waiting for transfers between devices: none -> 12.2 us  [body(): got = lax.all_to_all(sent, FLAT, 0, 0, tiled=True)]
    pallas_call x0 -> x7, Pallas kernels: none -> 10.3 us  [call(): pl.pallas_call(kernel, out_shape=outs, in_specs=[pl.BlockSpec(memory_spac...]
    ppermute x0 -> x1, starting transfers between devices: none -> 8.75 us  [body(): peer = lax.ppermute(own, 'core', [(0, 1), (1, 0)])]
  transfers between devices with their start and end apart: 6 -> 2, of which waited for: 6 -> 2; matrix products, arithmetic and copies ran while one was open for 3% -> 1% of each run, Pallas kernels for 0% -> 0%
where the time goes in v1:
time: 140 us
  blocking collectives  96.1 us (69%)
  starting transfers between devices  16.2 us (12%)
  waiting for transfers between devices  12.8 us (9%)
  Pallas kernels  10.3 us (7%)
  local copies, waits for them, and re-layouts  2.03 us (1%)
  other arithmetic  1.47 us (1%)
    all_to_all x1, blocking collectives, body(): own = lax.all_to_all(sent, 'z', 0, 0, tiled=True)  33.7 us
    all_to_all x2, blocking collectives, body(): got = lax.all_to_all(sent, 'z', 0, 0, tiled=True)  31.7 us
    all_to_all x2, blocking collectives, body(): got = lax.all_to_all(sent, FLAT, 0, 0, tiled=True)  30.7 us
    all_to_all x1, waiting for transfers between devices, body(): got = lax.all_to_all(sent, FLAT, 0, 0, tiled=True)  12.2 us
    pallas_call x7, Pallas kernels, call(): pl.pallas_call(kernel, out_shape=outs, in_specs=[pl.BlockSpec(memory_spac...  10.3 us
    ppermute x1, starting transfers between devices, body(): peer = lax.ppermute(own, 'core', [(0, 1), (1, 0)])  8.75 us
    all_to_all x1, starting transfers between devices, body(): got = lax.all_to_all(sent, FLAT, 0, 0, tiled=True)  7.48 us
  transfers between devices with their start and end apart: 2, of which 2 were waited for; matrix products, arithmetic and copies ran while one was open for 1% of the time, Pallas kernels for 0%

profile of v1, /device:TPU:1, one launch (start us, length us, event | category | flops | bytes accessed | tf_op | source)
XLA Modules:
  0.0 139.7 jit_solution(10520927402568402066)
XLA Ops:
  0.6 0.0 copy-start.3
  0.6 0.0 copy-start.1
  0.7 1.2 copy.9.w_out
  1.9 0.0 copy-done.3
  1.9 0.0 copy-done.1
  1.9 0.3 shard_map.86
  2.2 0.0 copy-start
  2.2 0.0 copy-start.2
  2.2 33.7 %all_to_all.30.own = bf16[16,96,128]{2,1,0:T(8,128)(2,1)S(1)} all-to-all(bf16[16,96,128]{2,1,0:T(8,128)(2,1)S(1)} %shard_map.86), channel_id=1, replica_groups=mesh['z'=16,'core'=2,'y'=4,'x'=4] {'z'}, dimensions={0} | all-to-all | bytes 786432 | tf_op jit(solution)/shard_map/all_to_all | solution.py:286
  35.9 0.0 copy-start.4
  35.9 8.7 %collective-permute-start = (bf16[16,96,128]{2,1,0:T(8,128)(2,1)S(1)}, bf16[16,96,128]{2,1,0:T(8,128)(2,1)S(1)}, u32[]{:S(2)}, u32[]{:S(2)}) collective-permute-start(bf16[16,96,128]{2,1,0:T(8,128)(2,1)S(1)} %all_to_all.30.own), channel_id=1, source_target_pairs={{0,16},{16,0},{1,17},{17,1},{2,18},{18,2},{3,19},{19,3},{4,20},{20... | collective-permute-start | bytes 1179656 | tf_op jit(solution)/shard_map/ppermute | solution.py:287
  44.6 0.0 copy-start.5
  44.6 0.6 copy-done.5
  45.3 0.6 collective-permute-done.peer
  45.9 0.0 copy-done
  45.9 0.0 copy-done.2
  45.9 0.0 copy-done.4
  45.9 2.2 %shard_map.87 = (bf16[32,96,128]{2,1,0:T(8,128)(2,1)}, bf16[5,128,128]{2,1,0:T(8,128)(2,1)S(1)}) custom-call(bf16[16,96,128]{2,1,0:T(8,128)(2,1)S(1)} %all_to_all.30.own, bf16[16,96,128]{2,1,0:T(8,128)(2,1)S(1)} %collective-permute-done.peer, bf16[64,1536]{1,0:T(8,128)(2,1)S(1)} %copy-done.2, bf16[1536,64]{1,0:T(8,128)(2,1)S(1)} %copy.9.w_out, ...), custom_call_target="tpu_custom_call" | custom-call | tf_op jit(solution)/shard_map/pallas_call | solution.py:65
  48.2 7.5 %all-to-all-start.1 = ((bf16[32,96,128]{2,1,0:T(8,128)(2,1)}), bf16[32,96,128]{2,1,0:T(8,128)(2,1)S(1)}, u32[]{:S(2)}, u32[]{:S(2)}) async-start(bf16[32,96,128]{2,1,0:T(8,128)(2,1)} %get-tuple-element.13), calls=%async_computation.1 | async-start | bytes 1572864 | tf_op jit(solution)/shard_map/all_to_all | solution.py:294
  55.7 0.1 add_bitcast_fusion
  55.7 0.6 subtract_bitcast_fusion
  56.4 0.1 constant_dynamic-slice_fusion
  56.5 0.1 reshape.10
  56.5 0.7 pad_maximum_fusion.1.coef
  57.3 12.2 %all-to-all-done.1.got = bf16[32,96,128]{2,1,0:T(8,128)(2,1)S(1)} async-done(((bf16[32,96,128]{2,1,0:T(8,128)(2,1)}), bf16[32,96,128]{2,1,0:T(8,128)(2,1)S(1)}, u32[]{:S(2)}, u32[]{:S(2)}) %all-to-all-start.1) | async-done | bytes 786464 | tf_op jit(solution)/shard_map/all_to_all | solution.py:294
  69.5 3.0 %shard_map.88 = (bf16[16,128,128]{2,1,0:T(8,128)(2,1)S(1)}, f32[16,128]{1,0:T(8,128)S(1)}, bf16[16,16,128]{2,1,0:T(8,128)(2,1)S(1)}) custom-call(f32[8]{0:T(128)S(1)} %pad_maximum_fusion.1.coef, bf16[32,96,128]{2,1,0:T(8,128)(2,1)S(1)} %all-to-all-done.1.got, f32[64,64]{1,0:T(8,128)S(1)} %copy-done, bf16[5,128,128]{2,1,0:T(8,128)(2,1)S(1)} %get-tuple-element.14.table), custom_call_target="tpu_custom_call" | custom-call | tf_op jit(solution)/shard_map/pallas_call | solution.py:65
  72.4 17.1 %all_to_all.31.got = bf16[16,16,128]{2,1,0:T(8,128)(2,1)S(1)} all-to-all(bf16[16,16,128]{2,1,0:T(8,128)(2,1)S(1)} %get-tuple-element.15), channel_id=1, replica_groups=mesh['z'=16,'core'=2,'y'=4,'x'=4] {'z'}, dimensions={0} | all-to-all | bytes 131072 | tf_op jit(solution)/shard_map/all_to_all | solution.py:302
  89.5 0.6 shard_map.89
  90.2 14.0 %all_to_all.32.got = bf16[32,32,128]{2,1,0:T(8,128)(2,1)S(1)} all-to-all(bf16[32,32,128]{2,1,0:T(8,128)(2,1)S(1)} %get-tuple-element.17), channel_id=1, replica_groups=mesh['z'=16,'core'=2,'y'=4,'x'=4] {'core','y','x'}, dimensions={0} | all-to-all | bytes 524288 | tf_op jit(solution)/shard_map/all_to_all | solution.py:306
  104.2 3.4 %shard_map.90 = (f32[16,128]{1,0:T(8,128)S(1)}, f32[16,16,128]{2,1,0:T(8,128)S(1)}) custom-call(f32[8]{0:T(128)S(1)} %pad_maximum_fusion.1.coef, bf16[32,32,128]{2,1,0:T(8,128)(2,1)S(1)} %all_to_all.32.got, f32[2,16,128]{2,1,0:T(8,128)S(1)} %get-tuple-element.18.latents, bf16[5,128,128]{2,1,0:T(8,128)(2,1)S(1)} %get-tuple-element.14.table, ...), custom_call_target="tpu_custom_call" | custom-call | tf_op jit(solution)/shard_map/pallas_call | solution.py:65
  107.5 14.6 %all_to_all.33.got = f32[16,16,128]{2,1,0:T(8,128)S(1)} all-to-all(f32[16,16,128]{2,1,0:T(8,128)S(1)} %get-tuple-element.20), channel_id=1, replica_groups=mesh['z'=16,'core'=2,'y'=4,'x'=4] {'z'}, dimensions={0} | all-to-all | bytes 262144 | tf_op jit(solution)/shard_map/all_to_all | solution.py:310
  122.2 0.1 shard_map.91
  122.3 16.7 %all_to_all.34.got = f32[32,24,128]{2,1,0:T(8,128)S(1)} all-to-all(f32[32,24,128]{2,1,0:T(8,128)S(1)} %shard_map.91), channel_id=1, replica_groups=mesh['z'=16,'core'=2,'y'=4,'x'=4] {'core','y','x'}, dimensions={0} | all-to-all | bytes 786432 | tf_op jit(solution)/shard_map/all_to_all | solution.py:312
  139.0 0.7 shard_map.92
  (3 shorter events, 0.1 us)
Async XLA Ops:
  0.6 1.2 copy-start.3
  0.6 1.2 copy-start.1
  2.2 43.8 %copy-start = (f32[64,64]{1,0:T(8,128)S(1)}, f32[64,64]{1,0:T(8,128)}, u32[]{:S(2)}) copy-start(f32[64,64]{1,0:T(8,128)} %start.7) | copy-start | bytes 49156
  2.2 43.8 %copy-start.2 = (bf16[64,1536]{1,0:T(8,128)(2,1)S(1)}, bf16[64,1536]{1,0:T(8,128)(2,1)}, u32[]{:S(2)}) copy-start(bf16[64,1536]{1,0:T(8,128)(2,1)} %w_in.1) | copy-start | bytes 589828
  35.9 10.1 %copy-start.4 = (bf16[1,3072]{1,0:T(2,128)(2,1)S(1)}, bf16[1,3072]{1,0:T(2,128)(2,1)}, u32[]{:S(2)}) copy-start(bf16[1,3072]{1,0:T(2,128)(2,1)} %modulation.1) | copy-start | bytes 18436
  35.9 10.1 %collective-permute-start = (bf16[16,96,128]{2,1,0:T(8,128)(2,1)S(1)}, bf16[16,96,128]{2,1,0:T(8,128)(2,1)S(1)}, u32[]{:S(2)}, u32[]{:S(2)}) collective-permute-start(bf16[16,96,128]{2,1,0:T(8,128)(2,1)S(1)} %all_to_all.30.own), channel_id=1, source_target_pairs={{0,16},{16,0},{1,17},{17,1},{2,18},{18,2},{3,19},{19,3},{4,20},{20... | collective-permute-start | bytes 1179656 | tf_op jit(solution)/shard_map/ppermute | solution.py:287
  44.6 0.7 copy-start.5
  48.2 21.3 %all-to-all-start.1 = ((bf16[32,96,128]{2,1,0:T(8,128)(2,1)}), bf16[32,96,128]{2,1,0:T(8,128)(2,1)S(1)}, u32[]{:S(2)}, u32[]{:S(2)}) async-start(bf16[32,96,128]{2,1,0:T(8,128)(2,1)} %get-tuple-element.13), calls=%async_computation.1 | async-start | bytes 1572864 | tf_op jit(solution)/shard_map/all_to_all | solution.py:294

commit v2 on v1

--- a/solution.py
+++ b/solution.py
@@ -22,6 +22,7 @@
 BF = jnp.bfloat16
 F32 = jnp.float32
 NT = (((1,), (1,)), ((), ()))
+BEST = lax.Precision.HIGHEST
 SCALE = 1.0 / (math.sqrt(HEAD_DIM) * math.log(2.0))
 
 
@@ -85,7 +86,7 @@
         block = w_qkv[:, pl.ds(start, HEAD_DIM)].astype(F32)
         return jnp.where(odd, block[:, C:], block[:, :C])
 
-    head = dot(w_o[...], w_out[...])
+    head = lax.dot_general(w_o[...], w_out[...], NT, preferred_element_type=F32)
     head = jnp.concatenate([head, jnp.zeros((ROWS - head.shape[0], C), F32)], axis=0)
     first = jnp.concatenate([columns(0), columns(INNER)], axis=1).astype(BF)
     second = jnp.concatenate([columns(2 * INNER), head], axis=1).astype(BF)
@@ -94,47 +95,44 @@
         out[to, ROWS : 2 * ROWS, :] = second
 
 
-def make_tables(own, peer, w_in, w_out, modulation, start, out, table, left, qk, vw):
-    _, core, seq = place()
-    for z in range(Z):
-        for source, parity in ((own, core), (peer, 1 - core)):
-            at = pl.ds(pl.multiple_of(z * 2 * ROWS + parity * ROWS, 16), ROWS)
-            qk[at, :] = source[z, 0:ROWS, :]
-            vw[at, :] = source[z, ROWS : 2 * ROWS, :]
+def make_tables(w_in, w_out, modulation, left, table):
     w = w_in[...].astype(F32)
     centred = w - jnp.mean(w, axis=1, keepdims=True)
     shift = modulation[:, 0:D].astype(F32)
     gain = modulation[:, D : 2 * D].astype(F32)
     left[0:C, :] = (centred * (1.0 + gain)).astype(BF)
     left[C : C + 16, :] = jnp.where(rows((16, D)) == 0, shift, 0.0).astype(BF)
-    first = dot(left[...], qk[...])
-    value = dot(left[...], vw[...])[:, :C]
-    query, key = first[:, :C], first[:, C:]
-    mine = own[seq, ROWS : ROWS + 32, C:].astype(F32)
-    other = peer[seq, ROWS : ROWS + 32, C:].astype(F32)
-    even = core == 0
-    head = jnp.concatenate([jnp.where(even, mine, other), jnp.where(even, other, mine)], axis=0)
-    best = lax.Precision.HIGHEST
-    a = lax.dot_general(query, key, NT, precision=best, preferred_element_type=F32) * SCALE
-    b = jnp.dot(value, head, precision=best, preferred_element_type=F32)
-    bias = lax.dot_general(key[C : C + 8], query, NT, precision=best, preferred_element_type=F32) * SCALE
-    bias = jnp.concatenate([bias, jnp.zeros((8, 128 - bias.shape[1]), F32)], axis=1)[0:1]
-    main = jnp.concatenate([a[:, :C], b], axis=1)
-    main = jnp.where(rows(main.shape) == C + 1, bias, main).astype(BF)
-    x = start[pl.ds(pl.multiple_of(core * 32, 32), 32), :]
-    x = jnp.concatenate([x[:16], x[16:]], axis=1).astype(BF)
-    for to in range(PEERS):
-        out[to, 0:80, :] = main
-        out[to, 80:96, :] = x
-    gram = lax.dot_general(centred, centred, NT, precision=best, preferred_element_type=F32) / D
-    direct = dot(w_in[...], w_out[...])
+    gram = lax.dot_general(centred, centred, NT, precision=BEST, preferred_element_type=F32) / D
+    direct = lax.dot_general(w_in[...], w_out[...], NT, preferred_element_type=F32)
     pad = jnp.zeros((C, C), F32)
-    below = jnp.zeros((C, 2 * C), BF)
     gram = jnp.concatenate([gram, pad], axis=1)
     direct = jnp.concatenate([pad, direct], axis=1)
     for at, piece in enumerate(split_of(gram, 3) + split_of(direct, 2)):
         table[at, 0:C, :] = piece
-        table[at, C : 2 * C, :] = below
+        table[at, C : 2 * C, :] = jnp.zeros((C, 2 * C), BF)
+
+
+def make_heads(both, left, start, out, qk, vw):
+    _, core, seq = place()
+    for z in range(Z):
+        for parity in range(2):
+            at = pl.ds((z * 2 + parity) * ROWS, ROWS)
+            qk[at, :] = both[parity, z, 0:ROWS, :]
+            vw[at, :] = both[parity, z, ROWS : 2 * ROWS, :]
+    first = dot(left[...], qk[...])
+    value = dot(left[...], vw[...])[:, :C]
+    query, key = first[:, :C], first[:, C:]
+    head = both[:, seq, ROWS : ROWS + 32, C:].astype(F32).reshape(C, C)
+    a = lax.dot_general(query, key, NT, precision=BEST, preferred_element_type=F32) * SCALE
+    b = jnp.dot(value, head, precision=BEST, preferred_element_type=F32)
+    bias = lax.dot_general(key[C : C + 8], query, NT, precision=BEST, preferred_element_type=F32) * SCALE
+    bias = jnp.concatenate([bias, jnp.zeros((8, 128 - bias.shape[1]), F32)], axis=1)[0:1]
+    main = jnp.concatenate([a[:, :C], b], axis=1)
+    main = jnp.where(rows(main.shape) == C + 1, bias, main).astype(BF)
+    x = packed_start(start, core).astype(BF)
+    for to in range(PEERS // 2):
+        out[to, 0:80, :] = main
+        out[to, 80:96, :] = x
 
 
 def normalized(x, table):
@@ -185,13 +183,13 @@
 def first_sweep(coef, got, start, table, heads, first_eps, out, *work):
     _, core, _ = place()
     for at in range(2 * HEADS):
-        source = 2 * at
-        both = got[source, 0:80, :].astype(F32) + got[source + 1, 0:80, :].astype(F32)
+        step, source = at // HEADS, 2 * (at % HEADS)
+        both = got[step, source, 0:80, :].astype(F32) + got[step, source + 1, 0:80, :].astype(F32)
         heads[at, 0:80, :] = both.astype(BF)
         heads[at, 80:128, :] = jnp.zeros((48, 128), BF)
     x = start[pl.ds(pl.multiple_of(core * 32, 32), 32), :].astype(BF).astype(F32)
     x = jnp.concatenate([x, jnp.zeros_like(x)], axis=1)
-    everything = got[:, 80:96, :].astype(F32).reshape(PEERS * 16, 128)
+    everything = got[:, :, 80:96, :].astype(F32).reshape(PEERS * 16, 128)
     work[1][...] = normalized(unpack(everything), table).astype(BF)
     eps = attend((0, 1), heads, table, x, work)
     first_eps[...] = eps[0]
@@ -239,28 +237,28 @@
         out[to] = both
 
 
-def second_prefix(got, start, latents, term, out):
+def second_prefix(got, start, latents, term, fresh, out):
     z, core, _ = place()
     even = packed_start(start, core) + below(got, z)
-    fresh = (even, even + term[...])
+    fresh[0] = even
+    fresh[1] = even + term[...]
     for step in range(2):
         change = fresh[step] - latents[step]
         squared = change * change
         squared = squared[:8] + squared[8:]
         for to in range(PEERS // 2):
-            out[step * 16 + to, 0:16, :] = fresh[step]
-            out[step * 16 + to, 16:24, :] = squared
-
-
-def finish(got, window, errors):
-    _, _, seq = place()
+            out[step * 16 + to] = squared
+
+
+def finish(got, halves, window, errors):
+    _, core, _ = place()
     for half in range(2):
-        packed = got[half * 16 + seq, 0:16, :]
+        packed = halves[half, core]
         window[0, half * 32 : half * 32 + 16, :] = packed[:, :C]
         window[0, half * 32 + 16 : half * 32 + 32, :] = packed[:, C:]
-    total = got[0, 16:24, :]
+    total = got[0]
     for at in range(1, PEERS):
-        total = total + got[at, 16:24, :]
+        total = total + got[at]
     total = jnp.sum(total, axis=(0, 1), keepdims=True)
     errors[...] = jnp.sqrt(total / (TOKENS * C) + 1e-06)
 
@@ -282,16 +280,16 @@
 
 def body(start, timesteps, modulation, w_in, w_qkv, w_o, w_out):
     coef = coefficients(timesteps)
-    sent = call(send_weights, shape((Z, 96, 128), BF), (w_qkv, w_o, w_out))
-    own = lax.all_to_all(sent, "z", 0, 0, tiled=True)
-    peer = lax.ppermute(own, "core", [(0, 1), (1, 0)])
-    sent, table = call(
-        make_tables,
-        (shape((PEERS, 96, 128), BF), shape((5, 128, 128), BF)),
-        (own, peer, w_in, w_out, modulation, start),
-        scratch=(pltpu.VMEM((80, D), BF), pltpu.VMEM((D, 128), BF), pltpu.VMEM((D, 128), BF)),
-    )
-    got = lax.all_to_all(sent, FLAT, 0, 0, tiled=True)
+    sent = call(send_weights, shape((Z, 96, 128), BF), (w_qkv, w_o, w_out.T))
+    got = lax.all_to_all(sent, "z", 0, 0, tiled=True)
+    left, table = call(make_tables, (shape((80, D), BF), shape((5, 128, 128), BF)), (w_in, w_out.T, modulation))
+    sent = call(
+        make_heads,
+        shape((PEERS // 2, 96, 128), BF),
+        (lax.all_gather(got, "core"), left, start),
+        scratch=(pltpu.VMEM((D, 128), BF), pltpu.VMEM((D, 128), BF)),
+    )
+    got = lax.all_gather(lax.all_to_all(sent, ("y", "x"), 0, 0, tiled=True), "core")
     heads, first_eps, sent = call(
         first_sweep,
         (shape((2 * HEADS, 128, 128), BF), shape((16, 128), F32), shape((Z, 16, 128), BF)),
@@ -308,9 +306,12 @@
         second_sweep, (shape((16, 128), F32), shape((Z, 16, 128), F32)), (coef, got, latents, table, heads), work_space(), (0,)
     )
     got = lax.all_to_all(sent, "z", 0, 0, tiled=True)
-    sent = call(second_prefix, shape((PEERS, 24, 128), F32), (got, start, latents, term))
+    fresh, sent = call(
+        second_prefix, (shape((2, 16, 128), F32), shape((PEERS, 8, 128), F32)), (got, start, latents, term)
+    )
     got = lax.all_to_all(sent, FLAT, 0, 0, tiled=True)
-    window, errors = call(finish, (shape((1, 64, C), F32), shape((1, 1), F32)), (got,))
+    halves = lax.all_gather(fresh, "core")
+    window, errors = call(finish, (shape((1, 64, C), F32), shape((1, 1), F32)), (got, halves))
     return window, errors.reshape(1)
 
 

time: 140 us -> 137 us (0.979)
  blocking collectives: 96.1 us -> 59 us
  waiting for transfers between devices: 12.8 us -> 30.8 us
  starting transfers between devices: 16.2 us -> 29.9 us
    all_to_all x1 -> x0, blocking collectives: 33.7 us -> none  [body(): own = lax.all_to_all(sent, 'z', 0, 0, tiled=True)]
    all_to_all x0 -> x2, waiting for transfers between devices: none -> 25.1 us  [the longest x1 17.1 us: body(): got = lax.all_to_all(sent, 'z', 0, 0, tiled=True)]
    all_to_all x0 -> x2, starting transfers between devices: none -> 22.6 us  [the longest x1 15.9 us: body(): got = lax.all_to_all(sent, 'z', 0, 0, tiled=True)]
    all_to_all x2 -> x1, blocking collectives: 30.7 us -> 13.3 us  [body(): got = lax.all_to_all(sent, FLAT, 0, 0, tiled=True)]
    all_gather x0 -> x3, blocking collectives: none -> 14 us  [the longest x1 8.71 us: body(): lax.all_gather(got, 'core')]
    ppermute x1 -> x0, starting transfers between devices: 8.75 us -> none  [body(): peer = lax.ppermute(own, 'core', [(0, 1), (1, 0)])]
    all_to_all x1, waiting for transfers between devices: 12.2 us -> 5.69 us  [body(): got = lax.all_to_all(sent, FLAT, 0, 0, tiled=True)]
    pallas_call x7 -> x8, Pallas kernels: 10.3 us -> 11.6 us  [call(): pl.pallas_call(kernel, out_shape=outs, in_specs=[pl.BlockSpec(memory_spac...]
  transfers between devices with their start and end apart: 2 -> 3, of which waited for: 2 -> 3; matrix products, arithmetic and copies ran while one was open for 1% -> 1% of each run, Pallas kernels for 0% -> 1%
where the time goes in v2:
time: 137 us; the launch traced here: 136 us
  blocking collectives  59 us (43%)
  waiting for transfers between devices  30.8 us (22%)
  starting transfers between devices  29.9 us (22%)
  Pallas kernels  11.6 us (8%)
  local copies, waits for them, and re-layouts  2.96 us (2%)
  other arithmetic  1.46 us (1%)
    all_to_all x2, blocking collectives, body(): got = lax.all_to_all(sent, 'z', 0, 0, tiled=True)  31.7 us
    all_to_all x1, waiting for transfers between devices, body(): got = lax.all_to_all(sent, 'z', 0, 0, tiled=True)  17.1 us
    all_to_all x1, starting transfers between devices, body(): got = lax.all_to_all(sent, 'z', 0, 0, tiled=True)  15.9 us
    all_to_all x1, blocking collectives, body(): got = lax.all_to_all(sent, FLAT, 0, 0, tiled=True)  13.3 us
    pallas_call x8, Pallas kernels, call(): pl.pallas_call(kernel, out_shape=outs, in_specs=[pl.BlockSpec(memory_spac...  11.6 us
    all_gather x1, blocking collectives, body(): lax.all_gather(got, 'core')  8.71 us
    all_to_all x1, waiting for transfers between devices, body(): lax.all_to_all(sent, ('y', 'x'), 0, 0, tiled=True)  8.02 us
    all_to_all x1, starting transfers between devices, body(): got = lax.all_to_all(sent, FLAT, 0, 0, tiled=True)  7.28 us
  transfers between devices with their start and end apart: 3, of which 3 were waited for; matrix products, arithmetic and copies ran while one was open for 1% of the time, Pallas kernels for 1%

profile of v2, /device:TPU:1, one launch (start us, length us, event | category | flops | bytes accessed | tf_op | source)
XLA Modules:
  0.0 136.5 jit_solution(10231902493194399673)
XLA Ops:
  0.6 0.0 copy-start
  0.6 0.9 copy-done
  1.6 0.0 copy-start.3
  1.6 1.0 copy-done.3
  2.5 0.0 copy-start.5
  2.5 0.9 copy-done.5
  3.4 1.0 shard_map.86
  4.4 0.0 copy-start.1
  4.4 0.0 copy-start.4
  4.4 0.0 copy-start.6
  4.4 15.9 %all-to-all-start = ((bf16[16,96,128]{2,1,0:T(8,128)(2,1)}), bf16[16,96,128]{2,1,0:T(8,128)(2,1)S(1)}, u32[]{:S(2)}, u32[]{:S(2)}) async-start(bf16[16,96,128]{2,1,0:T(8,128)(2,1)} %shard_map.86), calls=%async_computation | async-start | bytes 786432 | tf_op jit(solution)/shard_map/all_to_all | solution.py:284
  20.3 0.0 copy-done.1
  20.3 0.0 copy-done.4
  20.3 0.0 copy-done.6
  20.4 0.0 copy-start.7
  20.4 0.7 shard_map.87
  21.1 0.0 copy-done.7
  21.1 0.1 add_bitcast_fusion
  21.2 0.0 copy-start.2
  21.2 17.1 %all-to-all-done = bf16[16,96,128]{2,1,0:T(8,128)(2,1)S(1)} async-done(((bf16[16,96,128]{2,1,0:T(8,128)(2,1)}), bf16[16,96,128]{2,1,0:T(8,128)(2,1)S(1)}, u32[]{:S(2)}, u32[]{:S(2)}) %all-to-all-start) | async-done | bytes 393248 | tf_op jit(solution)/shard_map/all_to_all | solution.py:284
  38.3 8.7 %all-gather = bf16[32,96,128]{2,1,0:T(8,128)(2,1)S(1)} all-gather(bf16[16,96,128]{2,1,0:T(8,128)(2,1)S(1)} %all-to-all-done), channel_id=2, replica_groups=mesh['z'=16,'core'=2,'y'=4,'x'=4] {'core'}, dimensions={0}, use_global_device_ids=true | all-gather | bytes 1179648 | tf_op jit(solution)/shard_map/all_gather | solution.py:289
  47.0 0.0 copy-done.2
  47.0 1.4 %shard_map.88 = bf16[16,96,128]{2,1,0:T(8,128)(2,1)} custom-call(bf16[2,16,96,128]{3,2,1,0:T(8,128)(2,1)S(1)} %bitcast.11, bf16[80,1536]{1,0:T(8,128)(2,1)S(1)} %get-tuple-element.15.left, f32[64,64]{1,0:T(8,128)S(1)} %copy-done.2), custom_call_target="tpu_custom_call" | custom-call | tf_op jit(solution)/shard_map/pallas_call | solution.py:66
  48.5 6.8 %all-to-all-start.1 = ((bf16[16,96,128]{2,1,0:T(8,128)(2,1)}), bf16[16,96,128]{2,1,0:T(8,128)(2,1)S(1)}, u32[]{:S(2)}, u32[]{:S(2)}) async-start(bf16[16,96,128]{2,1,0:T(8,128)(2,1)} %shard_map.88), calls=%async_computation.1 | async-start | bytes 786432 | tf_op jit(solution)/shard_map/all_to_all | solution.py:292
  55.2 0.6 subtract_bitcast_fusion
  55.8 0.1 constant_dynamic-slice_fusion
  55.9 0.1 reshape.10
  56.0 0.7 pad_maximum_fusion.1.coef
  56.7 8.0 %all-to-all-done.1 = bf16[16,96,128]{2,1,0:T(8,128)(2,1)S(1)} async-done(((bf16[16,96,128]{2,1,0:T(8,128)(2,1)}), bf16[16,96,128]{2,1,0:T(8,128)(2,1)S(1)}, u32[]{:S(2)}, u32[]{:S(2)}) %all-to-all-start.1) | async-done | bytes 393248 | tf_op jit(solution)/shard_map/all_to_all | solution.py:292
  64.7 3.5 %all-gather.1 = bf16[32,96,128]{2,1,0:T(8,128)(2,1)S(1)} all-gather(bf16[16,96,128]{2,1,0:T(8,128)(2,1)S(1)} %all-to-all-done.1), channel_id=3, replica_groups=mesh['z'=16,'core'=2,'y'=4,'x'=4] {'core'}, dimensions={0}, use_global_device_ids=true | all-gather | bytes 1179648 | tf_op jit(solution)/shard_map/all_gather | solution.py:292
  68.2 3.0 %shard_map.89 = (bf16[16,128,128]{2,1,0:T(8,128)(2,1)S(1)}, f32[16,128]{1,0:T(8,128)S(1)}, bf16[16,16,128]{2,1,0:T(8,128)(2,1)S(1)}) custom-call(f32[8]{0:T(128)S(1)} %pad_maximum_fusion.1.coef, bf16[2,16,96,128]{3,2,1,0:T(8,128)(2,1)S(1)} %bitcast.10, f32[64,64]{1,0:T(8,128)S(1)} %copy-done.2, bf16[5,128,128]{2,1,0:T(8,128)(2,1)S(1)} %get-tuple-element.16.table), custom_call_target="tpu_custom_call" | custom-call | tf_op jit(solution)/shard_map/pallas_call | solution.py:66
  71.2 17.2 %all_to_all.30.got = bf16[16,16,128]{2,1,0:T(8,128)(2,1)S(1)} all-to-all(bf16[16,16,128]{2,1,0:T(8,128)(2,1)S(1)} %get-tuple-element.17), channel_id=1, replica_groups=mesh['z'=16,'core'=2,'y'=4,'x'=4] {'z'}, dimensions={0} | all-to-all | bytes 131072 | tf_op jit(solution)/shard_map/all_to_all | solution.py:300
  88.4 0.6 shard_map.90
  89.1 13.3 %all_to_all.31.got = bf16[32,32,128]{2,1,0:T(8,128)(2,1)S(1)} all-to-all(bf16[32,32,128]{2,1,0:T(8,128)(2,1)S(1)} %get-tuple-element.19), channel_id=1, replica_groups=mesh['z'=16,'core'=2,'y'=4,'x'=4] {'core','y','x'}, dimensions={0} | all-to-all | bytes 524288 | tf_op jit(solution)/shard_map/all_to_all | solution.py:304
  102.3 3.4 %shard_map.91 = (f32[16,128]{1,0:T(8,128)S(1)}, f32[16,16,128]{2,1,0:T(8,128)S(1)}) custom-call(f32[8]{0:T(128)S(1)} %pad_maximum_fusion.1.coef, bf16[32,32,128]{2,1,0:T(8,128)(2,1)S(1)} %all_to_all.31.got, f32[2,16,128]{2,1,0:T(8,128)S(1)} %get-tuple-element.20.latents, bf16[5,128,128]{2,1,0:T(8,128)(2,1)S(1)} %get-tuple-element.16.table, ...), custom_call_target="tpu_custom_call" | custom-call | tf_op jit(solution)/shard_map/pallas_call | solution.py:66
  105.7 14.5 %all_to_all.32.got = f32[16,16,128]{2,1,0:T(8,128)S(1)} all-to-all(f32[16,16,128]{2,1,0:T(8,128)S(1)} %get-tuple-element.22), channel_id=1, replica_groups=mesh['z'=16,'core'=2,'y'=4,'x'=4] {'z'}, dimensions={0} | all-to-all | bytes 262144 | tf_op jit(solution)/shard_map/all_to_all | solution.py:308
  120.2 0.7 shard_map.92
  120.9 7.3 %all-to-all-start.5 = ((f32[32,8,128]{2,1,0:T(8,128)}), f32[32,8,128]{2,1,0:T(8,128)S(1)}, u32[]{:S(2)}, u32[]{:S(2)}) async-start(f32[32,8,128]{2,1,0:T(8,128)} %get-tuple-element.24), calls=%async_computation.5 | async-start | bytes 262144 | tf_op jit(solution)/shard_map/all_to_all | solution.py:312
  128.2 1.8 %all-gather.2 = f32[4,16,128]{2,1,0:T(8,128)S(1)} all-gather(f32[2,16,128]{2,1,0:T(8,128)S(1)} %get-tuple-element.25), channel_id=4, replica_groups=mesh['z'=16,'core'=2,'y'=4,'x'=4] {'core'}, dimensions={0}, use_global_device_ids=true | all-gather | bytes 49152 | tf_op jit(solution)/shard_map/all_gather | solution.py:313
  130.1 5.7 %all-to-all-done.5.got = f32[32,8,128]{2,1,0:T(8,128)S(1)} async-done(((f32[32,8,128]{2,1,0:T(8,128)}), f32[32,8,128]{2,1,0:T(8,128)S(1)}, u32[]{:S(2)}, u32[]{:S(2)}) %all-to-all-start.5) | async-done | bytes 131104 | tf_op jit(solution)/shard_map/all_to_all | solution.py:312
  135.8 0.7 shard_map.93
  (3 shorter events, 0.1 us)
Async XLA Ops:
  0.6 0.9 copy-start
  1.6 1.0 copy-start.3
  2.5 0.9 copy-start.5
  4.4 15.9 %copy-start.1 = (bf16[1536,64]{0,1:T(8,128)(2,1)S(1)}, bf16[1536,64]{0,1:T(8,128)(2,1)}, u32[]{:S(2)}) copy-start(bf16[1536,64]{0,1:T(8,128)(2,1)} %param.13) | copy-start | bytes 589828
  4.4 15.9 %copy-start.4 = (bf16[64,1536]{1,0:T(8,128)(2,1)S(1)}, bf16[64,1536]{1,0:T(8,128)(2,1)}, u32[]{:S(2)}) copy-start(bf16[64,1536]{1,0:T(8,128)(2,1)} %w_in.1) | copy-start | bytes 589828
  4.4 15.9 %copy-start.6 = (bf16[1,3072]{1,0:T(2,128)(2,1)S(1)}, bf16[1,3072]{1,0:T(2,128)(2,1)}, u32[]{:S(2)}) copy-start(bf16[1,3072]{1,0:T(2,128)(2,1)} %modulation.1) | copy-start | bytes 18436
  4.4 33.9 %all-to-all-start = ((bf16[16,96,128]{2,1,0:T(8,128)(2,1)}), bf16[16,96,128]{2,1,0:T(8,128)(2,1)S(1)}, u32[]{:S(2)}, u32[]{:S(2)}) async-start(bf16[16,96,128]{2,1,0:T(8,128)(2,1)} %shard_map.86), calls=%async_computation | async-start | bytes 786432 | tf_op jit(solution)/shard_map/all_to_all | solution.py:284
  20.4 0.7 copy-start.7
  21.2 25.8 %copy-start.2 = (f32[64,64]{1,0:T(8,128)S(1)}, f32[64,64]{1,0:T(8,128)}, u32[]{:S(2)}) copy-start(f32[64,64]{1,0:T(8,128)} %start.7) | copy-start | bytes 49156
  48.5 16.3 %all-to-all-start.1 = ((bf16[16,96,128]{2,1,0:T(8,128)(2,1)}), bf16[16,96,128]{2,1,0:T(8,128)(2,1)S(1)}, u32[]{:S(2)}, u32[]{:S(2)}) async-start(bf16[16,96,128]{2,1,0:T(8,128)(2,1)} %shard_map.88), calls=%async_computation.1 | async-start | bytes 786432 | tf_op jit(solution)/shard_map/all_to_all | solution.py:292
  120.9 14.8 %all-to-all-start.5 = ((f32[32,8,128]{2,1,0:T(8,128)}), f32[32,8,128]{2,1,0:T(8,128)S(1)}, u32[]{:S(2)}, u32[]{:S(2)}) async-start(f32[32,8,128]{2,1,0:T(8,128)} %get-tuple-element.24), calls=%async_computation.5 | async-start | bytes 262144 | tf_op jit(solution)/shard_map/all_to_all | solution.py:312

commit v3 on v2

--- a/solution.py
+++ b/solution.py
@@ -62,14 +62,16 @@
     return pieces
 
 
-def call(kernel, outs, args, scratch=(), smem=()):
+def call(kernel, outs, args, scratch=(), smem=(), anywhere=(), flops=0):
+    spaces = [pltpu.SMEM if at in smem else pl.ANY if at in anywhere else pltpu.VMEM for at in range(len(args))]
     return pl.pallas_call(
         kernel,
         out_shape=outs,
-        in_specs=[pl.BlockSpec(memory_space=pltpu.SMEM if at in smem else pltpu.VMEM) for at in range(len(args))],
+        in_specs=[pl.BlockSpec(memory_space=space) for space in spaces],
         out_specs=jax.tree.map(lambda _: pl.BlockSpec(memory_space=pltpu.VMEM), outs),
         scratch_shapes=scratch,
         compiler_params=pltpu.CompilerParams(vmem_limit_bytes=40 * 1024 * 1024),
+        cost_estimate=pl.CostEstimate(flops=flops, bytes_accessed=0, transcendentals=0) if flops else None,
     )(*args)
 
 
@@ -77,25 +79,54 @@
     return jax.ShapeDtypeStruct(dims, kind)
 
 
-def send_weights(w_qkv, w_o, w_out, out):
+def send_weights(w_qkv, w_o, w_out, out, blocks, left, right, arrived):
     _, _, seq = place()
+    copies = [pltpu.make_async_copy(w_o, left, arrived.at[3]), pltpu.make_async_copy(w_out, right, arrived.at[4])]
+    for at in range(3):
+        start = pl.multiple_of(at * INNER + (seq // 2) * HEAD_DIM, HEAD_DIM)
+        copies.append(pltpu.make_async_copy(w_qkv.at[:, pl.ds(start, HEAD_DIM)], blocks.at[at], arrived.at[at]))
+    for copy in copies:
+        copy.start()
+    for copy in copies:
+        copy.wait()
     odd = lax.rem(seq, 2) == 1
 
-    def columns(base):
-        start = pl.multiple_of(base + (seq // 2) * HEAD_DIM, HEAD_DIM)
-        block = w_qkv[:, pl.ds(start, HEAD_DIM)].astype(F32)
+    def columns(at):
+        block = blocks[at].astype(F32)
         return jnp.where(odd, block[:, C:], block[:, :C])
 
-    head = lax.dot_general(w_o[...], w_out[...], NT, preferred_element_type=F32)
+    head = lax.dot_general(left[...], right[...], NT, preferred_element_type=F32)
     head = jnp.concatenate([head, jnp.zeros((ROWS - head.shape[0], C), F32)], axis=0)
-    first = jnp.concatenate([columns(0), columns(INNER)], axis=1).astype(BF)
-    second = jnp.concatenate([columns(2 * INNER), head], axis=1).astype(BF)
+    first = jnp.concatenate([columns(0), columns(1)], axis=1).astype(BF)
+    second = jnp.concatenate([columns(2), head], axis=1).astype(BF)
     for to in range(Z):
         out[to, 0:ROWS, :] = first
         out[to, ROWS : 2 * ROWS, :] = second
 
 
-def make_tables(w_in, w_out, modulation, left, table):
+def coefficients(timesteps):
+    z, _, _ = place()
+    lane = lanes((8, 128))
+    moments = jnp.zeros((8, 128), F32)
+    for at in range(STEPS + 1):
+        moments = jnp.where(lane == at, timesteps[at].astype(F32), moments)
+    angle = (moments / 1000.0 + 0.008) / 1.008 * (math.pi / 2)
+    abar = jnp.cos(angle) ** 2
+    after = pltpu.roll(abar, 127, 1)
+    keep = jnp.sqrt(after / abar)
+    noise = jnp.sqrt(1.0 - after) - keep * jnp.sqrt(1.0 - abar)
+    less = keep - 1.0
+    row = rows((8, 128))
+    chosen = jnp.where(
+        row < 2,
+        jnp.where(lane == 2 * z + row, less, 0.0),
+        jnp.where(row < 4, jnp.where(lane == 2 * z + row - 2, noise, 0.0), jnp.where(lane < 2 * z, less, 0.0)),
+    )
+    return jnp.broadcast_to(jnp.sum(chosen, axis=1, keepdims=True), (8, 128))
+
+
+def make_tables(timesteps, w_in, w_out, modulation, left, table, coef):
+    coef[...] = coefficients(timesteps)
     w = w_in[...].astype(F32)
     centred = w - jnp.mean(w, axis=1, keepdims=True)
     shift = modulation[:, 0:D].astype(F32)
@@ -142,45 +173,43 @@
     return jnp.where(lanes(x.shape) == C, 1.0, x * lax.rsqrt(spread + 1e-06))
 
 
-def attend(steps, heads, table, x, work):
-    query_ref, key_ref, weight_ref, mixed_ref, direct_ref = work
+def ask(steps, heads, table, x, query, direct):
     count = x.shape[0]
-    span = HEADS * count
     mine = normalized(x, table)
     short = mine.astype(BF)
     lane = lanes((count, 128))
     exact = x.astype(BF)
-    direct_ref[...] = dot(exact, table[3]) + dot(exact, table[4])
-    results = []
     for step in steps:
+        direct[step] = dot(exact, table[3]) + dot(exact, table[4])
         for head in range(HEADS):
             both = heads[step * HEADS + head]
             grown = dot(short, both)
             constant = jnp.sum(mine * both[C : C + 16].astype(F32)[1:2], axis=1, keepdims=True)
             grown = jnp.where(lane < C, grown, jnp.where(lane == C, constant, 0.0)).astype(BF)
-            query_ref[step, head * count : (head + 1) * count, :] = grown
-        scores = lax.dot_general(query_ref[step], key_ref[...], NT, preferred_element_type=F32)
-        weight_ref[step] = jnp.exp2(scores - jnp.max(scores, axis=1, keepdims=True)).astype(BF)
-        mixed = dot(weight_ref[step], key_ref[...])
-        mixed_ref[step] = (mixed / mixed[:, C : C + 1]).astype(BF)
-        eps = jnp.zeros((count, 128), F32)
-        for head in range(HEADS):
-            eps = eps + dot(mixed_ref[step, head * count : (head + 1) * count, :], heads[step * HEADS + head])
-        results.append(pack_high(eps + direct_ref[...]))
-    return results
+            query[step, head * count : (head + 1) * count, :] = grown
+
+
+def attend(step, heads, query, direct, key, weight, mix):
+    count = direct.shape[1]
+    scores = lax.dot_general(query[step], key[...], NT, preferred_element_type=F32)
+    weight[step] = jnp.exp2(scores - jnp.max(scores, axis=1, keepdims=True)).astype(BF)
+    mixed = dot(weight[step], key[...])
+    mix[step] = (mixed / mixed[:, C : C + 1]).astype(BF)
+    eps = jnp.zeros((count, 128), F32)
+    for head in range(HEADS):
+        eps = eps + dot(mix[step, head * count : (head + 1) * count, :], heads[step * HEADS + head])
+    return pack_high(eps + direct[step])
 
 
 def work_space():
     return (
-        pltpu.VMEM((2, HEADS * 32, 128), BF),
         pltpu.VMEM((TOKENS, 128), BF),
         pltpu.VMEM((2, HEADS * 32, TOKENS), BF),
         pltpu.VMEM((2, HEADS * 32, 128), BF),
-        pltpu.VMEM((32, 128), F32),
-    )
-
-
-def first_sweep(coef, got, start, table, heads, first_eps, out, *work):
+    )
+
+
+def first_sweep(coef, got, start, table, heads, first_eps, out, query, direct, key, weight, mix):
     _, core, _ = place()
     for at in range(2 * HEADS):
         step, source = at // HEADS, 2 * (at % HEADS)
@@ -190,10 +219,11 @@
     x = start[pl.ds(pl.multiple_of(core * 32, 32), 32), :].astype(BF).astype(F32)
     x = jnp.concatenate([x, jnp.zeros_like(x)], axis=1)
     everything = got[:, :, 80:96, :].astype(F32).reshape(PEERS * 16, 128)
-    work[1][...] = normalized(unpack(everything), table).astype(BF)
-    eps = attend((0, 1), heads, table, x, work)
+    key[...] = normalized(unpack(everything), table).astype(BF)
+    ask((0, 1), heads, table, x, query, direct)
+    eps = [attend(step, heads, query, direct, key, weight, mix) for step in range(2)]
     first_eps[...] = eps[0]
-    both = (coef[2] * eps[0] + coef[3] * eps[1]).astype(BF)
+    both = (coef[2:3] * eps[0] + coef[3:4] * eps[1]).astype(BF)
     for to in range(Z):
         out[to] = both
 
@@ -213,8 +243,8 @@
 def first_prefix(coef, got, start, first_eps, latents, out):
     z, core, _ = place()
     x = packed_start(start, core)
-    even = x + coef[4] * x + below(got, z)
-    odd = even + coef[0] * x + coef[2] * first_eps[...]
+    even = x + coef[4:5] * x + below(got, z)
+    odd = even + coef[0:1] * x + coef[2:3] * first_eps[...]
     latents[0] = even
     latents[1] = odd
     for to in range(PEERS):
@@ -222,17 +252,20 @@
         out[to, 16:32, :] = odd.astype(BF)
 
 
-def second_sweep(coef, got, latents, table, heads, term, out, *work):
+def second_queries(latents, table, heads, query, direct):
+    for step in range(2):
+        ask((step,), heads, table, unpack(latents[step].astype(BF).astype(F32)), query, direct)
+
+
+def second_sweep(coef, got, latents, table, heads, query, direct, term, out, key, weight, mix):
     terms = []
     for step in range(2):
         everything = got[:, 16 * step : 16 * step + 16, :].astype(F32).reshape(PEERS * 16, 128)
-        work[1][...] = normalized(unpack(everything), table).astype(BF)
-        latent = latents[step]
-        x = unpack(latent.astype(BF).astype(F32))
-        eps = attend((step,), heads, table, x, work)[0]
-        terms.append(coef[step] * latent + coef[2 + step] * eps)
+        key[...] = normalized(unpack(everything), table).astype(BF)
+        eps = attend(step, heads, query, direct, key, weight, mix)
+        terms.append(coef[step : step + 1] * latents[step] + coef[2 + step : 3 + step] * eps)
     term[...] = terms[0]
-    both = terms[0] + terms[1]
+    both = (terms[0] + terms[1]).astype(BF)
     for to in range(Z):
         out[to] = both
 
@@ -263,26 +296,27 @@
     errors[...] = jnp.sqrt(total / (TOKENS * C) + 1e-06)
 
 
-def alpha_bar(steps_in):
-    angle = (steps_in.astype(jnp.float32) / 1000.0 + 0.008) / 1.008 * (math.pi / 2)
-    return jnp.cos(angle) ** 2
-
-
-def coefficients(timesteps):
-    z = lax.axis_index("z")
-    abar = alpha_bar(timesteps)
-    keep = jnp.sqrt(abar[1:] / abar[:-1])
-    noise = jnp.sqrt(1.0 - abar[1:]) - keep * jnp.sqrt(1.0 - abar[:-1])
-    before = jnp.sum(jnp.where(jnp.arange(STEPS) < 2 * z, keep - 1.0, 0.0))
-    pair = lax.dynamic_slice_in_dim(jnp.stack([keep - 1.0, noise]), 2 * z, 2, axis=1)
-    return jnp.concatenate([pair.reshape(4), before[None], jnp.zeros((3,), F32)])
-
-
 def body(start, timesteps, modulation, w_in, w_qkv, w_o, w_out):
-    coef = coefficients(timesteps)
-    sent = call(send_weights, shape((Z, 96, 128), BF), (w_qkv, w_o, w_out.T))
+    sent = call(
+        send_weights,
+        shape((Z, 96, 128), BF),
+        (w_qkv, w_o, w_out.T),
+        scratch=(
+            pltpu.VMEM((3, ROWS, HEAD_DIM), BF),
+            pltpu.VMEM((32, D), BF),
+            pltpu.VMEM((C, D), BF),
+            pltpu.SemaphoreType.DMA((5,)),
+        ),
+        anywhere=(0, 1, 2),
+    )
     got = lax.all_to_all(sent, "z", 0, 0, tiled=True)
-    left, table = call(make_tables, (shape((80, D), BF), shape((5, 128, 128), BF)), (w_in, w_out.T, modulation))
+    left, table, coef = call(
+        make_tables,
+        (shape((80, D), BF), shape((5, 128, 128), BF), shape((8, 128), F32)),
+        (timesteps, w_in, w_out.T, modulation),
+        smem=(0,),
+        flops=10**9,
+    )
     sent = call(
         make_heads,
         shape((PEERS // 2, 96, 128), BF),
@@ -294,16 +328,24 @@
         first_sweep,
         (shape((2 * HEADS, 128, 128), BF), shape((16, 128), F32), shape((Z, 16, 128), BF)),
         (coef, got, start, table),
-        scratch=work_space(),
-        smem=(0,),
+        scratch=(pltpu.VMEM((2, HEADS * 32, 128), BF), pltpu.VMEM((2, 32, 128), F32), *work_space()),
     )
     got = lax.all_to_all(sent, "z", 0, 0, tiled=True)
     latents, sent = call(
-        first_prefix, (shape((2, 16, 128), F32), shape((PEERS, 32, 128), BF)), (coef, got, start, first_eps), smem=(0,)
+        first_prefix, (shape((2, 16, 128), F32), shape((PEERS, 32, 128), BF)), (coef, got, start, first_eps)
     )
     got = lax.all_to_all(sent, FLAT, 0, 0, tiled=True)
+    query, direct = call(
+        second_queries,
+        (shape((2, HEADS * 32, 128), BF), shape((2, 32, 128), F32)),
+        (latents, table, heads),
+        flops=10**9,
+    )
     term, sent = call(
-        second_sweep, (shape((16, 128), F32), shape((Z, 16, 128), F32)), (coef, got, latents, table, heads), work_space(), (0,)
+        second_sweep,
+        (shape((16, 128), F32), shape((Z, 16, 128), BF)),
+        (coef, got, latents, table, heads, query, direct),
+        scratch=work_space(),
     )
     got = lax.all_to_all(sent, "z", 0, 0, tiled=True)
     fresh, sent = call(

time: 137 us -> 135 us (0.985)
  blocking collectives: 59 us -> 61.6 us
  starting transfers between devices: 29.9 us -> 27.7 us
  other arithmetic: 1.46 us -> 0 us
    all_to_all x1 -> x0, waiting for transfers between devices: 8.02 us -> none  [body(): lax.all_to_all(sent, ('y', 'x'), 0, 0, tiled=True)]
    all_to_all x1 -> x2, waiting for transfers between devices: 5.69 us -> 13.2 us  [body(): got = lax.all_to_all(sent, FLAT, 0, 0, tiled=True)]
    all_to_all x1 -> x0, starting transfers between devices: 6.76 us -> none  [body(): lax.all_to_all(sent, ('y', 'x'), 0, 0, tiled=True)]
    all_to_all x1 -> x2, starting transfers between devices: 7.28 us -> 11.8 us  [body(): got = lax.all_to_all(sent, FLAT, 0, 0, tiled=True)]
    all_to_all x1, blocking collectives: 13.3 us -> 16.1 us  [body(): lax.all_to_all(sent, ('y', 'x'), 0, 0, tiled=True)]
    pallas_call x8 -> x9, Pallas kernels: 11.6 us -> 11.3 us  [call(): pl.pallas_call(kernel, out_shape=outs, in_specs=[pl.BlockSpec(memory_spac...]
  transfers between devices with their start and end apart: 3 -> 3, of which waited for: 3 -> 3; matrix products, arithmetic and copies ran while one was open for 1% -> 0% of each run, Pallas kernels for 1% -> 2%
where the time goes in v3:
time: 135 us; the launch traced here: 134 us
  blocking collectives  61.6 us (46%)
  waiting for transfers between devices  29.9 us (22%)
  starting transfers between devices  27.7 us (21%)
  Pallas kernels  11.3 us (8%)
  local copies, waits for them, and re-layouts  2.8 us (2%)
    all_to_all x2, blocking collectives, body(): got = lax.all_to_all(sent, 'z', 0, 0, tiled=True)  31.5 us
    all_to_all x1, waiting for transfers between devices, body(): got = lax.all_to_all(sent, 'z', 0, 0, tiled=True)  16.7 us
    all_to_all x1, blocking collectives, body(): lax.all_to_all(sent, ('y', 'x'), 0, 0, tiled=True)  16.1 us
    all_to_all x1, starting transfers between devices, body(): got = lax.all_to_all(sent, 'z', 0, 0, tiled=True)  15.9 us
    all_to_all x2, waiting for transfers between devices, body(): got = lax.all_to_all(sent, FLAT, 0, 0, tiled=True)  13.2 us
    all_to_all x2, starting transfers between devices, body(): got = lax.all_to_all(sent, FLAT, 0, 0, tiled=True)  11.8 us
    pallas_call x9, Pallas kernels, call(): pl.pallas_call(kernel, out_shape=outs, in_specs=[pl.BlockSpec(memory_spac...  11.3 us
    all_gather x1, blocking collectives, body(): lax.all_gather(got, 'core')  8.71 us
  transfers between devices with their start and end apart: 3, of which 3 were waited for; matrix products, arithmetic and copies ran while one was open for 0% of the time, Pallas kernels for 2%

profile of v3, /device:TPU:1, one launch (start us, length us, event | category | flops | bytes accessed | tf_op | source)
XLA Modules:
  0.0 134.0 jit_solution(13215746481804877786)
XLA Ops:
  0.6 0.0 copy-start.1
  0.6 1.0 copy-done.1
  1.6 0.0 copy-start.2
  1.6 0.9 copy-done.2
  2.5 0.0 copy-start.4
  2.5 0.9 copy-done.4
  3.4 1.4 %shard_map.87 = bf16[16,96,128]{2,1,0:T(8,128)(2,1)} custom-call(bf16[48,3072]{1,0:T(8,128)(2,1)S(1)} %copy-done.1, bf16[32,1536]{1,0:T(8,128)(2,1)S(1)} %copy-done.4, bf16[64,1536]{1,0:T(8,128)(2,1)S(1)} %bitcast.7), custom_call_target="tpu_custom_call" | custom-call | tf_op jit(solution)/shard_map/pallas_call | solution.py:67
  4.8 0.0 copy-start.3
  4.9 0.0 copy-start.5
  4.9 0.0 copy-start.6
  4.9 0.0 copy-start.7
  4.9 15.9 %all-to-all-start = ((bf16[16,96,128]{2,1,0:T(8,128)(2,1)}), bf16[16,96,128]{2,1,0:T(8,128)(2,1)S(1)}, u32[]{:S(2)}, u32[]{:S(2)}) async-start(bf16[16,96,128]{2,1,0:T(8,128)(2,1)} %shard_map.87), calls=%async_computation | async-start | bytes 786432 | tf_op jit(solution)/shard_map/all_to_all | solution.py:312
  20.8 0.0 copy-done.3
  20.8 0.0 copy-done.5
  20.8 0.0 copy-done.6
  20.8 0.0 copy-done.7
  20.8 1.3 shard_map.86
  22.1 0.0 copy-start
  22.1 16.7 %all-to-all-done = bf16[16,96,128]{2,1,0:T(8,128)(2,1)S(1)} async-done(((bf16[16,96,128]{2,1,0:T(8,128)(2,1)}), bf16[16,96,128]{2,1,0:T(8,128)(2,1)S(1)}, u32[]{:S(2)}, u32[]{:S(2)}) %all-to-all-start) | async-done | bytes 393248 | tf_op jit(solution)/shard_map/all_to_all | solution.py:312
  38.8 8.7 %all-gather = bf16[32,96,128]{2,1,0:T(8,128)(2,1)S(1)} all-gather(bf16[16,96,128]{2,1,0:T(8,128)(2,1)S(1)} %all-to-all-done), channel_id=2, replica_groups=mesh['z'=16,'core'=2,'y'=4,'x'=4] {'core'}, dimensions={0}, use_global_device_ids=true | all-gather | bytes 1179648 | tf_op jit(solution)/shard_map/all_gather | solution.py:323
  47.5 0.0 copy-done
  47.5 0.7 shard_map.88
  48.2 16.1 %all_to_all.30 = bf16[16,96,128]{2,1,0:T(8,128)(2,1)S(1)} all-to-all(bf16[16,96,128]{2,1,0:T(8,128)(2,1)S(1)} %shard_map.88), channel_id=1, replica_groups=mesh['z'=16,'core'=2,'y'=4,'x'=4] {'y','x'}, dimensions={0} | all-to-all | bytes 786432 | tf_op jit(solution)/shard_map/all_to_all | solution.py:326
  64.3 3.5 %all-gather.1 = bf16[32,96,128]{2,1,0:T(8,128)(2,1)S(1)} all-gather(bf16[16,96,128]{2,1,0:T(8,128)(2,1)S(1)} %all_to_all.30), channel_id=3, replica_groups=mesh['z'=16,'core'=2,'y'=4,'x'=4] {'core'}, dimensions={0}, use_global_device_ids=true | all-gather | bytes 1179648 | tf_op jit(solution)/shard_map/all_gather | solution.py:326
  67.8 2.1 %shard_map.89 = (bf16[16,128,128]{2,1,0:T(8,128)(2,1)S(1)}, f32[16,128]{1,0:T(8,128)S(1)}, bf16[16,16,128]{2,1,0:T(8,128)(2,1)S(1)}) custom-call(f32[8,128]{1,0:T(8,128)S(1)} %get-tuple-element.18.coef, bf16[2,16,96,128]{3,2,1,0:T(8,128)(2,1)S(1)} %bitcast.6, f32[64,64]{1,0:T(8,128)S(1)} %copy-done, bf16[5,128,128]{2,1,0:T(8,128)(2,1)S(1)} %get-tuple-element.20.table), custom_call_target="tpu_custom_call" | custom-call | tf_op jit(solution)/shard_map/pallas_call | solution.py:67
  69.9 17.3 %all_to_all.31.got = bf16[16,16,128]{2,1,0:T(8,128)(2,1)S(1)} all-to-all(bf16[16,16,128]{2,1,0:T(8,128)(2,1)S(1)} %get-tuple-element.21), channel_id=1, replica_groups=mesh['z'=16,'core'=2,'y'=4,'x'=4] {'z'}, dimensions={0} | all-to-all | bytes 131072 | tf_op jit(solution)/shard_map/all_to_all | solution.py:333
  87.1 0.8 shard_map.90
  87.9 5.6 %all-to-all-start.3 = ((bf16[32,32,128]{2,1,0:T(8,128)(2,1)}), bf16[32,32,128]{2,1,0:T(8,128)(2,1)S(1)}, u32[]{:S(2)}, u32[]{:S(2)}) async-start(bf16[32,32,128]{2,1,0:T(8,128)(2,1)} %get-tuple-element.23), calls=%async_computation.3 | async-start | bytes 524288 | tf_op jit(solution)/shard_map/all_to_all | solution.py:337
  93.5 0.8 shard_map.91
  94.3 7.5 %all-to-all-done.3.got = bf16[32,32,128]{2,1,0:T(8,128)(2,1)S(1)} async-done(((bf16[32,32,128]{2,1,0:T(8,128)(2,1)}), bf16[32,32,128]{2,1,0:T(8,128)(2,1)S(1)}, u32[]{:S(2)}, u32[]{:S(2)}) %all-to-all-start.3) | async-done | bytes 262176 | tf_op jit(solution)/shard_map/all_to_all | solution.py:337
  101.8 2.8 %shard_map.92 = (f32[16,128]{1,0:T(8,128)S(1)}, bf16[16,16,128]{2,1,0:T(8,128)(2,1)S(1)}) custom-call(f32[8,128]{1,0:T(8,128)S(1)} %get-tuple-element.18.coef, bf16[32,32,128]{2,1,0:T(8,128)(2,1)S(1)} %all-to-all-done.3.got, f32[2,16,128]{2,1,0:T(8,128)S(1)} %get-tuple-element.24.latents, bf16[5,128,128]{2,1,0:T(8,128)(2,1)S(1)} %get-tuple-element.20.table, ...), custom_call_target="tpu_custom_call" | custom-call | tf_op jit(solution)/shard_map/pallas_call | solution.py:67
  104.6 14.2 %all_to_all.32.got = bf16[16,16,128]{2,1,0:T(8,128)(2,1)S(1)} all-to-all(bf16[16,16,128]{2,1,0:T(8,128)(2,1)S(1)} %get-tuple-element.28), channel_id=1, replica_groups=mesh['z'=16,'core'=2,'y'=4,'x'=4] {'z'}, dimensions={0} | all-to-all | bytes 131072 | tf_op jit(solution)/shard_map/all_to_all | solution.py:350
  118.8 0.7 shard_map.93
  119.6 6.2 %all-to-all-start.5 = ((f32[32,8,128]{2,1,0:T(8,128)}), f32[32,8,128]{2,1,0:T(8,128)S(1)}, u32[]{:S(2)}, u32[]{:S(2)}) async-start(f32[32,8,128]{2,1,0:T(8,128)} %get-tuple-element.30), calls=%async_computation.5 | async-start | bytes 262144 | tf_op jit(solution)/shard_map/all_to_all | solution.py:354
  125.7 1.8 %all-gather.2 = f32[4,16,128]{2,1,0:T(8,128)S(1)} all-gather(f32[2,16,128]{2,1,0:T(8,128)S(1)} %get-tuple-element.31), channel_id=4, replica_groups=mesh['z'=16,'core'=2,'y'=4,'x'=4] {'core'}, dimensions={0}, use_global_device_ids=true | all-gather | bytes 49152 | tf_op jit(solution)/shard_map/all_gather | solution.py:355
  127.6 5.7 %all-to-all-done.5.got = f32[32,8,128]{2,1,0:T(8,128)S(1)} async-done(((f32[32,8,128]{2,1,0:T(8,128)}), f32[32,8,128]{2,1,0:T(8,128)S(1)}, u32[]{:S(2)}, u32[]{:S(2)}) %all-to-all-start.5) | async-done | bytes 131104 | tf_op jit(solution)/shard_map/all_to_all | solution.py:354
  133.3 0.7 shard_map.94
Async XLA Ops:
  0.6 1.0 copy-start.1
  1.6 0.9 copy-start.2
  2.5 0.9 copy-start.4
  4.8 15.9 %copy-start.3 = (bf16[1536,64]{0,1:T(8,128)(2,1)S(1)}, bf16[1536,64]{0,1:T(8,128)(2,1)}, u32[]{:S(2)}) copy-start(bf16[1536,64]{0,1:T(8,128)(2,1)} %param.13) | copy-start | bytes 589828
  4.9 15.9 %copy-start.5 = (bf16[64,1536]{1,0:T(8,128)(2,1)S(1)}, bf16[64,1536]{1,0:T(8,128)(2,1)}, u32[]{:S(2)}) copy-start(bf16[64,1536]{1,0:T(8,128)(2,1)} %w_in.1) | copy-start | bytes 589828
  4.9 15.9 %copy-start.6 = (bf16[1,3072]{1,0:T(2,128)(2,1)S(1)}, bf16[1,3072]{1,0:T(2,128)(2,1)}, u32[]{:S(2)}) copy-start(bf16[1,3072]{1,0:T(2,128)(2,1)} %modulation.1) | copy-start | bytes 18436
  4.9 15.9 %copy-start.7 = (s32[33]{0:T(128)S(1)}, s32[33]{0:T(128)}, u32[]{:S(2)}) copy-start(s32[33]{0:T(128)} %timesteps.1) | copy-start | bytes 400
  4.9 33.9 %all-to-all-start = ((bf16[16,96,128]{2,1,0:T(8,128)(2,1)}), bf16[16,96,128]{2,1,0:T(8,128)(2,1)S(1)}, u32[]{:S(2)}, u32[]{:S(2)}) async-start(bf16[16,96,128]{2,1,0:T(8,128)(2,1)} %shard_map.87), calls=%async_computation | async-start | bytes 786432 | tf_op jit(solution)/shard_map/all_to_all | solution.py:312
  22.1 25.4 %copy-start = (f32[64,64]{1,0:T(8,128)S(1)}, f32[64,64]{1,0:T(8,128)}, u32[]{:S(2)}) copy-start(f32[64,64]{1,0:T(8,128)} %start.7) | copy-start | bytes 49156
  87.9 13.9 %all-to-all-start.3 = ((bf16[32,32,128]{2,1,0:T(8,128)(2,1)}), bf16[32,32,128]{2,1,0:T(8,128)(2,1)S(1)}, u32[]{:S(2)}, u32[]{:S(2)}) async-start(bf16[32,32,128]{2,1,0:T(8,128)(2,1)} %get-tuple-element.23), calls=%async_computation.3 | async-start | bytes 524288 | tf_op jit(solution)/shard_map/all_to_all | solution.py:337
  119.6 13.7 %all-to-all-start.5 = ((f32[32,8,128]{2,1,0:T(8,128)}), f32[32,8,128]{2,1,0:T(8,128)S(1)}, u32[]{:S(2)}, u32[]{:S(2)}) async-start(f32[32,8,128]{2,1,0:T(8,128)} %get-tuple-element.30), calls=%async_computation.5 | async-start | bytes 262144 | tf_op jit(solution)/shard_map/all_to_all | solution.py:354

commit v4 on v3

--- a/solution.py
+++ b/solution.py
@@ -42,9 +42,16 @@
     return jnp.dot(a, b, preferred_element_type=F32)
 
 
-def unpack(packed):
-    low = lanes(packed.shape) < C
-    return jnp.concatenate([jnp.where(low, packed, 0.0), jnp.where(low, pltpu.roll(packed, C, 1), 0.0)], axis=0)
+def unpack(packed, after=0.0):
+    lane = lanes(packed.shape)
+    low = lane < C
+    rest = jnp.where(lane == C, after, 0.0)
+    return jnp.concatenate([jnp.where(low, packed, rest), jnp.where(low, pltpu.roll(packed, C, 1), rest)], axis=0)
+
+
+def pack(values):
+    half = values.shape[0] // 2
+    return jnp.where(lanes((half, 2 * C)) < C, values[:half], pltpu.roll(values[half:], C, 1))
 
 
 def pack_high(values):
@@ -62,8 +69,8 @@
     return pieces
 
 
-def call(kernel, outs, args, scratch=(), smem=(), anywhere=(), flops=0):
-    spaces = [pltpu.SMEM if at in smem else pl.ANY if at in anywhere else pltpu.VMEM for at in range(len(args))]
+def call(kernel, outs, args, scratch=(), smem=(), far=(), flops=0):
+    spaces = [pltpu.SMEM if at in smem else pltpu.HBM if at in far else pltpu.VMEM for at in range(len(args))]
     return pl.pallas_call(
         kernel,
         out_shape=outs,
@@ -143,7 +150,7 @@
         table[at, C : 2 * C, :] = jnp.zeros((C, 2 * C), BF)
 
 
-def make_heads(both, left, start, out, qk, vw):
+def make_heads(both, left, start, table, out, qk, vw):
     _, core, seq = place()
     for z in range(Z):
         for parity in range(2):
@@ -160,7 +167,7 @@
     bias = jnp.concatenate([bias, jnp.zeros((8, 128 - bias.shape[1]), F32)], axis=1)[0:1]
     main = jnp.concatenate([a[:, :C], b], axis=1)
     main = jnp.where(rows(main.shape) == C + 1, bias, main).astype(BF)
-    x = packed_start(start, core).astype(BF)
+    x = pack(normalized(unpack(packed_start(start, core).astype(BF).astype(F32)), table)).astype(BF)
     for to in range(PEERS // 2):
         out[to, 0:80, :] = main
         out[to, 80:96, :] = x
@@ -219,7 +226,7 @@
     x = start[pl.ds(pl.multiple_of(core * 32, 32), 32), :].astype(BF).astype(F32)
     x = jnp.concatenate([x, jnp.zeros_like(x)], axis=1)
     everything = got[:, :, 80:96, :].astype(F32).reshape(PEERS * 16, 128)
-    key[...] = normalized(unpack(everything), table).astype(BF)
+    key[...] = unpack(everything, 1.0).astype(BF)
     ask((0, 1), heads, table, x, query, direct)
     eps = [attend(step, heads, query, direct, key, weight, mix) for step in range(2)]
     first_eps[...] = eps[0]
@@ -240,16 +247,17 @@
     return total
 
 
-def first_prefix(coef, got, start, first_eps, latents, out):
+def first_prefix(coef, got, start, first_eps, table, latents, out):
     z, core, _ = place()
     x = packed_start(start, core)
     even = x + coef[4:5] * x + below(got, z)
     odd = even + coef[0:1] * x + coef[2:3] * first_eps[...]
     latents[0] = even
     latents[1] = odd
+    sent = [pack(normalized(unpack(x.astype(BF).astype(F32)), table)).astype(BF) for x in (even, odd)]
     for to in range(PEERS):
-        out[to, 0:16, :] = even.astype(BF)
-        out[to, 16:32, :] = odd.astype(BF)
+        out[to, 0:16, :] = sent[0]
+        out[to, 16:32, :] = sent[1]
 
 
 def second_queries(latents, table, heads, query, direct):
@@ -261,7 +269,7 @@
     terms = []
     for step in range(2):
         everything = got[:, 16 * step : 16 * step + 16, :].astype(F32).reshape(PEERS * 16, 128)
-        key[...] = normalized(unpack(everything), table).astype(BF)
+        key[...] = unpack(everything, 1.0).astype(BF)
         eps = attend(step, heads, query, direct, key, weight, mix)
         terms.append(coef[step : step + 1] * latents[step] + coef[2 + step : 3 + step] * eps)
     term[...] = terms[0]
@@ -307,7 +315,7 @@
             pltpu.VMEM((C, D), BF),
             pltpu.SemaphoreType.DMA((5,)),
         ),
-        anywhere=(0, 1, 2),
+        far=(0, 1, 2),
     )
     got = lax.all_to_all(sent, "z", 0, 0, tiled=True)
     left, table, coef = call(
@@ -320,7 +328,7 @@
     sent = call(
         make_heads,
         shape((PEERS // 2, 96, 128), BF),
-        (lax.all_gather(got, "core"), left, start),
+        (lax.all_gather(got, "core"), left, start, table),
         scratch=(pltpu.VMEM((D, 128), BF), pltpu.VMEM((D, 128), BF)),
     )
     got = lax.all_gather(lax.all_to_all(sent, ("y", "x"), 0, 0, tiled=True), "core")
@@ -332,7 +340,7 @@
     )
     got = lax.all_to_all(sent, "z", 0, 0, tiled=True)
     latents, sent = call(
-        first_prefix, (shape((2, 16, 128), F32), shape((PEERS, 32, 128), BF)), (coef, got, start, first_eps)
+        first_prefix, (shape((2, 16, 128), F32), shape((PEERS, 32, 128), BF)), (coef, got, start, first_eps, table)
     )
     got = lax.all_to_all(sent, FLAT, 0, 0, tiled=True)
     query, direct = call(

time: 135 us -> 134 us (level)
  no operation moved by 1% of the time
where the time goes in v4:
time: 134 us; the launch traced here: 133 us
  blocking collectives  61.6 us (46%)
  waiting for transfers between devices  29.9 us (22%)
  starting transfers between devices  27.7 us (21%)
  Pallas kernels  10.7 us (8%)
  local copies, waits for them, and re-layouts  2.8 us (2%)
    all_to_all x2, blocking collectives, body(): got = lax.all_to_all(sent, 'z', 0, 0, tiled=True)  31.4 us
    all_to_all x1, waiting for transfers between devices, body(): got = lax.all_to_all(sent, 'z', 0, 0, tiled=True)  16.7 us
    all_to_all x1, blocking collectives, body(): lax.all_to_all(sent, ('y', 'x'), 0, 0, tiled=True)  16.1 us
    all_to_all x1, starting transfers between devices, body(): got = lax.all_to_all(sent, 'z', 0, 0, tiled=True)  15.9 us
    all_to_all x2, waiting for transfers between devices, body(): got = lax.all_to_all(sent, FLAT, 0, 0, tiled=True)  13.2 us
    all_to_all x2, starting transfers between devices, body(): got = lax.all_to_all(sent, FLAT, 0, 0, tiled=True)  11.8 us
    pallas_call x9, Pallas kernels, call(): pl.pallas_call(kernel, out_shape=outs, in_specs=[pl.BlockSpec(memory_spac...  10.7 us
    all_gather x1, blocking collectives, body(): lax.all_gather(got, 'core')  8.71 us
  transfers between devices with their start and end apart: 3, of which 3 were waited for; matrix products, arithmetic and copies ran while one was open for 0% of the time, Pallas kernels for 2%

profile of v4, /device:TPU:1, one launch (start us, length us, event | category | flops | bytes accessed | tf_op | source)
XLA Modules:
  0.0 133.4 jit_solution(34429441744033892)
XLA Ops:
  0.6 0.0 copy-start.1
  0.6 1.0 copy-done.1
  1.6 0.0 copy-start.2
  1.6 0.9 copy-done.2
  2.5 0.0 copy-start.4
  2.5 0.9 copy-done.4
  3.4 1.4 %shard_map.87 = bf16[16,96,128]{2,1,0:T(8,128)(2,1)} custom-call(bf16[48,3072]{1,0:T(8,128)(2,1)S(1)} %copy-done.1, bf16[32,1536]{1,0:T(8,128)(2,1)S(1)} %copy-done.4, bf16[64,1536]{1,0:T(8,128)(2,1)S(1)} %bitcast.7), custom_call_target="tpu_custom_call" | custom-call | tf_op jit(solution)/shard_map/pallas_call | solution.py:74
  4.8 0.0 copy-start.3
  4.9 0.0 copy-start.5
  4.9 0.0 copy-start.6
  4.9 0.0 copy-start.7
  4.9 15.9 %all-to-all-start = ((bf16[16,96,128]{2,1,0:T(8,128)(2,1)}), bf16[16,96,128]{2,1,0:T(8,128)(2,1)S(1)}, u32[]{:S(2)}, u32[]{:S(2)}) async-start(bf16[16,96,128]{2,1,0:T(8,128)(2,1)} %shard_map.87), calls=%async_computation | async-start | bytes 786432 | tf_op jit(solution)/shard_map/all_to_all | solution.py:320
  20.8 0.0 copy-done.3
  20.8 0.0 copy-done.5
  20.8 0.0 copy-done.6
  20.8 0.0 copy-done.7
  20.8 1.3 shard_map.86
  22.1 0.0 copy-start
  22.1 16.7 %all-to-all-done = bf16[16,96,128]{2,1,0:T(8,128)(2,1)S(1)} async-done(((bf16[16,96,128]{2,1,0:T(8,128)(2,1)}), bf16[16,96,128]{2,1,0:T(8,128)(2,1)S(1)}, u32[]{:S(2)}, u32[]{:S(2)}) %all-to-all-start) | async-done | bytes 393248 | tf_op jit(solution)/shard_map/all_to_all | solution.py:320
  38.8 8.7 %all-gather = bf16[32,96,128]{2,1,0:T(8,128)(2,1)S(1)} all-gather(bf16[16,96,128]{2,1,0:T(8,128)(2,1)S(1)} %all-to-all-done), channel_id=2, replica_groups=mesh['z'=16,'core'=2,'y'=4,'x'=4] {'core'}, dimensions={0}, use_global_device_ids=true | all-gather | bytes 1179648 | tf_op jit(solution)/shard_map/all_gather | solution.py:331
  47.5 0.0 copy-done
  47.5 0.8 shard_map.88
  48.3 16.1 %all_to_all.30 = bf16[16,96,128]{2,1,0:T(8,128)(2,1)S(1)} all-to-all(bf16[16,96,128]{2,1,0:T(8,128)(2,1)S(1)} %shard_map.88), channel_id=1, replica_groups=mesh['z'=16,'core'=2,'y'=4,'x'=4] {'y','x'}, dimensions={0} | all-to-all | bytes 786432 | tf_op jit(solution)/shard_map/all_to_all | solution.py:334
  64.3 3.5 %all-gather.1 = bf16[32,96,128]{2,1,0:T(8,128)(2,1)S(1)} all-gather(bf16[16,96,128]{2,1,0:T(8,128)(2,1)S(1)} %all_to_all.30), channel_id=3, replica_groups=mesh['z'=16,'core'=2,'y'=4,'x'=4] {'core'}, dimensions={0}, use_global_device_ids=true | all-gather | bytes 1179648 | tf_op jit(solution)/shard_map/all_gather | solution.py:334
  67.8 2.1 %shard_map.89 = (bf16[16,128,128]{2,1,0:T(8,128)(2,1)S(1)}, f32[16,128]{1,0:T(8,128)S(1)}, bf16[16,16,128]{2,1,0:T(8,128)(2,1)S(1)}) custom-call(f32[8,128]{1,0:T(8,128)S(1)} %get-tuple-element.18.coef, bf16[2,16,96,128]{3,2,1,0:T(8,128)(2,1)S(1)} %bitcast.6, f32[64,64]{1,0:T(8,128)S(1)} %copy-done, bf16[5,128,128]{2,1,0:T(8,128)(2,1)S(1)} %get-tuple-element.20.table), custom_call_target="tpu_custom_call" | custom-call | tf_op jit(solution)/shard_map/pallas_call | solution.py:74
  70.0 17.3 %all_to_all.31.got = bf16[16,16,128]{2,1,0:T(8,128)(2,1)S(1)} all-to-all(bf16[16,16,128]{2,1,0:T(8,128)(2,1)S(1)} %get-tuple-element.21), channel_id=1, replica_groups=mesh['z'=16,'core'=2,'y'=4,'x'=4] {'z'}, dimensions={0} | all-to-all | bytes 131072 | tf_op jit(solution)/shard_map/all_to_all | solution.py:341
  87.2 1.2 shard_map.90
  88.4 5.6 %all-to-all-start.3 = ((bf16[32,32,128]{2,1,0:T(8,128)(2,1)}), bf16[32,32,128]{2,1,0:T(8,128)(2,1)S(1)}, u32[]{:S(2)}, u32[]{:S(2)}) async-start(bf16[32,32,128]{2,1,0:T(8,128)(2,1)} %get-tuple-element.23), calls=%async_computation.3 | async-start | bytes 524288 | tf_op jit(solution)/shard_map/all_to_all | solution.py:345
  94.0 0.8 shard_map.91
  94.8 7.5 %all-to-all-done.3.got = bf16[32,32,128]{2,1,0:T(8,128)(2,1)S(1)} async-done(((bf16[32,32,128]{2,1,0:T(8,128)(2,1)}), bf16[32,32,128]{2,1,0:T(8,128)(2,1)S(1)}, u32[]{:S(2)}, u32[]{:S(2)}) %all-to-all-start.3) | async-done | bytes 262176 | tf_op jit(solution)/shard_map/all_to_all | solution.py:345
  102.3 1.7 %shard_map.92 = (f32[16,128]{1,0:T(8,128)S(1)}, bf16[16,16,128]{2,1,0:T(8,128)(2,1)S(1)}) custom-call(f32[8,128]{1,0:T(8,128)S(1)} %get-tuple-element.18.coef, bf16[32,32,128]{2,1,0:T(8,128)(2,1)S(1)} %all-to-all-done.3.got, f32[2,16,128]{2,1,0:T(8,128)S(1)} %get-tuple-element.24.latents, bf16[5,128,128]{2,1,0:T(8,128)(2,1)S(1)} %get-tuple-element.20.table, ...), custom_call_target="tpu_custom_call" | custom-call | tf_op jit(solution)/shard_map/pallas_call | solution.py:74
  104.0 14.2 %all_to_all.32.got = bf16[16,16,128]{2,1,0:T(8,128)(2,1)S(1)} all-to-all(bf16[16,16,128]{2,1,0:T(8,128)(2,1)S(1)} %get-tuple-element.28), channel_id=1, replica_groups=mesh['z'=16,'core'=2,'y'=4,'x'=4] {'z'}, dimensions={0} | all-to-all | bytes 131072 | tf_op jit(solution)/shard_map/all_to_all | solution.py:358
  118.2 0.7 shard_map.93
  118.9 6.2 %all-to-all-start.5 = ((f32[32,8,128]{2,1,0:T(8,128)}), f32[32,8,128]{2,1,0:T(8,128)S(1)}, u32[]{:S(2)}, u32[]{:S(2)}) async-start(f32[32,8,128]{2,1,0:T(8,128)} %get-tuple-element.30), calls=%async_computation.5 | async-start | bytes 262144 | tf_op jit(solution)/shard_map/all_to_all | solution.py:362
  125.1 1.8 %all-gather.2 = f32[4,16,128]{2,1,0:T(8,128)S(1)} all-gather(f32[2,16,128]{2,1,0:T(8,128)S(1)} %get-tuple-element.31), channel_id=4, replica_groups=mesh['z'=16,'core'=2,'y'=4,'x'=4] {'core'}, dimensions={0}, use_global_device_ids=true | all-gather | bytes 49152 | tf_op jit(solution)/shard_map/all_gather | solution.py:363
  127.0 5.7 %all-to-all-done.5.got = f32[32,8,128]{2,1,0:T(8,128)S(1)} async-done(((f32[32,8,128]{2,1,0:T(8,128)}), f32[32,8,128]{2,1,0:T(8,128)S(1)}, u32[]{:S(2)}, u32[]{:S(2)}) %all-to-all-start.5) | async-done | bytes 131104 | tf_op jit(solution)/shard_map/all_to_all | solution.py:362
  132.7 0.7 shard_map.94
Async XLA Ops:
  0.6 1.0 copy-start.1
  1.6 0.9 copy-start.2
  2.5 0.9 copy-start.4
  4.8 15.9 %copy-start.3 = (bf16[1536,64]{0,1:T(8,128)(2,1)S(1)}, bf16[1536,64]{0,1:T(8,128)(2,1)}, u32[]{:S(2)}) copy-start(bf16[1536,64]{0,1:T(8,128)(2,1)} %param.13) | copy-start | bytes 589828
  4.9 15.9 %copy-start.5 = (bf16[64,1536]{1,0:T(8,128)(2,1)S(1)}, bf16[64,1536]{1,0:T(8,128)(2,1)}, u32[]{:S(2)}) copy-start(bf16[64,1536]{1,0:T(8,128)(2,1)} %w_in.1) | copy-start | bytes 589828
  4.9 15.9 %copy-start.6 = (bf16[1,3072]{1,0:T(2,128)(2,1)S(1)}, bf16[1,3072]{1,0:T(2,128)(2,1)}, u32[]{:S(2)}) copy-start(bf16[1,3072]{1,0:T(2,128)(2,1)} %modulation.1) | copy-start | bytes 18436
  4.9 15.9 %copy-start.7 = (s32[33]{0:T(128)S(1)}, s32[33]{0:T(128)}, u32[]{:S(2)}) copy-start(s32[33]{0:T(128)} %timesteps.1) | copy-start | bytes 400
  4.9 33.9 %all-to-all-start = ((bf16[16,96,128]{2,1,0:T(8,128)(2,1)}), bf16[16,96,128]{2,1,0:T(8,128)(2,1)S(1)}, u32[]{:S(2)}, u32[]{:S(2)}) async-start(bf16[16,96,128]{2,1,0:T(8,128)(2,1)} %shard_map.87), calls=%async_computation | async-start | bytes 786432 | tf_op jit(solution)/shard_map/all_to_all | solution.py:320
  22.1 25.4 %copy-start = (f32[64,64]{1,0:T(8,128)S(1)}, f32[64,64]{1,0:T(8,128)}, u32[]{:S(2)}) copy-start(f32[64,64]{1,0:T(8,128)} %start.7) | copy-start | bytes 49156
  88.4 13.9 %all-to-all-start.3 = ((bf16[32,32,128]{2,1,0:T(8,128)(2,1)}), bf16[32,32,128]{2,1,0:T(8,128)(2,1)S(1)}, u32[]{:S(2)}, u32[]{:S(2)}) async-start(bf16[32,32,128]{2,1,0:T(8,128)(2,1)} %get-tuple-element.23), calls=%async_computation.3 | async-start | bytes 524288 | tf_op jit(solution)/shard_map/all_to_all | solution.py:345
  118.9 13.7 %all-to-all-start.5 = ((f32[32,8,128]{2,1,0:T(8,128)}), f32[32,8,128]{2,1,0:T(8,128)S(1)}, u32[]{:S(2)}, u32[]{:S(2)}) async-start(f32[32,8,128]{2,1,0:T(8,128)} %get-tuple-element.30), calls=%async_computation.5 | async-start | bytes 262144 | tf_op jit(solution)/shard_map/all_to_all | solution.py:362

commit v5 on v4

--- a/solution.py
+++ b/solution.py
@@ -69,15 +69,15 @@
     return pieces
 
 
-def call(kernel, outs, args, scratch=(), smem=(), far=(), flops=0):
-    spaces = [pltpu.SMEM if at in smem else pltpu.HBM if at in far else pltpu.VMEM for at in range(len(args))]
+def call(kernel, outs, args, scratch=(), smem=(), far=(), flops=0, grant=40):
+    spaces = [pltpu.SMEM if at in smem else pl.ANY if at in far else pltpu.VMEM for at in range(len(args))]
     return pl.pallas_call(
         kernel,
         out_shape=outs,
         in_specs=[pl.BlockSpec(memory_space=space) for space in spaces],
         out_specs=jax.tree.map(lambda _: pl.BlockSpec(memory_space=pltpu.VMEM), outs),
         scratch_shapes=scratch,
-        compiler_params=pltpu.CompilerParams(vmem_limit_bytes=40 * 1024 * 1024),
+        compiler_params=pltpu.CompilerParams(vmem_limit_bytes=grant * 1024 * 1024),
         cost_estimate=pl.CostEstimate(flops=flops, bytes_accessed=0, transcendentals=0) if flops else None,
     )(*args)
 
@@ -102,13 +102,18 @@
         block = blocks[at].astype(F32)
         return jnp.where(odd, block[:, C:], block[:, :C])
 
+    first = jnp.concatenate([columns(0), columns(1)], axis=1).astype(BF)
+    at, to = rows((HEAD_DIM, C)), lanes((HEAD_DIM, C))
+    wanted = (to // 16) * 32 + to % 16 + jnp.where(odd, 16, 0)
+    value = dot(blocks[2], jnp.where(at == wanted, 1.0, 0.0).astype(BF))
     head = lax.dot_general(left[...], right[...], NT, preferred_element_type=F32)
-    head = jnp.concatenate([head, jnp.zeros((ROWS - head.shape[0], C), F32)], axis=0)
-    first = jnp.concatenate([columns(0), columns(1)], axis=1).astype(BF)
-    second = jnp.concatenate([columns(2), head], axis=1).astype(BF)
+    head = jnp.where(odd, head[16:], head[:16])
+    second = jnp.concatenate([value[0:16], value[16:32]], axis=1).astype(BF)
+    third = jnp.concatenate([value[32:48], head], axis=1).astype(BF)
     for to in range(Z):
-        out[to, 0:ROWS, :] = first
-        out[to, ROWS : 2 * ROWS, :] = second
+        out[to, 0:48, :] = first
+        out[to, 48:64, :] = second
+        out[to, 64:80, :] = third
 
 
 def coefficients(timesteps):
@@ -154,13 +159,18 @@
     _, core, seq = place()
     for z in range(Z):
         for parity in range(2):
-            at = pl.ds((z * 2 + parity) * ROWS, ROWS)
-            qk[at, :] = both[parity, z, 0:ROWS, :]
-            vw[at, :] = both[parity, z, ROWS : 2 * ROWS, :]
+            at = (z * 2 + parity) * ROWS
+            qk[at : at + 48, :] = both[parity, z, 0:48, :]
+            values = both[parity, z, 48:64, :]
+            vw[at : at + 16, :] = values
+            vw[at + 16 : at + 32, :] = pltpu.roll(values.astype(F32), C, 1).astype(BF)
+            vw[at + 32 : at + 48, :] = both[parity, z, 64:80, :]
     first = dot(left[...], qk[...])
     value = dot(left[...], vw[...])[:, :C]
     query, key = first[:, :C], first[:, C:]
-    head = both[:, seq, ROWS : ROWS + 32, C:].astype(F32).reshape(C, C)
+    even = seq - lax.rem(seq, 2)
+    head = [both[group % 2, even + group // 2, 64:80, C:].astype(F32) for group in range(4)]
+    head = jnp.concatenate(head, axis=0)
     a = lax.dot_general(query, key, NT, precision=BEST, preferred_element_type=F32) * SCALE
     b = jnp.dot(value, head, precision=BEST, preferred_element_type=F32)
     bias = lax.dot_general(key[C : C + 8], query, NT, precision=BEST, preferred_element_type=F32) * SCALE
@@ -210,7 +220,7 @@
 
 def work_space():
     return (
-        pltpu.VMEM((TOKENS, 128), BF),
+        pltpu.VMEM((2, TOKENS, 128), BF),
         pltpu.VMEM((2, HEADS * 32, TOKENS), BF),
         pltpu.VMEM((2, HEADS * 32, 128), BF),
     )
@@ -226,9 +236,9 @@
     x = start[pl.ds(pl.multiple_of(core * 32, 32), 32), :].astype(BF).astype(F32)
     x = jnp.concatenate([x, jnp.zeros_like(x)], axis=1)
     everything = got[:, :, 80:96, :].astype(F32).reshape(PEERS * 16, 128)
-    key[...] = unpack(everything, 1.0).astype(BF)
+    key[0] = unpack(everything, 1.0).astype(BF)
     ask((0, 1), heads, table, x, query, direct)
-    eps = [attend(step, heads, query, direct, key, weight, mix) for step in range(2)]
+    eps = [attend(step, heads, query, direct, key.at[0], weight, mix) for step in range(2)]
     first_eps[...] = eps[0]
     both = (coef[2:3] * eps[0] + coef[3:4] * eps[1]).astype(BF)
     for to in range(Z):
@@ -269,8 +279,8 @@
     terms = []
     for step in range(2):
         everything = got[:, 16 * step : 16 * step + 16, :].astype(F32).reshape(PEERS * 16, 128)
-        key[...] = unpack(everything, 1.0).astype(BF)
-        eps = attend(step, heads, query, direct, key, weight, mix)
+        key[step] = unpack(everything, 1.0).astype(BF)
+        eps = attend(step, heads, query, direct, key.at[step], weight, mix)
         terms.append(coef[step : step + 1] * latents[step] + coef[2 + step : 3 + step] * eps)
     term[...] = terms[0]
     both = (terms[0] + terms[1]).astype(BF)
@@ -307,7 +317,7 @@
 def body(start, timesteps, modulation, w_in, w_qkv, w_o, w_out):
     sent = call(
         send_weights,
-        shape((Z, 96, 128), BF),
+        shape((Z, 80, 128), BF),
         (w_qkv, w_o, w_out.T),
         scratch=(
             pltpu.VMEM((3, ROWS, HEAD_DIM), BF),
@@ -316,6 +326,7 @@
             pltpu.SemaphoreType.DMA((5,)),
         ),
         far=(0, 1, 2),
+        grant=62,
     )
     got = lax.all_to_all(sent, "z", 0, 0, tiled=True)
     left, table, coef = call(

time: 134 us -> 129 us (0.963)
  waiting for transfers between devices: 29.9 us -> 27.1 us
  local copies, waits for them, and re-layouts: 2.8 us -> 0.03 us
    all_to_all x1, waiting for transfers between devices: 16.7 us -> 13.9 us  [body(): got = lax.all_to_all(sent, 'z', 0, 0, tiled=True)]
    unnamed x16 -> x10, local copies, waits for them, and re-layouts: 2.8 us -> 0.03 us
where the time goes in v5:
time: 129 us; the launch traced here: 128 us
  blocking collectives  61.4 us (48%)
  starting transfers between devices  27.7 us (21%)
  waiting for transfers between devices  27.1 us (21%)
  Pallas kernels  11.3 us (9%)
    all_to_all x2, blocking collectives, body(): got = lax.all_to_all(sent, 'z', 0, 0, tiled=True)  31.6 us
    all_to_all x1, blocking collectives, body(): lax.all_to_all(sent, ('y', 'x'), 0, 0, tiled=True)  16.1 us
    all_to_all x1, starting transfers between devices, body(): got = lax.all_to_all(sent, 'z', 0, 0, tiled=True)  15.9 us
    all_to_all x1, waiting for transfers between devices, body(): got = lax.all_to_all(sent, 'z', 0, 0, tiled=True)  13.9 us
    all_to_all x2, waiting for transfers between devices, body(): got = lax.all_to_all(sent, FLAT, 0, 0, tiled=True)  13.2 us
    all_to_all x2, starting transfers between devices, body(): got = lax.all_to_all(sent, FLAT, 0, 0, tiled=True)  11.8 us
    pallas_call x9, Pallas kernels, call(): pl.pallas_call(kernel, out_shape=outs, in_specs=[pl.BlockSpec(memory_spac...  11.3 us
    all_gather x1, blocking collectives, body(): lax.all_gather(got, 'core')  8.39 us
  transfers between devices with their start and end apart: 3, of which 3 were waited for; matrix products, arithmetic and copies ran while one was open for 0% of the time, Pallas kernels for 2%

profile of v5, /device:TPU:1, one launch (start us, length us, event | category | flops | bytes accessed | tf_op | source)
XLA Modules:
  0.0 128.4 jit_solution(7341937249195661144)
XLA Ops:
  0.6 2.0 %shard_map.87 = bf16[16,80,128]{2,1,0:T(8,128)(2,1)} custom-call(bf16[48,3072]{1,0:T(8,128)(2,1)} %w_qkv.1, bf16[32,1536]{1,0:T(8,128)(2,1)} %w_o.1, bf16[64,1536]{1,0:T(8,128)(2,1)} %bitcast.7), custom_call_target="tpu_custom_call" | custom-call | tf_op jit(solution)/shard_map/pallas_call | solution.py:74
  2.7 0.0 copy-start.1
  2.7 0.0 copy-start.2
  2.7 0.0 copy-start.3
  2.7 0.0 copy-start.4
  2.7 15.9 %all-to-all-start = ((bf16[16,80,128]{2,1,0:T(8,128)(2,1)}), bf16[16,80,128]{2,1,0:T(8,128)(2,1)S(1)}, u32[]{:S(2)}, u32[]{:S(2)}) async-start(bf16[16,80,128]{2,1,0:T(8,128)(2,1)} %shard_map.87), calls=%async_computation | async-start | bytes 655360 | tf_op jit(solution)/shard_map/all_to_all | solution.py:331
  18.6 0.0 copy-done.1
  18.6 0.0 copy-done.2
  18.6 0.0 copy-done.3
  18.6 0.0 copy-done.4
  18.6 1.3 shard_map.86
  19.9 0.0 copy-start
  19.9 13.9 %all-to-all-done = bf16[16,80,128]{2,1,0:T(8,128)(2,1)S(1)} async-done(((bf16[16,80,128]{2,1,0:T(8,128)(2,1)}), bf16[16,80,128]{2,1,0:T(8,128)(2,1)S(1)}, u32[]{:S(2)}, u32[]{:S(2)}) %all-to-all-start) | async-done | bytes 327712 | tf_op jit(solution)/shard_map/all_to_all | solution.py:331
  33.8 8.4 %all-gather = bf16[32,80,128]{2,1,0:T(8,128)(2,1)S(1)} all-gather(bf16[16,80,128]{2,1,0:T(8,128)(2,1)S(1)} %all-to-all-done), channel_id=2, replica_groups=mesh['z'=16,'core'=2,'y'=4,'x'=4] {'core'}, dimensions={0}, use_global_device_ids=true | all-gather | bytes 983040 | tf_op jit(solution)/shard_map/all_gather | solution.py:342
  42.2 0.0 copy-done
  42.2 0.8 shard_map.88
  43.0 16.1 %all_to_all.30 = bf16[16,96,128]{2,1,0:T(8,128)(2,1)S(1)} all-to-all(bf16[16,96,128]{2,1,0:T(8,128)(2,1)S(1)} %shard_map.88), channel_id=1, replica_groups=mesh['z'=16,'core'=2,'y'=4,'x'=4] {'y','x'}, dimensions={0} | all-to-all | bytes 786432 | tf_op jit(solution)/shard_map/all_to_all | solution.py:345
  59.1 3.5 %all-gather.1 = bf16[32,96,128]{2,1,0:T(8,128)(2,1)S(1)} all-gather(bf16[16,96,128]{2,1,0:T(8,128)(2,1)S(1)} %all_to_all.30), channel_id=3, replica_groups=mesh['z'=16,'core'=2,'y'=4,'x'=4] {'core'}, dimensions={0}, use_global_device_ids=true | all-gather | bytes 1179648 | tf_op jit(solution)/shard_map/all_gather | solution.py:345
  62.6 2.1 %shard_map.89 = (bf16[16,128,128]{2,1,0:T(8,128)(2,1)S(1)}, f32[16,128]{1,0:T(8,128)S(1)}, bf16[16,16,128]{2,1,0:T(8,128)(2,1)S(1)}) custom-call(f32[8,128]{1,0:T(8,128)S(1)} %get-tuple-element.18.coef, bf16[2,16,96,128]{3,2,1,0:T(8,128)(2,1)S(1)} %bitcast.5, f32[64,64]{1,0:T(8,128)S(1)} %copy-done, bf16[5,128,128]{2,1,0:T(8,128)(2,1)S(1)} %get-tuple-element.20.table), custom_call_target="tpu_custom_call" | custom-call | tf_op jit(solution)/shard_map/pallas_call | solution.py:74
  64.7 17.4 %all_to_all.31.got = bf16[16,16,128]{2,1,0:T(8,128)(2,1)S(1)} all-to-all(bf16[16,16,128]{2,1,0:T(8,128)(2,1)S(1)} %get-tuple-element.21), channel_id=1, replica_groups=mesh['z'=16,'core'=2,'y'=4,'x'=4] {'z'}, dimensions={0} | all-to-all | bytes 131072 | tf_op jit(solution)/shard_map/all_to_all | solution.py:352
  82.2 1.2 shard_map.90
  83.3 5.6 %all-to-all-start.3 = ((bf16[32,32,128]{2,1,0:T(8,128)(2,1)}), bf16[32,32,128]{2,1,0:T(8,128)(2,1)S(1)}, u32[]{:S(2)}, u32[]{:S(2)}) async-start(bf16[32,32,128]{2,1,0:T(8,128)(2,1)} %get-tuple-element.23), calls=%async_computation.3 | async-start | bytes 524288 | tf_op jit(solution)/shard_map/all_to_all | solution.py:356
  88.9 0.8 shard_map.91
  89.7 7.5 %all-to-all-done.3.got = bf16[32,32,128]{2,1,0:T(8,128)(2,1)S(1)} async-done(((bf16[32,32,128]{2,1,0:T(8,128)(2,1)}), bf16[32,32,128]{2,1,0:T(8,128)(2,1)S(1)}, u32[]{:S(2)}, u32[]{:S(2)}) %all-to-all-start.3) | async-done | bytes 262176 | tf_op jit(solution)/shard_map/all_to_all | solution.py:356
  97.2 1.8 %shard_map.92 = (f32[16,128]{1,0:T(8,128)S(1)}, bf16[16,16,128]{2,1,0:T(8,128)(2,1)S(1)}) custom-call(f32[8,128]{1,0:T(8,128)S(1)} %get-tuple-element.18.coef, bf16[32,32,128]{2,1,0:T(8,128)(2,1)S(1)} %all-to-all-done.3.got, f32[2,16,128]{2,1,0:T(8,128)S(1)} %get-tuple-element.24.latents, bf16[5,128,128]{2,1,0:T(8,128)(2,1)S(1)} %get-tuple-element.20.table, ...), custom_call_target="tpu_custom_call" | custom-call | tf_op jit(solution)/shard_map/pallas_call | solution.py:74
  99.0 14.2 %all_to_all.32.got = bf16[16,16,128]{2,1,0:T(8,128)(2,1)S(1)} all-to-all(bf16[16,16,128]{2,1,0:T(8,128)(2,1)S(1)} %get-tuple-element.28), channel_id=1, replica_groups=mesh['z'=16,'core'=2,'y'=4,'x'=4] {'z'}, dimensions={0} | all-to-all | bytes 131072 | tf_op jit(solution)/shard_map/all_to_all | solution.py:369
  113.2 0.7 shard_map.93
  113.9 6.2 %all-to-all-start.5 = ((f32[32,8,128]{2,1,0:T(8,128)}), f32[32,8,128]{2,1,0:T(8,128)S(1)}, u32[]{:S(2)}, u32[]{:S(2)}) async-start(f32[32,8,128]{2,1,0:T(8,128)} %get-tuple-element.30), calls=%async_computation.5 | async-start | bytes 262144 | tf_op jit(solution)/shard_map/all_to_all | solution.py:373
  120.1 1.8 %all-gather.2 = f32[4,16,128]{2,1,0:T(8,128)S(1)} all-gather(f32[2,16,128]{2,1,0:T(8,128)S(1)} %get-tuple-element.31), channel_id=4, replica_groups=mesh['z'=16,'core'=2,'y'=4,'x'=4] {'core'}, dimensions={0}, use_global_device_ids=true | all-gather | bytes 49152 | tf_op jit(solution)/shard_map/all_gather | solution.py:374
  121.9 5.7 %all-to-all-done.5.got = f32[32,8,128]{2,1,0:T(8,128)S(1)} async-done(((f32[32,8,128]{2,1,0:T(8,128)}), f32[32,8,128]{2,1,0:T(8,128)S(1)}, u32[]{:S(2)}, u32[]{:S(2)}) %all-to-all-start.5) | async-done | bytes 131104 | tf_op jit(solution)/shard_map/all_to_all | solution.py:373
  127.6 0.7 shard_map.94
Async XLA Ops:
  2.7 15.9 %copy-start.1 = (bf16[1536,64]{0,1:T(8,128)(2,1)S(1)}, bf16[1536,64]{0,1:T(8,128)(2,1)}, u32[]{:S(2)}) copy-start(bf16[1536,64]{0,1:T(8,128)(2,1)} %param.13) | copy-start | bytes 589828
  2.7 15.9 %copy-start.2 = (bf16[64,1536]{1,0:T(8,128)(2,1)S(1)}, bf16[64,1536]{1,0:T(8,128)(2,1)}, u32[]{:S(2)}) copy-start(bf16[64,1536]{1,0:T(8,128)(2,1)} %w_in.1) | copy-start | bytes 589828
  2.7 15.9 %copy-start.3 = (bf16[1,3072]{1,0:T(2,128)(2,1)S(1)}, bf16[1,3072]{1,0:T(2,128)(2,1)}, u32[]{:S(2)}) copy-start(bf16[1,3072]{1,0:T(2,128)(2,1)} %modulation.1) | copy-start | bytes 18436
  2.7 15.9 %copy-start.4 = (s32[33]{0:T(128)S(1)}, s32[33]{0:T(128)}, u32[]{:S(2)}) copy-start(s32[33]{0:T(128)} %timesteps.1) | copy-start | bytes 400
  2.7 31.1 %all-to-all-start = ((bf16[16,80,128]{2,1,0:T(8,128)(2,1)}), bf16[16,80,128]{2,1,0:T(8,128)(2,1)S(1)}, u32[]{:S(2)}, u32[]{:S(2)}) async-start(bf16[16,80,128]{2,1,0:T(8,128)(2,1)} %shard_map.87), calls=%async_computation | async-start | bytes 655360 | tf_op jit(solution)/shard_map/all_to_all | solution.py:331
  19.9 22.3 %copy-start = (f32[64,64]{1,0:T(8,128)S(1)}, f32[64,64]{1,0:T(8,128)}, u32[]{:S(2)}) copy-start(f32[64,64]{1,0:T(8,128)} %start.7) | copy-start | bytes 49156
  83.3 13.9 %all-to-all-start.3 = ((bf16[32,32,128]{2,1,0:T(8,128)(2,1)}), bf16[32,32,128]{2,1,0:T(8,128)(2,1)S(1)}, u32[]{:S(2)}, u32[]{:S(2)}) async-start(bf16[32,32,128]{2,1,0:T(8,128)(2,1)} %get-tuple-element.23), calls=%async_computation.3 | async-start | bytes 524288 | tf_op jit(solution)/shard_map/all_to_all | solution.py:356
  113.9 13.7 %all-to-all-start.5 = ((f32[32,8,128]{2,1,0:T(8,128)}), f32[32,8,128]{2,1,0:T(8,128)S(1)}, u32[]{:S(2)}, u32[]{:S(2)}) async-start(f32[32,8,128]{2,1,0:T(8,128)} %get-tuple-element.30), calls=%async_computation.5 | async-start | bytes 262144 | tf_op jit(solution)/shard_map/all_to_all | solution.py:373

commit v6 on v5

--- a/solution.py
+++ b/solution.py
@@ -19,6 +19,11 @@
 PEERS = 32
 ROWS = 48
 FLAT = ("core", "y", "x")
+FIRST_Z = 8
+FIRST_SEQ = 10
+Z_ORDER = [(at + FIRST_Z) % Z for at in range(Z)]
+SEQ_ORDER = [(at + FIRST_SEQ) % 16 for at in range(16)]
+FLAT_ORDER = SEQ_ORDER + [16 + at for at in SEQ_ORDER]
 BF = jnp.bfloat16
 F32 = jnp.float32
 NT = (((1,), (1,)), ((), ()))
@@ -80,6 +85,11 @@
         compiler_params=pltpu.CompilerParams(vmem_limit_bytes=grant * 1024 * 1024),
         cost_estimate=pl.CostEstimate(flops=flops, bytes_accessed=0, transcendentals=0) if flops else None,
     )(*args)
+
+
+def exchange(values, axis):
+    order = {"z": Z_ORDER, ("y", "x"): SEQ_ORDER, FLAT: FLAT_ORDER}[axis]
+    return lax.all_to_all(values, axis, 0, 0, axis_index_groups=[order], tiled=True)
 
 
 def shape(dims, kind):
@@ -157,19 +167,19 @@
 
 def make_heads(both, left, start, table, out, qk, vw):
     _, core, seq = place()
-    for z in range(Z):
+    for rank, z in enumerate(Z_ORDER):
         for parity in range(2):
             at = (z * 2 + parity) * ROWS
-            qk[at : at + 48, :] = both[parity, z, 0:48, :]
-            values = both[parity, z, 48:64, :]
+            qk[at : at + 48, :] = both[parity, rank, 0:48, :]
+            values = both[parity, rank, 48:64, :]
             vw[at : at + 16, :] = values
             vw[at + 16 : at + 32, :] = pltpu.roll(values.astype(F32), C, 1).astype(BF)
-            vw[at + 32 : at + 48, :] = both[parity, z, 64:80, :]
+            vw[at + 32 : at + 48, :] = both[parity, rank, 64:80, :]
     first = dot(left[...], qk[...])
     value = dot(left[...], vw[...])[:, :C]
     query, key = first[:, :C], first[:, C:]
-    even = seq - lax.rem(seq, 2)
-    head = [both[group % 2, even + group // 2, 64:80, C:].astype(F32) for group in range(4)]
+    rank = lax.rem(seq - lax.rem(seq, 2) + Z - FIRST_Z, Z)
+    head = [both[group % 2, rank + group // 2, 64:80, C:].astype(F32) for group in range(4)]
     head = jnp.concatenate(head, axis=0)
     a = lax.dot_general(query, key, NT, precision=BEST, preferred_element_type=F32) * SCALE
     b = jnp.dot(value, head, precision=BEST, preferred_element_type=F32)
@@ -229,8 +239,9 @@
 def first_sweep(coef, got, start, table, heads, first_eps, out, query, direct, key, weight, mix):
     _, core, _ = place()
     for at in range(2 * HEADS):
-        step, source = at // HEADS, 2 * (at % HEADS)
-        both = got[step, source, 0:80, :].astype(F32) + got[step, source + 1, 0:80, :].astype(F32)
+        step, first = at // HEADS, SEQ_ORDER.index(2 * (at % HEADS))
+        second = SEQ_ORDER.index(2 * (at % HEADS) + 1)
+        both = got[step, first, 0:80, :].astype(F32) + got[step, second, 0:80, :].astype(F32)
         heads[at, 0:80, :] = both.astype(BF)
         heads[at, 80:128, :] = jnp.zeros((48, 128), BF)
     x = start[pl.ds(pl.multiple_of(core * 32, 32), 32), :].astype(BF).astype(F32)
@@ -252,8 +263,8 @@
 
 def below(got, z):
     total = jnp.zeros((16, 128), F32)
-    for at in range(Z):
-        total = total + jnp.where(at < z, got[at].astype(F32), 0.0)
+    for rank, at in enumerate(Z_ORDER):
+        total = total + jnp.where(at < z, got[rank].astype(F32), 0.0)
     return total
 
 
@@ -328,7 +339,7 @@
         far=(0, 1, 2),
         grant=62,
     )
-    got = lax.all_to_all(sent, "z", 0, 0, tiled=True)
+    got = exchange(sent, "z")
     left, table, coef = call(
         make_tables,
         (shape((80, D), BF), shape((5, 128, 128), BF), shape((8, 128), F32)),
@@ -342,18 +353,18 @@
         (lax.all_gather(got, "core"), left, start, table),
         scratch=(pltpu.VMEM((D, 128), BF), pltpu.VMEM((D, 128), BF)),
     )
-    got = lax.all_gather(lax.all_to_all(sent, ("y", "x"), 0, 0, tiled=True), "core")
+    got = lax.all_gather(exchange(sent, ("y", "x")), "core")
     heads, first_eps, sent = call(
         first_sweep,
         (shape((2 * HEADS, 128, 128), BF), shape((16, 128), F32), shape((Z, 16, 128), BF)),
         (coef, got, start, table),
         scratch=(pltpu.VMEM((2, HEADS * 32, 128), BF), pltpu.VMEM((2, 32, 128), F32), *work_space()),
     )
-    got = lax.all_to_all(sent, "z", 0, 0, tiled=True)
+    got = exchange(sent, "z")
     latents, sent = call(
         first_prefix, (shape((2, 16, 128), F32), shape((PEERS, 32, 128), BF)), (coef, got, start, first_eps, table)
     )
-    got = lax.all_to_all(sent, FLAT, 0, 0, tiled=True)
+    got = exchange(sent, FLAT)
     query, direct = call(
         second_queries,
         (shape((2, HEADS * 32, 128), BF), shape((2, 32, 128), F32)),
@@ -366,11 +377,11 @@
         (coef, got, latents, table, heads, query, direct),
         scratch=work_space(),
     )
-    got = lax.all_to_all(sent, "z", 0, 0, tiled=True)
+    got = exchange(sent, "z")
     fresh, sent = call(
         second_prefix, (shape((2, 16, 128), F32), shape((PEERS, 8, 128), F32)), (got, start, latents, term)
     )
-    got = lax.all_to_all(sent, FLAT, 0, 0, tiled=True)
+    got = exchange(sent, FLAT)
     halves = lax.all_gather(fresh, "core")
     window, errors = call(finish, (shape((1, 64, C), F32), shape((1, 1), F32)), (got, halves))
     return window, errors.reshape(1)

time: 129 us -> 120 us (0.930)
  blocking collectives: 61.4 us -> 51.7 us
  starting transfers between devices: 27.7 us -> 37 us
  waiting for transfers between devices: 27.1 us -> 18.3 us
    all_to_all x3, starting transfers between devices: 27.7 us -> 37 us  [exchange(): lax.all_to_all(values, axis, 0, 0, axis_index_groups=[order], tiled=True)]
    all_to_all x3, waiting for transfers between devices: 27.1 us -> 18.3 us  [exchange(): lax.all_to_all(values, axis, 0, 0, axis_index_groups=[order], tiled=True)]
    all_gather x1, blocking collectives: 8.39 us -> 2.78 us  [body(): lax.all_gather(got, 'core')]
    all_to_all x3, blocking collectives: 47.7 us -> 44.1 us  [exchange(): lax.all_to_all(values, axis, 0, 0, axis_index_groups=[order], tiled=True)]
where the time goes in v6:
time: 120 us; the launch traced here: 119 us
  blocking collectives  51.7 us (43%)
  starting transfers between devices  37 us (31%)
  waiting for transfers between devices  18.3 us (15%)
  Pallas kernels  11.4 us (10%)
    all_to_all x3, blocking collectives, exchange(): lax.all_to_all(values, axis, 0, 0, axis_index_groups=[order], tiled=True)  44.1 us
    all_to_all x3, starting transfers between devices, exchange(): lax.all_to_all(values, axis, 0, 0, axis_index_groups=[order], tiled=True)  37 us
    all_to_all x3, waiting for transfers between devices, exchange(): lax.all_to_all(values, axis, 0, 0, axis_index_groups=[order], tiled=True)  18.3 us
    pallas_call x9, Pallas kernels, call(): pl.pallas_call(kernel, out_shape=outs, in_specs=[pl.BlockSpec(memory_spac...  11.4 us
    all_gather x1, blocking collectives, body(): got = lax.all_gather(exchange(sent, ('y', 'x')), 'core')  2.97 us
    all_gather x1, blocking collectives, body(): lax.all_gather(got, 'core')  2.78 us
  transfers between devices with their start and end apart: 3, of which 3 were waited for; matrix products, arithmetic and copies ran while one was open for 0% of the time, Pallas kernels for 2%

profile of v6, /device:TPU:1, one launch (start us, length us, event | category | flops | bytes accessed | tf_op | source)
XLA Modules:
  0.0 119.1 jit_solution(9523808390896252422)
XLA Ops:
  0.6 2.0 %shard_map.87 = bf16[16,80,128]{2,1,0:T(8,128)(2,1)} custom-call(bf16[48,3072]{1,0:T(8,128)(2,1)} %w_qkv.1, bf16[32,1536]{1,0:T(8,128)(2,1)} %w_o.1, bf16[64,1536]{1,0:T(8,128)(2,1)} %bitcast.7), custom_call_target="tpu_custom_call" | custom-call | tf_op jit(solution)/shard_map/pallas_call | solution.py:79
  2.7 0.0 copy-start.1
  2.7 0.0 copy-start.2
  2.7 0.0 copy-start.3
  2.7 0.0 copy-start.4
  2.7 19.3 %all-to-all-start = ((bf16[16,80,128]{2,1,0:T(8,128)(2,1)}), bf16[16,80,128]{2,1,0:T(8,128)(2,1)S(1)}, u32[]{:S(2)}, u32[]{:S(2)}) async-start(bf16[16,80,128]{2,1,0:T(8,128)(2,1)} %shard_map.87), calls=%async_computation | async-start | bytes 655360 | tf_op jit(solution)/shard_map/all_to_all | solution.py:92
  22.0 0.0 copy-done.1
  22.0 0.0 copy-done.2
  22.0 0.0 copy-done.3
  22.0 0.0 copy-done.4
  22.0 1.3 %shard_map.86 = (bf16[80,1536]{1,0:T(8,128)(2,1)S(1)}, bf16[5,128,128]{2,1,0:T(8,128)(2,1)S(1)}, f32[8,128]{1,0:T(8,128)S(1)}) custom-call(s32[33]{0:T(128)S(1)} %copy-done.4, bf16[64,1536]{1,0:T(8,128)(2,1)S(1)} %copy-done.2, bf16[64,1536]{1,0:T(8,128)(2,1)S(1)} %bitcast.8, bf16[1,3072]{1,0:T(2,128)(2,1)S(1)} %copy-done.3), custom_call_target="tpu_custom_call" | custom-call | flops 1000000000 | tf_op jit(solution)/shard_map/pallas_call | solution.py:79
  23.3 0.0 copy-start
  23.3 14.0 %all-to-all-done = bf16[16,80,128]{2,1,0:T(8,128)(2,1)S(1)} async-done(((bf16[16,80,128]{2,1,0:T(8,128)(2,1)}), bf16[16,80,128]{2,1,0:T(8,128)(2,1)S(1)}, u32[]{:S(2)}, u32[]{:S(2)}) %all-to-all-start) | async-done | bytes 327712 | tf_op jit(solution)/shard_map/all_to_all | solution.py:92
  37.2 2.8 %all-gather = bf16[32,80,128]{2,1,0:T(8,128)(2,1)S(1)} all-gather(bf16[16,80,128]{2,1,0:T(8,128)(2,1)S(1)} %all-to-all-done), channel_id=2, replica_groups=mesh['z'=16,'core'=2,'y'=4,'x'=4] {'core'}, dimensions={0}, use_global_device_ids=true | all-gather | bytes 983040 | tf_op jit(solution)/shard_map/all_gather | solution.py:353
  40.0 0.0 copy-done
  40.0 0.8 shard_map.88
  40.9 13.4 %all_to_all.30 = bf16[16,96,128]{2,1,0:T(8,128)(2,1)S(1)} all-to-all(bf16[16,96,128]{2,1,0:T(8,128)(2,1)S(1)} %shard_map.88), channel_id=1, replica_groups={{10,11,12,13,14,15,0,1,2,3,4,5,6,7,8,9},{26,27,28,29,30,31,16,17,18,19,..., dimensions={0} | all-to-all | bytes 786432 | tf_op jit(solution)/shard_map/all_to_all | solution.py:92
  54.3 3.0 %all-gather.1 = bf16[32,96,128]{2,1,0:T(8,128)(2,1)S(1)} all-gather(bf16[16,96,128]{2,1,0:T(8,128)(2,1)S(1)} %all_to_all.30), channel_id=3, replica_groups=mesh['z'=16,'core'=2,'y'=4,'x'=4] {'core'}, dimensions={0}, use_global_device_ids=true | all-gather | bytes 1179648 | tf_op jit(solution)/shard_map/all_gather | solution.py:356
  57.3 2.1 %shard_map.89 = (bf16[16,128,128]{2,1,0:T(8,128)(2,1)S(1)}, f32[16,128]{1,0:T(8,128)S(1)}, bf16[16,16,128]{2,1,0:T(8,128)(2,1)S(1)}) custom-call(f32[8,128]{1,0:T(8,128)S(1)} %get-tuple-element.18.coef, bf16[2,16,96,128]{3,2,1,0:T(8,128)(2,1)S(1)} %bitcast.5, f32[64,64]{1,0:T(8,128)S(1)} %copy-done, bf16[5,128,128]{2,1,0:T(8,128)(2,1)S(1)} %get-tuple-element.20.table), custom_call_target="tpu_custom_call" | custom-call | tf_op jit(solution)/shard_map/pallas_call | solution.py:79
  59.4 15.4 %all_to_all.31.got = bf16[16,16,128]{2,1,0:T(8,128)(2,1)S(1)} all-to-all(bf16[16,16,128]{2,1,0:T(8,128)(2,1)S(1)} %get-tuple-element.21), channel_id=1, replica_groups={{256,288,320,352,384,416,448,480,0,32,64,96,128,160,192,224},{257,289,3..., dimensions={0} | all-to-all | bytes 131072 | tf_op jit(solution)/shard_map/all_to_all | solution.py:92
  74.8 1.2 shard_map.90
  75.9 8.2 %all-to-all-start.3 = ((bf16[32,32,128]{2,1,0:T(8,128)(2,1)}), bf16[32,32,128]{2,1,0:T(8,128)(2,1)S(1)}, u32[]{:S(2)}, u32[]{:S(2)}) async-start(bf16[32,32,128]{2,1,0:T(8,128)(2,1)} %get-tuple-element.23), calls=%async_computation.3 | async-start | bytes 524288 | tf_op jit(solution)/shard_map/all_to_all | solution.py:92
  84.1 0.8 shard_map.91
  84.9 3.4 %all-to-all-done.3.got = bf16[32,32,128]{2,1,0:T(8,128)(2,1)S(1)} async-done(((bf16[32,32,128]{2,1,0:T(8,128)(2,1)}), bf16[32,32,128]{2,1,0:T(8,128)(2,1)S(1)}, u32[]{:S(2)}, u32[]{:S(2)}) %all-to-all-start.3) | async-done | bytes 262176 | tf_op jit(solution)/shard_map/all_to_all | solution.py:92
  88.3 1.8 %shard_map.92 = (f32[16,128]{1,0:T(8,128)S(1)}, bf16[16,16,128]{2,1,0:T(8,128)(2,1)S(1)}) custom-call(f32[8,128]{1,0:T(8,128)S(1)} %get-tuple-element.18.coef, bf16[32,32,128]{2,1,0:T(8,128)(2,1)S(1)} %all-to-all-done.3.got, f32[2,16,128]{2,1,0:T(8,128)S(1)} %get-tuple-element.24.latents, bf16[5,128,128]{2,1,0:T(8,128)(2,1)S(1)} %get-tuple-element.20.table, ...), custom_call_target="tpu_custom_call" | custom-call | tf_op jit(solution)/shard_map/pallas_call | solution.py:79
  90.1 15.3 %all_to_all.32.got = bf16[16,16,128]{2,1,0:T(8,128)(2,1)S(1)} all-to-all(bf16[16,16,128]{2,1,0:T(8,128)(2,1)S(1)} %get-tuple-element.28), channel_id=1, replica_groups={{256,288,320,352,384,416,448,480,0,32,64,96,128,160,192,224},{257,289,3..., dimensions={0} | all-to-all | bytes 131072 | tf_op jit(solution)/shard_map/all_to_all | solution.py:92
  105.3 0.7 shard_map.93
  106.1 9.5 %all-to-all-start.5 = ((f32[32,8,128]{2,1,0:T(8,128)}), f32[32,8,128]{2,1,0:T(8,128)S(1)}, u32[]{:S(2)}, u32[]{:S(2)}) async-start(f32[32,8,128]{2,1,0:T(8,128)} %get-tuple-element.30), calls=%async_computation.5 | async-start | bytes 262144 | tf_op jit(solution)/shard_map/all_to_all | solution.py:92
  115.6 1.8 %all-gather.2 = f32[4,16,128]{2,1,0:T(8,128)S(1)} all-gather(f32[2,16,128]{2,1,0:T(8,128)S(1)} %get-tuple-element.31), channel_id=4, replica_groups=mesh['z'=16,'core'=2,'y'=4,'x'=4] {'core'}, dimensions={0}, use_global_device_ids=true | all-gather | bytes 49152 | tf_op jit(solution)/shard_map/all_gather | solution.py:385
  117.4 1.0 all-to-all-done.5.got
  118.4 0.7 shard_map.94
Async XLA Ops:
  2.7 19.3 %copy-start.1 = (bf16[1536,64]{0,1:T(8,128)(2,1)S(1)}, bf16[1536,64]{0,1:T(8,128)(2,1)}, u32[]{:S(2)}) copy-start(bf16[1536,64]{0,1:T(8,128)(2,1)} %param.13) | copy-start | bytes 589828
  2.7 19.3 %copy-start.2 = (bf16[64,1536]{1,0:T(8,128)(2,1)S(1)}, bf16[64,1536]{1,0:T(8,128)(2,1)}, u32[]{:S(2)}) copy-start(bf16[64,1536]{1,0:T(8,128)(2,1)} %w_in.1) | copy-start | bytes 589828
  2.7 19.3 %copy-start.3 = (bf16[1,3072]{1,0:T(2,128)(2,1)S(1)}, bf16[1,3072]{1,0:T(2,128)(2,1)}, u32[]{:S(2)}) copy-start(bf16[1,3072]{1,0:T(2,128)(2,1)} %modulation.1) | copy-start | bytes 18436
  2.7 19.3 %copy-start.4 = (s32[33]{0:T(128)S(1)}, s32[33]{0:T(128)}, u32[]{:S(2)}) copy-start(s32[33]{0:T(128)} %timesteps.1) | copy-start | bytes 400
  2.7 34.5 %all-to-all-start = ((bf16[16,80,128]{2,1,0:T(8,128)(2,1)}), bf16[16,80,128]{2,1,0:T(8,128)(2,1)S(1)}, u32[]{:S(2)}, u32[]{:S(2)}) async-start(bf16[16,80,128]{2,1,0:T(8,128)(2,1)} %shard_map.87), calls=%async_computation | async-start | bytes 655360 | tf_op jit(solution)/shard_map/all_to_all | solution.py:92
  23.3 16.8 %copy-start = (f32[64,64]{1,0:T(8,128)S(1)}, f32[64,64]{1,0:T(8,128)}, u32[]{:S(2)}) copy-start(f32[64,64]{1,0:T(8,128)} %start.7) | copy-start | bytes 49156
  75.9 12.4 %all-to-all-start.3 = ((bf16[32,32,128]{2,1,0:T(8,128)(2,1)}), bf16[32,32,128]{2,1,0:T(8,128)(2,1)S(1)}, u32[]{:S(2)}, u32[]{:S(2)}) async-start(bf16[32,32,128]{2,1,0:T(8,128)(2,1)} %get-tuple-element.23), calls=%async_computation.3 | async-start | bytes 524288 | tf_op jit(solution)/shard_map/all_to_all | solution.py:92
  106.1 12.3 %all-to-all-start.5 = ((f32[32,8,128]{2,1,0:T(8,128)}), f32[32,8,128]{2,1,0:T(8,128)S(1)}, u32[]{:S(2)}, u32[]{:S(2)}) async-start(f32[32,8,128]{2,1,0:T(8,128)} %get-tuple-element.30), calls=%async_computation.5 | async-start | bytes 262144 | tf_op jit(solution)/shard_map/all_to_all | solution.py:92

commit v7 on v6

--- a/solution.py
+++ b/solution.py
@@ -74,13 +74,13 @@
     return pieces
 
 
-def call(kernel, outs, args, scratch=(), smem=(), far=(), flops=0, grant=40):
+def call(kernel, outs, args, scratch=(), smem=(), far=(), flops=0, grant=40, out_far=False):
     spaces = [pltpu.SMEM if at in smem else pl.ANY if at in far else pltpu.VMEM for at in range(len(args))]
     return pl.pallas_call(
         kernel,
         out_shape=outs,
         in_specs=[pl.BlockSpec(memory_space=space) for space in spaces],
-        out_specs=jax.tree.map(lambda _: pl.BlockSpec(memory_space=pltpu.VMEM), outs),
+        out_specs=jax.tree.map(lambda _: pl.BlockSpec(memory_space=pl.ANY if out_far else pltpu.VMEM), outs),
         scratch_shapes=scratch,
         compiler_params=pltpu.CompilerParams(vmem_limit_bytes=grant * 1024 * 1024),
         cost_estimate=pl.CostEstimate(flops=flops, bytes_accessed=0, transcendentals=0) if flops else None,
@@ -96,34 +96,47 @@
     return jax.ShapeDtypeStruct(dims, kind)
 
 
-def send_weights(w_qkv, w_o, w_out, out, blocks, left, right, arrived):
+def send_weights(w_qkv, w_o, w_out, out, blocks, left, right, early, late, arrived, gone):
     _, _, seq = place()
-    copies = [pltpu.make_async_copy(w_o, left, arrived.at[3]), pltpu.make_async_copy(w_out, right, arrived.at[4])]
+    odd = lax.rem(seq, 2) == 1
+    copies = []
     for at in range(3):
         start = pl.multiple_of(at * INNER + (seq // 2) * HEAD_DIM, HEAD_DIM)
         copies.append(pltpu.make_async_copy(w_qkv.at[:, pl.ds(start, HEAD_DIM)], blocks.at[at], arrived.at[at]))
+    copies.append(pltpu.make_async_copy(w_o, left, arrived.at[3]))
+    copies.append(pltpu.make_async_copy(w_out, right, arrived.at[4]))
     for copy in copies:
         copy.start()
-    for copy in copies:
-        copy.wait()
-    odd = lax.rem(seq, 2) == 1
 
     def columns(at):
         block = blocks[at].astype(F32)
         return jnp.where(odd, block[:, C:], block[:, :C])
 
+    copies[0].wait()
+    copies[1].wait()
     first = jnp.concatenate([columns(0), columns(1)], axis=1).astype(BF)
+    for to in range(Z):
+        early[to] = first
+    first_out = pltpu.make_async_copy(early, out.at[:, 0:48, :], gone.at[0])
+    first_out.start()
     at, to = rows((HEAD_DIM, C)), lanes((HEAD_DIM, C))
     wanted = (to // 16) * 32 + to % 16 + jnp.where(odd, 16, 0)
-    value = dot(blocks[2], jnp.where(at == wanted, 1.0, 0.0).astype(BF))
+    chosen = jnp.where(at == wanted, 1.0, 0.0).astype(BF)
+    copies[2].wait()
+    value = dot(blocks[2], chosen)
+    copies[3].wait()
+    copies[4].wait()
     head = lax.dot_general(left[...], right[...], NT, preferred_element_type=F32)
     head = jnp.where(odd, head[16:], head[:16])
     second = jnp.concatenate([value[0:16], value[16:32]], axis=1).astype(BF)
     third = jnp.concatenate([value[32:48], head], axis=1).astype(BF)
     for to in range(Z):
-        out[to, 0:48, :] = first
-        out[to, 48:64, :] = second
-        out[to, 64:80, :] = third
+        late[to, 0:16, :] = second
+        late[to, 16:32, :] = third
+    second_out = pltpu.make_async_copy(late, out.at[:, 48:80, :], gone.at[1])
+    second_out.start()
+    first_out.wait()
+    second_out.wait()
 
 
 def coefficients(timesteps):
@@ -147,7 +160,7 @@
     return jnp.broadcast_to(jnp.sum(chosen, axis=1, keepdims=True), (8, 128))
 
 
-def make_tables(timesteps, w_in, w_out, modulation, left, table, coef):
+def make_tables(timesteps, w_in, w_out, modulation, start, left, table, coef, mine, direct, own):
     coef[...] = coefficients(timesteps)
     w = w_in[...].astype(F32)
     centred = w - jnp.mean(w, axis=1, keepdims=True)
@@ -156,17 +169,22 @@
     left[0:C, :] = (centred * (1.0 + gain)).astype(BF)
     left[C : C + 16, :] = jnp.where(rows((16, D)) == 0, shift, 0.0).astype(BF)
     gram = lax.dot_general(centred, centred, NT, precision=BEST, preferred_element_type=F32) / D
-    direct = lax.dot_general(w_in[...], w_out[...], NT, preferred_element_type=F32)
+    embed = lax.dot_general(w_in[...], w_out[...], NT, preferred_element_type=F32)
     pad = jnp.zeros((C, C), F32)
     gram = jnp.concatenate([gram, pad], axis=1)
-    direct = jnp.concatenate([pad, direct], axis=1)
-    for at, piece in enumerate(split_of(gram, 3) + split_of(direct, 2)):
+    embed = jnp.concatenate([pad, embed], axis=1)
+    for at, piece in enumerate(split_of(gram, 3) + split_of(embed, 2)):
         table[at, 0:C, :] = piece
         table[at, C : 2 * C, :] = jnp.zeros((C, 2 * C), BF)
-
-
-def make_heads(both, left, start, table, out, qk, vw):
-    _, core, seq = place()
+    _, core, _ = place()
+    x = unpack(packed_start(start, core).astype(BF).astype(F32))
+    mine[...] = normalized(x, table)
+    own[...] = pack(mine[...]).astype(BF)
+    direct[...] = direct_of(x, table)
+
+
+def make_heads(both, left, own, out, qk, vw):
+    _, _, seq = place()
     for rank, z in enumerate(Z_ORDER):
         for parity in range(2):
             at = (z * 2 + parity) * ROWS
@@ -187,7 +205,7 @@
     bias = jnp.concatenate([bias, jnp.zeros((8, 128 - bias.shape[1]), F32)], axis=1)[0:1]
     main = jnp.concatenate([a[:, :C], b], axis=1)
     main = jnp.where(rows(main.shape) == C + 1, bias, main).astype(BF)
-    x = pack(normalized(unpack(packed_start(start, core).astype(BF).astype(F32)), table)).astype(BF)
+    x = own[...]
     for to in range(PEERS // 2):
         out[to, 0:80, :] = main
         out[to, 80:96, :] = x
@@ -200,56 +218,60 @@
     return jnp.where(lanes(x.shape) == C, 1.0, x * lax.rsqrt(spread + 1e-06))
 
 
-def ask(steps, heads, table, x, query, direct):
-    count = x.shape[0]
-    mine = normalized(x, table)
+def direct_of(x, table):
+    exact = x.astype(BF)
+    return pack_high(dot(exact, table[3]) + dot(exact, table[4]))
+
+
+def ask(step, heads, mine, query):
     short = mine.astype(BF)
-    lane = lanes((count, 128))
-    exact = x.astype(BF)
-    for step in steps:
-        direct[step] = dot(exact, table[3]) + dot(exact, table[4])
+    lane = lanes(mine.shape)
+    for head in range(HEADS):
+        both = heads[step * HEADS + head]
+        grown = dot(short, both)
+        constant = jnp.sum(mine * both[C : C + 16].astype(F32)[1:2], axis=1, keepdims=True)
+        grown = jnp.where(lane < C, grown, jnp.where(lane == C, constant, 0.0)).astype(BF)
+        query[step, head * 32 : (head + 1) * 32, :] = grown
+
+
+def attend(heads, query, direct, keys, weight, mix):
+    both = range(2)
+    scores = [lax.dot_general(query[step], keys[step][...], NT, preferred_element_type=F32) for step in both]
+    tops = [jnp.max(score, axis=1, keepdims=True) for score in scores]
+    for step in both:
+        weight[step] = jnp.exp2(scores[step] - tops[step]).astype(BF)
+    mixed = [dot(weight[step], keys[step][...]) for step in both]
+    for step in both:
+        shares = (mixed[step] / mixed[step][:, C : C + 1]).astype(BF)
         for head in range(HEADS):
-            both = heads[step * HEADS + head]
-            grown = dot(short, both)
-            constant = jnp.sum(mine * both[C : C + 16].astype(F32)[1:2], axis=1, keepdims=True)
-            grown = jnp.where(lane < C, grown, jnp.where(lane == C, constant, 0.0)).astype(BF)
-            query[step, head * count : (head + 1) * count, :] = grown
-
-
-def attend(step, heads, query, direct, key, weight, mix):
-    count = direct.shape[1]
-    scores = lax.dot_general(query[step], key[...], NT, preferred_element_type=F32)
-    weight[step] = jnp.exp2(scores - jnp.max(scores, axis=1, keepdims=True)).astype(BF)
-    mixed = dot(weight[step], key[...])
-    mix[step] = (mixed / mixed[:, C : C + 1]).astype(BF)
-    eps = jnp.zeros((count, 128), F32)
-    for head in range(HEADS):
-        eps = eps + dot(mix[step, head * count : (head + 1) * count, :], heads[step * HEADS + head])
-    return pack_high(eps + direct[step])
+            mix[step, :, head * 128 : (head + 1) * 128] = shares[head * 32 : (head + 1) * 32]
+    eps = []
+    for step in both:
+        blocks = heads[step * HEADS : (step + 1) * HEADS].reshape(HEADS * 128, 128)
+        eps.append(pack_high(dot(mix[step], blocks)) + direct[step])
+    return eps
 
 
 def work_space():
     return (
         pltpu.VMEM((2, TOKENS, 128), BF),
         pltpu.VMEM((2, HEADS * 32, TOKENS), BF),
-        pltpu.VMEM((2, HEADS * 32, 128), BF),
-    )
-
-
-def first_sweep(coef, got, start, table, heads, first_eps, out, query, direct, key, weight, mix):
-    _, core, _ = place()
+        pltpu.VMEM((2, 32, HEADS * 128), BF),
+    )
+
+
+def first_sweep(coef, got, mine, direct, heads, first_eps, out, query, key, weight, mix):
     for at in range(2 * HEADS):
         step, first = at // HEADS, SEQ_ORDER.index(2 * (at % HEADS))
         second = SEQ_ORDER.index(2 * (at % HEADS) + 1)
         both = got[step, first, 0:80, :].astype(F32) + got[step, second, 0:80, :].astype(F32)
         heads[at, 0:80, :] = both.astype(BF)
         heads[at, 80:128, :] = jnp.zeros((48, 128), BF)
-    x = start[pl.ds(pl.multiple_of(core * 32, 32), 32), :].astype(BF).astype(F32)
-    x = jnp.concatenate([x, jnp.zeros_like(x)], axis=1)
     everything = got[:, :, 80:96, :].astype(F32).reshape(PEERS * 16, 128)
     key[0] = unpack(everything, 1.0).astype(BF)
-    ask((0, 1), heads, table, x, query, direct)
-    eps = [attend(step, heads, query, direct, key.at[0], weight, mix) for step in range(2)]
+    for step in range(2):
+        ask(step, heads, mine[...], query)
+    eps = attend(heads, query, (direct[...], direct[...]), (key.at[0], key.at[0]), weight, mix)
     first_eps[...] = eps[0]
     both = (coef[2:3] * eps[0] + coef[3:4] * eps[1]).astype(BF)
     for to in range(Z):
@@ -283,16 +305,17 @@
 
 def second_queries(latents, table, heads, query, direct):
     for step in range(2):
-        ask((step,), heads, table, unpack(latents[step].astype(BF).astype(F32)), query, direct)
-
-
-def second_sweep(coef, got, latents, table, heads, query, direct, term, out, key, weight, mix):
-    terms = []
+        x = unpack(latents[step].astype(BF).astype(F32))
+        direct[step] = direct_of(x, table)
+        ask(step, heads, normalized(x, table), query)
+
+
+def second_sweep(coef, got, latents, heads, query, direct, term, out, key, weight, mix):
     for step in range(2):
         everything = got[:, 16 * step : 16 * step + 16, :].astype(F32).reshape(PEERS * 16, 128)
         key[step] = unpack(everything, 1.0).astype(BF)
-        eps = attend(step, heads, query, direct, key.at[step], weight, mix)
-        terms.append(coef[step : step + 1] * latents[step] + coef[2 + step : 3 + step] * eps)
+    eps = attend(heads, query, direct, (key.at[0], key.at[1]), weight, mix)
+    terms = [coef[step : step + 1] * latents[step] + coef[2 + step : 3 + step] * eps[step] for step in range(2)]
     term[...] = terms[0]
     both = (terms[0] + terms[1]).astype(BF)
     for to in range(Z):
@@ -334,31 +357,42 @@
             pltpu.VMEM((3, ROWS, HEAD_DIM), BF),
             pltpu.VMEM((32, D), BF),
             pltpu.VMEM((C, D), BF),
+            pltpu.VMEM((Z, 48, 128), BF),
+            pltpu.VMEM((Z, 32, 128), BF),
             pltpu.SemaphoreType.DMA((5,)),
+            pltpu.SemaphoreType.DMA((2,)),
         ),
         far=(0, 1, 2),
         grant=62,
+        out_far=True,
     )
     got = exchange(sent, "z")
-    left, table, coef = call(
+    left, table, coef, mine, direct, own = call(
         make_tables,
-        (shape((80, D), BF), shape((5, 128, 128), BF), shape((8, 128), F32)),
-        (timesteps, w_in, w_out.T, modulation),
+        (
+            shape((80, D), BF),
+            shape((5, 128, 128), BF),
+            shape((8, 128), F32),
+            shape((32, 128), F32),
+            shape((16, 128), F32),
+            shape((16, 128), BF),
+        ),
+        (timesteps, w_in, w_out.T, modulation, start),
         smem=(0,),
         flops=10**9,
     )
     sent = call(
         make_heads,
         shape((PEERS // 2, 96, 128), BF),
-        (lax.all_gather(got, "core"), left, start, table),
+        (lax.all_gather(got, "core"), left, own),
         scratch=(pltpu.VMEM((D, 128), BF), pltpu.VMEM((D, 128), BF)),
     )
     got = lax.all_gather(exchange(sent, ("y", "x")), "core")
     heads, first_eps, sent = call(
         first_sweep,
         (shape((2 * HEADS, 128, 128), BF), shape((16, 128), F32), shape((Z, 16, 128), BF)),
-        (coef, got, start, table),
-        scratch=(pltpu.VMEM((2, HEADS * 32, 128), BF), pltpu.VMEM((2, 32, 128), F32), *work_space()),
+        (coef, got, mine, direct),
+        scratch=(pltpu.VMEM((2, HEADS * 32, 128), BF), *work_space()),
     )
     got = exchange(sent, "z")
     latents, sent = call(
@@ -367,14 +401,14 @@
     got = exchange(sent, FLAT)
     query, direct = call(
         second_queries,
-        (shape((2, HEADS * 32, 128), BF), shape((2, 32, 128), F32)),
+        (shape((2, HEADS * 32, 128), BF), shape((2, 16, 128), F32)),
         (latents, table, heads),
         flops=10**9,
     )
     term, sent = call(
         second_sweep,
         (shape((16, 128), F32), shape((Z, 16, 128), BF)),
-        (coef, got, latents, table, heads, query, direct),
+        (coef, got, latents, heads, query, direct),
         scratch=work_space(),
     )
     got = exchange(sent, "z")

time: 120 us -> 118 us (0.983)
  Pallas kernels: 11.4 us -> 10.1 us
    pallas_call x9, Pallas kernels: 11.4 us -> 10.1 us  [call(): pl.pallas_call(kernel, out_shape=outs, in_specs=[pl.BlockSpec(memory_spac...]
where the time goes in v7:
time: 118 us
  blocking collectives  51.7 us (44%)
  starting transfers between devices  36.9 us (31%)
  waiting for transfers between devices  18 us (15%)
  Pallas kernels  10.1 us (9%)
    all_to_all x3, blocking collectives, exchange(): lax.all_to_all(values, axis, 0, 0, axis_index_groups=[order], tiled=True)  44.1 us
    all_to_all x3, starting transfers between devices, exchange(): lax.all_to_all(values, axis, 0, 0, axis_index_groups=[order], tiled=True)  36.9 us
    all_to_all x3, waiting for transfers between devices, exchange(): lax.all_to_all(values, axis, 0, 0, axis_index_groups=[order], tiled=True)  18 us
    pallas_call x9, Pallas kernels, call(): pl.pallas_call(kernel, out_shape=outs, in_specs=[pl.BlockSpec(memory_spac...  10.1 us
    all_gather x1, blocking collectives, body(): got = lax.all_gather(exchange(sent, ('y', 'x')), 'core')  2.97 us
    all_gather x1, blocking collectives, body(): lax.all_gather(got, 'core')  2.78 us
  transfers between devices with their start and end apart: 3, of which 3 were waited for; matrix products, arithmetic and copies ran while one was open for 0% of the time, Pallas kernels for 2%

profile of v7, /device:TPU:1, one launch (start us, length us, event | category | flops | bytes accessed | tf_op | source)
XLA Modules:
  0.0 117.5 jit_solution(7711717671978770076)
XLA Ops:
  0.6 2.0 %shard_map.87 = bf16[16,80,128]{2,1,0:T(8,128)(2,1)} custom-call(bf16[48,3072]{1,0:T(8,128)(2,1)} %w_qkv.1, bf16[32,1536]{1,0:T(8,128)(2,1)} %w_o.1, bf16[64,1536]{1,0:T(8,128)(2,1)} %bitcast.7), custom_call_target="tpu_custom_call" | custom-call | tf_op jit(solution)/shard_map/pallas_call | solution.py:79
  2.7 0.0 copy-start
  2.7 0.0 copy-start.1
  2.7 0.0 copy-start.2
  2.7 0.0 copy-start.3
  2.7 0.0 copy-start.4
  2.7 19.3 %all-to-all-start = ((bf16[16,80,128]{2,1,0:T(8,128)(2,1)}), bf16[16,80,128]{2,1,0:T(8,128)(2,1)S(1)}, u32[]{:S(2)}, u32[]{:S(2)}) async-start(bf16[16,80,128]{2,1,0:T(8,128)(2,1)} %shard_map.87), calls=%async_computation | async-start | bytes 655360 | tf_op jit(solution)/shard_map/all_to_all | solution.py:92
  22.0 0.0 copy-done
  22.0 0.0 copy-done.1
  22.0 0.0 copy-done.2
  22.0 0.0 copy-done.3
  22.0 0.0 copy-done.4
  22.0 1.5 %shard_map.86 = (bf16[80,1536]{1,0:T(8,128)(2,1)S(1)}, bf16[5,128,128]{2,1,0:T(8,128)(2,1)S(1)}, f32[8,128]{1,0:T(8,128)S(1)}, f32[32,128]{1,0:T(8,128)S(1)}, f3...) custom-call(s32[33]{0:T(128)S(1)} %copy-done.4, bf16[64,1536]{1,0:T(8,128)(2,1)S(1)} %copy-done.2, ...), custom_call_target="tpu_custom_call" | custom-call | flops 1000000000 | tf_op jit(solution)/shard_map/pallas_call | solution.py:79
  23.6 13.7 %all-to-all-done = bf16[16,80,128]{2,1,0:T(8,128)(2,1)S(1)} async-done(((bf16[16,80,128]{2,1,0:T(8,128)(2,1)}), bf16[16,80,128]{2,1,0:T(8,128)(2,1)S(1)}, u32[]{:S(2)}, u32[]{:S(2)}) %all-to-all-start) | async-done | bytes 327712 | tf_op jit(solution)/shard_map/all_to_all | solution.py:92
  37.3 2.8 %all-gather = bf16[32,80,128]{2,1,0:T(8,128)(2,1)S(1)} all-gather(bf16[16,80,128]{2,1,0:T(8,128)(2,1)S(1)} %all-to-all-done), channel_id=2, replica_groups=mesh['z'=16,'core'=2,'y'=4,'x'=4] {'core'}, dimensions={0}, use_global_device_ids=true | all-gather | bytes 983040 | tf_op jit(solution)/shard_map/all_gather | solution.py:387
  40.1 0.7 shard_map.88
  40.8 13.4 %all_to_all.30 = bf16[16,96,128]{2,1,0:T(8,128)(2,1)S(1)} all-to-all(bf16[16,96,128]{2,1,0:T(8,128)(2,1)S(1)} %shard_map.88), channel_id=1, replica_groups={{10,11,12,13,14,15,0,1,2,3,4,5,6,7,8,9},{26,27,28,29,30,31,16,17,18,19,..., dimensions={0} | all-to-all | bytes 786432 | tf_op jit(solution)/shard_map/all_to_all | solution.py:92
  54.2 3.0 %all-gather.1 = bf16[32,96,128]{2,1,0:T(8,128)(2,1)S(1)} all-gather(bf16[16,96,128]{2,1,0:T(8,128)(2,1)S(1)} %all_to_all.30), channel_id=3, replica_groups=mesh['z'=16,'core'=2,'y'=4,'x'=4] {'core'}, dimensions={0}, use_global_device_ids=true | all-gather | bytes 1179648 | tf_op jit(solution)/shard_map/all_gather | solution.py:390
  57.2 1.3 %shard_map.89 = (bf16[16,128,128]{2,1,0:T(8,128)(2,1)S(1)}, f32[16,128]{1,0:T(8,128)S(1)}, bf16[16,16,128]{2,1,0:T(8,128)(2,1)S(1)}) custom-call(f32[8,128]{1,0:T(8,128)S(1)} %get-tuple-element.21.coef, bf16[2,16,96,128]{3,2,1,0:T(8,128)(2,1)S(1)} %bitcast.5, f32[32,128]{1,0:T(8,128)S(1)} %get-tuple-element.24.mine, f32[16,128]{1,0:T(8,128)S(1)} %get-tuple-element.25.direct), custom_call_target="tpu_custom_call" | custom-call | tf_op jit(solution)/shard_map/pallas_call | solution.py:79
  58.5 15.4 %all_to_all.31.got = bf16[16,16,128]{2,1,0:T(8,128)(2,1)S(1)} all-to-all(bf16[16,16,128]{2,1,0:T(8,128)(2,1)S(1)} %get-tuple-element.26), channel_id=1, replica_groups={{256,288,320,352,384,416,448,480,0,32,64,96,128,160,192,224},{257,289,3..., dimensions={0} | all-to-all | bytes 131072 | tf_op jit(solution)/shard_map/all_to_all | solution.py:92
  73.9 1.2 shard_map.90
  75.0 8.2 %all-to-all-start.3 = ((bf16[32,32,128]{2,1,0:T(8,128)(2,1)}), bf16[32,32,128]{2,1,0:T(8,128)(2,1)S(1)}, u32[]{:S(2)}, u32[]{:S(2)}) async-start(bf16[32,32,128]{2,1,0:T(8,128)(2,1)} %get-tuple-element.29), calls=%async_computation.3 | async-start | bytes 524288 | tf_op jit(solution)/shard_map/all_to_all | solution.py:92
  83.2 0.8 shard_map.91
  84.0 3.3 %all-to-all-done.3.got = bf16[32,32,128]{2,1,0:T(8,128)(2,1)S(1)} async-done(((bf16[32,32,128]{2,1,0:T(8,128)(2,1)}), bf16[32,32,128]{2,1,0:T(8,128)(2,1)S(1)}, u32[]{:S(2)}, u32[]{:S(2)}) %all-to-all-start.3) | async-done | bytes 262176 | tf_op jit(solution)/shard_map/all_to_all | solution.py:92
  87.4 1.1 shard_map.92
  88.5 15.3 %all_to_all.32.got = bf16[16,16,128]{2,1,0:T(8,128)(2,1)S(1)} all-to-all(bf16[16,16,128]{2,1,0:T(8,128)(2,1)S(1)} %get-tuple-element.34), channel_id=1, replica_groups={{256,288,320,352,384,416,448,480,0,32,64,96,128,160,192,224},{257,289,3..., dimensions={0} | all-to-all | bytes 131072 | tf_op jit(solution)/shard_map/all_to_all | solution.py:92
  103.8 0.7 shard_map.93
  104.5 9.5 %all-to-all-start.5 = ((f32[32,8,128]{2,1,0:T(8,128)}), f32[32,8,128]{2,1,0:T(8,128)S(1)}, u32[]{:S(2)}, u32[]{:S(2)}) async-start(f32[32,8,128]{2,1,0:T(8,128)} %get-tuple-element.36), calls=%async_computation.5 | async-start | bytes 262144 | tf_op jit(solution)/shard_map/all_to_all | solution.py:92
  114.0 1.8 %all-gather.2 = f32[4,16,128]{2,1,0:T(8,128)S(1)} all-gather(f32[2,16,128]{2,1,0:T(8,128)S(1)} %get-tuple-element.37), channel_id=4, replica_groups=mesh['z'=16,'core'=2,'y'=4,'x'=4] {'core'}, dimensions={0}, use_global_device_ids=true | all-gather | bytes 49152 | tf_op jit(solution)/shard_map/all_gather | solution.py:419
  115.8 1.0 all-to-all-done.5.got
  116.8 0.7 shard_map.94
Async XLA Ops:
  2.7 19.3 %copy-start = (bf16[1536,64]{0,1:T(8,128)(2,1)S(1)}, bf16[1536,64]{0,1:T(8,128)(2,1)}, u32[]{:S(2)}) copy-start(bf16[1536,64]{0,1:T(8,128)(2,1)} %param.13) | copy-start | bytes 589828
  2.7 19.3 %copy-start.1 = (f32[64,64]{1,0:T(8,128)S(1)}, f32[64,64]{1,0:T(8,128)}, u32[]{:S(2)}) copy-start(f32[64,64]{1,0:T(8,128)} %start.5) | copy-start | bytes 49156
  2.7 19.3 %copy-start.2 = (bf16[64,1536]{1,0:T(8,128)(2,1)S(1)}, bf16[64,1536]{1,0:T(8,128)(2,1)}, u32[]{:S(2)}) copy-start(bf16[64,1536]{1,0:T(8,128)(2,1)} %w_in.1) | copy-start | bytes 589828
  2.7 19.3 %copy-start.3 = (bf16[1,3072]{1,0:T(2,128)(2,1)S(1)}, bf16[1,3072]{1,0:T(2,128)(2,1)}, u32[]{:S(2)}) copy-start(bf16[1,3072]{1,0:T(2,128)(2,1)} %modulation.1) | copy-start | bytes 18436
  2.7 19.3 %copy-start.4 = (s32[33]{0:T(128)S(1)}, s32[33]{0:T(128)}, u32[]{:S(2)}) copy-start(s32[33]{0:T(128)} %timesteps.1) | copy-start | bytes 400
  2.7 34.5 %all-to-all-start = ((bf16[16,80,128]{2,1,0:T(8,128)(2,1)}), bf16[16,80,128]{2,1,0:T(8,128)(2,1)S(1)}, u32[]{:S(2)}, u32[]{:S(2)}) async-start(bf16[16,80,128]{2,1,0:T(8,128)(2,1)} %shard_map.87), calls=%async_computation | async-start | bytes 655360 | tf_op jit(solution)/shard_map/all_to_all | solution.py:92
  75.0 12.4 %all-to-all-start.3 = ((bf16[32,32,128]{2,1,0:T(8,128)(2,1)}), bf16[32,32,128]{2,1,0:T(8,128)(2,1)S(1)}, u32[]{:S(2)}, u32[]{:S(2)}) async-start(bf16[32,32,128]{2,1,0:T(8,128)(2,1)} %get-tuple-element.29), calls=%async_computation.3 | async-start | bytes 524288 | tf_op jit(solution)/shard_map/all_to_all | solution.py:92
  104.5 12.3 %all-to-all-start.5 = ((f32[32,8,128]{2,1,0:T(8,128)}), f32[32,8,128]{2,1,0:T(8,128)S(1)}, u32[]{:S(2)}, u32[]{:S(2)}) async-start(f32[32,8,128]{2,1,0:T(8,128)} %get-tuple-element.36), calls=%async_computation.5 | async-start | bytes 262144 | tf_op jit(solution)/shard_map/all_to_all | solution.py:92

commit v8 on v7

--- a/solution.py
+++ b/solution.py
@@ -196,8 +196,8 @@
     first = dot(left[...], qk[...])
     value = dot(left[...], vw[...])[:, :C]
     query, key = first[:, :C], first[:, C:]
-    rank = lax.rem(seq - lax.rem(seq, 2) + Z - FIRST_Z, Z)
-    head = [both[group % 2, rank + group // 2, 64:80, C:].astype(F32) for group in range(4)]
+    ranks = [sum(jnp.where(seq // 2 == z // 2, Z_ORDER.index(z), 0) for z in range(late, Z, 2)) for late in range(2)]
+    head = [both[group % 2, ranks[group // 2], 64:80, C:].astype(F32) for group in range(4)]
     head = jnp.concatenate(head, axis=0)
     a = lax.dot_general(query, key, NT, precision=BEST, preferred_element_type=F32) * SCALE
     b = jnp.dot(value, head, precision=BEST, preferred_element_type=F32)
@@ -290,30 +290,29 @@
     return total
 
 
-def first_prefix(coef, got, start, first_eps, table, latents, out):
+def first_prefix(coef, got, start, first_eps, table, latents, mine, out):
     z, core, _ = place()
     x = packed_start(start, core)
     even = x + coef[4:5] * x + below(got, z)
     odd = even + coef[0:1] * x + coef[2:3] * first_eps[...]
     latents[0] = even
     latents[1] = odd
-    sent = [pack(normalized(unpack(x.astype(BF).astype(F32)), table)).astype(BF) for x in (even, odd)]
+    sent = []
+    for step, x in enumerate((even, odd)):
+        mine[step] = normalized(unpack(x.astype(BF).astype(F32)), table)
+        sent.append(pack(mine[step]).astype(BF))
     for to in range(PEERS):
         out[to, 0:16, :] = sent[0]
         out[to, 16:32, :] = sent[1]
 
 
-def second_queries(latents, table, heads, query, direct):
-    for step in range(2):
-        x = unpack(latents[step].astype(BF).astype(F32))
-        direct[step] = direct_of(x, table)
-        ask(step, heads, normalized(x, table), query)
-
-
-def second_sweep(coef, got, latents, heads, query, direct, term, out, key, weight, mix):
+def second_sweep(coef, got, latents, mine, table, heads, term, out, query, key, weight, mix):
+    direct = []
     for step in range(2):
         everything = got[:, 16 * step : 16 * step + 16, :].astype(F32).reshape(PEERS * 16, 128)
         key[step] = unpack(everything, 1.0).astype(BF)
+        direct.append(direct_of(unpack(latents[step].astype(BF).astype(F32)), table))
+        ask(step, heads, mine[step], query)
     eps = attend(heads, query, direct, (key.at[0], key.at[1]), weight, mix)
     terms = [coef[step : step + 1] * latents[step] + coef[2 + step : 3 + step] * eps[step] for step in range(2)]
     term[...] = terms[0]
@@ -322,27 +321,32 @@
         out[to] = both
 
 
-def second_prefix(got, start, latents, term, fresh, out):
+def second_prefix(got, start, latents, term, out):
     z, core, _ = place()
     even = packed_start(start, core) + below(got, z)
-    fresh[0] = even
-    fresh[1] = even + term[...]
+    fresh = (even, even + term[...])
     for step in range(2):
         change = fresh[step] - latents[step]
         squared = change * change
-        squared = squared[:8] + squared[8:]
-        for to in range(PEERS // 2):
-            out[step * 16 + to] = squared
+        out[step, 0:16, :] = fresh[step]
+        out[step, 16:24, :] = squared[:8] + squared[8:]
+
+
+def send_errors(halves, out):
+    _, core, _ = place()
+    squared = halves[0, core, 16:24, :] + halves[1, core, 16:24, :]
+    for to in range(PEERS // 2):
+        out[to] = squared
 
 
 def finish(got, halves, window, errors):
     _, core, _ = place()
     for half in range(2):
-        packed = halves[half, core]
+        packed = halves[half, core, 0:16, :]
         window[0, half * 32 : half * 32 + 16, :] = packed[:, :C]
         window[0, half * 32 + 16 : half * 32 + 32, :] = packed[:, C:]
     total = got[0]
-    for at in range(1, PEERS):
+    for at in range(1, PEERS // 2):
         total = total + got[at]
     total = jnp.sum(total, axis=(0, 1), keepdims=True)
     errors[...] = jnp.sqrt(total / (TOKENS * C) + 1e-06)
@@ -395,28 +399,23 @@
         scratch=(pltpu.VMEM((2, HEADS * 32, 128), BF), *work_space()),
     )
     got = exchange(sent, "z")
-    latents, sent = call(
-        first_prefix, (shape((2, 16, 128), F32), shape((PEERS, 32, 128), BF)), (coef, got, start, first_eps, table)
+    latents, mine, sent = call(
+        first_prefix,
+        (shape((2, 16, 128), F32), shape((2, 32, 128), F32), shape((PEERS, 32, 128), BF)),
+        (coef, got, start, first_eps, table),
     )
     got = exchange(sent, FLAT)
-    query, direct = call(
-        second_queries,
-        (shape((2, HEADS * 32, 128), BF), shape((2, 16, 128), F32)),
-        (latents, table, heads),
-        flops=10**9,
-    )
     term, sent = call(
         second_sweep,
         (shape((16, 128), F32), shape((Z, 16, 128), BF)),
-        (coef, got, latents, heads, query, direct),
-        scratch=work_space(),
+        (coef, got, latents, mine, table, heads),
+        scratch=(pltpu.VMEM((2, HEADS * 32, 128), BF), *work_space()),
     )
     got = exchange(sent, "z")
-    fresh, sent = call(
-        second_prefix, (shape((2, 16, 128), F32), shape((PEERS, 8, 128), F32)), (got, start, latents, term)
-    )
-    got = exchange(sent, FLAT)
+    fresh = call(second_prefix, shape((2, 24, 128), F32), (got, start, latents, term))
     halves = lax.all_gather(fresh, "core")
+    sent = call(send_errors, shape((PEERS // 2, 8, 128), F32), (halves,))
+    got = exchange(sent, ("y", "x"))
     window, errors = call(finish, (shape((1, 64, C), F32), shape((1, 1), F32)), (got, halves))
     return window, errors.reshape(1)
 

time: 118 us -> 116 us (0.983)
  blocking collectives: 51.7 us -> 73.9 us
  starting transfers between devices: 36.9 us -> 19.3 us
  waiting for transfers between devices: 18 us -> 13.7 us
  Pallas kernels: 10.1 us -> 8.31 us
    all_to_all x3 -> x5, blocking collectives: 44.1 us -> 65.7 us  [exchange(): lax.all_to_all(values, axis, 0, 0, axis_index_groups=[order], tiled=True)]
    all_to_all x3 -> x1, starting transfers between devices: 36.9 us -> 19.3 us  [exchange(): lax.all_to_all(values, axis, 0, 0, axis_index_groups=[order], tiled=True)]
    all_to_all x3 -> x1, waiting for transfers between devices: 18 us -> 13.7 us  [exchange(): lax.all_to_all(values, axis, 0, 0, axis_index_groups=[order], tiled=True)]
    pallas_call x9, Pallas kernels: 10.1 us -> 8.31 us  [call(): pl.pallas_call(kernel, out_shape=outs, in_specs=[pl.BlockSpec(memory_spac...]
  transfers between devices with their start and end apart: 3 -> 1, of which waited for: 3 -> 1; matrix products, arithmetic and copies ran while one was open for 0% -> 0% of each run, Pallas kernels for 2% -> 1%
where the time goes in v8:
time: 116 us
  blocking collectives  73.9 us (64%)
  starting transfers between devices  19.3 us (17%)
  waiting for transfers between devices  13.7 us (12%)
  Pallas kernels  8.31 us (7%)
    all_to_all x5, blocking collectives, exchange(): lax.all_to_all(values, axis, 0, 0, axis_index_groups=[order], tiled=True)  65.7 us
    all_to_all x1, starting transfers between devices, exchange(): lax.all_to_all(values, axis, 0, 0, axis_index_groups=[order], tiled=True)  19.3 us
    all_to_all x1, waiting for transfers between devices, exchange(): lax.all_to_all(values, axis, 0, 0, axis_index_groups=[order], tiled=True)  13.7 us
    pallas_call x9, Pallas kernels, call(): pl.pallas_call(kernel, out_shape=outs, in_specs=[pl.BlockSpec(memory_spac...  8.31 us
    all_gather x1, blocking collectives, body(): got = lax.all_gather(exchange(sent, ('y', 'x')), 'core')  2.97 us
    all_gather x1, blocking collectives, body(): lax.all_gather(got, 'core')  2.78 us
    all_gather x1, blocking collectives, body(): halves = lax.all_gather(fresh, 'core')  2.45 us
  transfers between devices with their start and end apart: 1, of which 1 were waited for; matrix products, arithmetic and copies ran while one was open for 0% of the time, Pallas kernels for 1%

profile of v8, /device:TPU:1, one launch (start us, length us, event | category | flops | bytes accessed | tf_op | source)
XLA Modules:
  0.0 115.9 jit_solution(10427219823272145722)
XLA Ops:
  0.6 2.0 %shard_map.87 = bf16[16,80,128]{2,1,0:T(8,128)(2,1)} custom-call(bf16[48,3072]{1,0:T(8,128)(2,1)} %w_qkv.1, bf16[32,1536]{1,0:T(8,128)(2,1)} %w_o.1, bf16[64,1536]{1,0:T(8,128)(2,1)} %bitcast.9), custom_call_target="tpu_custom_call" | custom-call | tf_op jit(solution)/shard_map/pallas_call | solution.py:79
  2.7 0.0 copy-start
  2.7 0.0 copy-start.1
  2.7 0.0 copy-start.2
  2.7 0.0 copy-start.3
  2.7 0.0 copy-start.4
  2.7 19.3 %all-to-all-start = ((bf16[16,80,128]{2,1,0:T(8,128)(2,1)}), bf16[16,80,128]{2,1,0:T(8,128)(2,1)S(1)}, u32[]{:S(2)}, u32[]{:S(2)}) async-start(bf16[16,80,128]{2,1,0:T(8,128)(2,1)} %shard_map.87), calls=%async_computation | async-start | bytes 655360 | tf_op jit(solution)/shard_map/all_to_all | solution.py:92
  22.0 0.0 copy-done
  22.0 0.0 copy-done.1
  22.0 0.0 copy-done.2
  22.0 0.0 copy-done.3
  22.0 0.0 copy-done.4
  22.1 1.5 %shard_map.86 = (bf16[80,1536]{1,0:T(8,128)(2,1)S(1)}, bf16[5,128,128]{2,1,0:T(8,128)(2,1)S(1)}, f32[8,128]{1,0:T(8,128)S(1)}, f32[32,128]{1,0:T(8,128)S(1)}, f3...) custom-call(s32[33]{0:T(128)S(1)} %copy-done.4, bf16[64,1536]{1,0:T(8,128)(2,1)S(1)} %copy-done.2, ...), custom_call_target="tpu_custom_call" | custom-call | flops 1000000000 | tf_op jit(solution)/shard_map/pallas_call | solution.py:79
  23.6 13.7 %all-to-all-done = bf16[16,80,128]{2,1,0:T(8,128)(2,1)S(1)} async-done(((bf16[16,80,128]{2,1,0:T(8,128)(2,1)}), bf16[16,80,128]{2,1,0:T(8,128)(2,1)S(1)}, u32[]{:S(2)}, u32[]{:S(2)}) %all-to-all-start) | async-done | bytes 327712 | tf_op jit(solution)/shard_map/all_to_all | solution.py:92
  37.3 2.8 %all-gather = bf16[32,80,128]{2,1,0:T(8,128)(2,1)S(1)} all-gather(bf16[16,80,128]{2,1,0:T(8,128)(2,1)S(1)} %all-to-all-done), channel_id=2, replica_groups=mesh['z'=16,'core'=2,'y'=4,'x'=4] {'core'}, dimensions={0}, use_global_device_ids=true | all-gather | bytes 983040 | tf_op jit(solution)/shard_map/all_gather | solution.py:391
  40.1 0.7 shard_map.88
  40.8 13.4 %all_to_all.30 = bf16[16,96,128]{2,1,0:T(8,128)(2,1)S(1)} all-to-all(bf16[16,96,128]{2,1,0:T(8,128)(2,1)S(1)} %shard_map.88), channel_id=1, replica_groups={{10,11,12,13,14,15,0,1,2,3,4,5,6,7,8,9},{26,27,28,29,30,31,16,17,18,19,..., dimensions={0} | all-to-all | bytes 786432 | tf_op jit(solution)/shard_map/all_to_all | solution.py:92
  54.2 3.0 %all-gather.1 = bf16[32,96,128]{2,1,0:T(8,128)(2,1)S(1)} all-gather(bf16[16,96,128]{2,1,0:T(8,128)(2,1)S(1)} %all_to_all.30), channel_id=3, replica_groups=mesh['z'=16,'core'=2,'y'=4,'x'=4] {'core'}, dimensions={0}, use_global_device_ids=true | all-gather | bytes 1179648 | tf_op jit(solution)/shard_map/all_gather | solution.py:394
  57.2 1.3 %shard_map.89 = (bf16[16,128,128]{2,1,0:T(8,128)(2,1)S(1)}, f32[16,128]{1,0:T(8,128)S(1)}, bf16[16,16,128]{2,1,0:T(8,128)(2,1)S(1)}) custom-call(f32[8,128]{1,0:T(8,128)S(1)} %get-tuple-element.18.coef, bf16[2,16,96,128]{3,2,1,0:T(8,128)(2,1)S(1)} %bitcast.5, f32[32,128]{1,0:T(8,128)S(1)} %get-tuple-element.21.mine, f32[16,128]{1,0:T(8,128)S(1)} %get-tuple-element.22.direct), custom_call_target="tpu_custom_call" | custom-call | tf_op jit(solution)/shard_map/pallas_call | solution.py:79
  58.5 15.4 %all_to_all.31.got = bf16[16,16,128]{2,1,0:T(8,128)(2,1)S(1)} all-to-all(bf16[16,16,128]{2,1,0:T(8,128)(2,1)S(1)} %get-tuple-element.23), channel_id=1, replica_groups={{256,288,320,352,384,416,448,480,0,32,64,96,128,160,192,224},{257,289,3..., dimensions={0} | all-to-all | bytes 131072 | tf_op jit(solution)/shard_map/all_to_all | solution.py:92
  73.9 0.5 shard_map.90
  74.4 12.2 %all_to_all.32.got = bf16[32,32,128]{2,1,0:T(8,128)(2,1)S(1)} all-to-all(bf16[32,32,128]{2,1,0:T(8,128)(2,1)S(1)} %get-tuple-element.26), channel_id=1, replica_groups={{10,11,12,13,14,15,0,1,2,3,4,5,6,7,8,9,26,27,28,29,30,31,16,17,18,19,20..., dimensions={0} | all-to-all | bytes 524288 | tf_op jit(solution)/shard_map/all_to_all | solution.py:92
  86.5 1.4 %shard_map.91 = (f32[16,128]{1,0:T(8,128)S(1)}, bf16[16,16,128]{2,1,0:T(8,128)(2,1)S(1)}) custom-call(f32[8,128]{1,0:T(8,128)S(1)} %get-tuple-element.18.coef, bf16[32,32,128]{2,1,0:T(8,128)(2,1)S(1)} %all_to_all.32.got, f32[2,16,128]{2,1,0:T(8,128)S(1)} %get-tuple-element.27.latents, f32[2,32,128]{2,1,0:T(8,128)S(1)} %get-tuple-element.28.mine, ...), custom_call_target="tpu_custom_call" | custom-call | tf_op jit(solution)/shard_map/pallas_call | solution.py:79
  87.9 15.3 %all_to_all.33.got = bf16[16,16,128]{2,1,0:T(8,128)(2,1)S(1)} all-to-all(bf16[16,16,128]{2,1,0:T(8,128)(2,1)S(1)} %get-tuple-element.30), channel_id=1, replica_groups={{256,288,320,352,384,416,448,480,0,32,64,96,128,160,192,224},{257,289,3..., dimensions={0} | all-to-all | bytes 131072 | tf_op jit(solution)/shard_map/all_to_all | solution.py:92
  103.2 0.1 shard_map.92
  103.3 2.4 %all-gather.2 = f32[4,24,128]{2,1,0:T(8,128)S(1)} all-gather(f32[2,24,128]{2,1,0:T(8,128)S(1)} %shard_map.92), channel_id=4, replica_groups=mesh['z'=16,'core'=2,'y'=4,'x'=4] {'core'}, dimensions={0}, use_global_device_ids=true | all-gather | bytes 73728 | tf_op jit(solution)/shard_map/all_gather | solution.py:416
  105.7 9.5 %all_to_all.34.got = f32[16,8,128]{2,1,0:T(8,128)S(1)} all-to-all(f32[16,8,128]{2,1,0:T(8,128)S(1)} %shard_map.93), channel_id=1, replica_groups={{10,11,12,13,14,15,0,1,2,3,4,5,6,7,8,9},{26,27,28,29,30,31,16,17,18,19,..., dimensions={0} | all-to-all | bytes 131072 | tf_op jit(solution)/shard_map/all_to_all | solution.py:92
  115.2 0.7 shard_map.94
  (1 shorter events, 0.0 us)
Async XLA Ops:
  2.7 19.3 %copy-start = (bf16[1536,64]{0,1:T(8,128)(2,1)S(1)}, bf16[1536,64]{0,1:T(8,128)(2,1)}, u32[]{:S(2)}) copy-start(bf16[1536,64]{0,1:T(8,128)(2,1)} %param.13) | copy-start | bytes 589828
  2.7 19.3 %copy-start.1 = (f32[64,64]{1,0:T(8,128)S(1)}, f32[64,64]{1,0:T(8,128)}, u32[]{:S(2)}) copy-start(f32[64,64]{1,0:T(8,128)} %start.5) | copy-start | bytes 49156
  2.7 19.3 %copy-start.2 = (bf16[64,1536]{1,0:T(8,128)(2,1)S(1)}, bf16[64,1536]{1,0:T(8,128)(2,1)}, u32[]{:S(2)}) copy-start(bf16[64,1536]{1,0:T(8,128)(2,1)} %w_in.1) | copy-start | bytes 589828
  2.7 19.3 %copy-start.3 = (bf16[1,3072]{1,0:T(2,128)(2,1)S(1)}, bf16[1,3072]{1,0:T(2,128)(2,1)}, u32[]{:S(2)}) copy-start(bf16[1,3072]{1,0:T(2,128)(2,1)} %modulation.1) | copy-start | bytes 18436
  2.7 19.3 %copy-start.4 = (s32[33]{0:T(128)S(1)}, s32[33]{0:T(128)}, u32[]{:S(2)}) copy-start(s32[33]{0:T(128)} %timesteps.1) | copy-start | bytes 400
  2.7 34.5 %all-to-all-start = ((bf16[16,80,128]{2,1,0:T(8,128)(2,1)}), bf16[16,80,128]{2,1,0:T(8,128)(2,1)S(1)}, u32[]{:S(2)}, u32[]{:S(2)}) async-start(bf16[16,80,128]{2,1,0:T(8,128)(2,1)} %shard_map.87), calls=%async_computation | async-start | bytes 655360 | tf_op jit(solution)/shard_map/all_to_all | solution.py:92

commit v9 on v8

--- a/solution.py
+++ b/solution.py
@@ -103,7 +103,8 @@
     for at in range(3):
         start = pl.multiple_of(at * INNER + (seq // 2) * HEAD_DIM, HEAD_DIM)
         copies.append(pltpu.make_async_copy(w_qkv.at[:, pl.ds(start, HEAD_DIM)], blocks.at[at], arrived.at[at]))
-    copies.append(pltpu.make_async_copy(w_o, left, arrived.at[3]))
+    part = pl.multiple_of(lax.rem(seq, 2) * 16, 16)
+    copies.append(pltpu.make_async_copy(w_o.at[pl.ds(part, 16), :], left, arrived.at[3]))
     copies.append(pltpu.make_async_copy(w_out, right, arrived.at[4]))
     for copy in copies:
         copy.start()
@@ -127,7 +128,6 @@
     copies[3].wait()
     copies[4].wait()
     head = lax.dot_general(left[...], right[...], NT, preferred_element_type=F32)
-    head = jnp.where(odd, head[16:], head[:16])
     second = jnp.concatenate([value[0:16], value[16:32]], axis=1).astype(BF)
     third = jnp.concatenate([value[32:48], head], axis=1).astype(BF)
     for to in range(Z):
@@ -214,7 +214,7 @@
 def normalized(x, table):
     exact = x.astype(BF)
     y = dot(exact, table[0]) + dot(exact, table[1]) + dot(exact, table[2])
-    spread = jnp.sum(x * y, axis=1, keepdims=True)
+    spread = jnp.maximum(jnp.sum(x * y, axis=1, keepdims=True), 0.0)
     return jnp.where(lanes(x.shape) == C, 1.0, x * lax.rsqrt(spread + 1e-06))
 
 
@@ -359,7 +359,7 @@
         (w_qkv, w_o, w_out.T),
         scratch=(
             pltpu.VMEM((3, ROWS, HEAD_DIM), BF),
-            pltpu.VMEM((32, D), BF),
+            pltpu.VMEM((16, D), BF),
             pltpu.VMEM((C, D), BF),
             pltpu.VMEM((Z, 48, 128), BF),
             pltpu.VMEM((Z, 32, 128), BF),

time: 116 us -> 116 us (level)
  no operation moved by 1% of the time
where the time goes in v9:
time: 116 us
  blocking collectives  73.9 us (64%)
  starting transfers between devices  19.3 us (17%)
  waiting for transfers between devices  13.7 us (12%)
  Pallas kernels  8.3 us (7%)
    all_to_all x5, blocking collectives, exchange(): lax.all_to_all(values, axis, 0, 0, axis_index_groups=[order], tiled=True)  65.7 us
    all_to_all x1, starting transfers between devices, exchange(): lax.all_to_all(values, axis, 0, 0, axis_index_groups=[order], tiled=True)  19.3 us
    all_to_all x1, waiting for transfers between devices, exchange(): lax.all_to_all(values, axis, 0, 0, axis_index_groups=[order], tiled=True)  13.7 us
    pallas_call x9, Pallas kernels, call(): pl.pallas_call(kernel, out_shape=outs, in_specs=[pl.BlockSpec(memory_spac...  8.3 us
    all_gather x1, blocking collectives, body(): got = lax.all_gather(exchange(sent, ('y', 'x')), 'core')  2.97 us
    all_gather x1, blocking collectives, body(): lax.all_gather(got, 'core')  2.79 us
    all_gather x1, blocking collectives, body(): halves = lax.all_gather(fresh, 'core')  2.45 us
  transfers between devices with their start and end apart: 1, of which 1 were waited for; matrix products, arithmetic and copies ran while one was open for 0% of the time, Pallas kernels for 1%

profile of v9, /device:TPU:1, one launch (start us, length us, event | category | flops | bytes accessed | tf_op | source)
XLA Modules:
  0.0 115.9 jit_solution(8027038198130194768)
XLA Ops:
  0.6 2.0 %shard_map.87 = bf16[16,80,128]{2,1,0:T(8,128)(2,1)} custom-call(bf16[48,3072]{1,0:T(8,128)(2,1)} %w_qkv.1, bf16[32,1536]{1,0:T(8,128)(2,1)} %w_o.1, bf16[64,1536]{1,0:T(8,128)(2,1)} %bitcast.9), custom_call_target="tpu_custom_call" | custom-call | tf_op jit(solution)/shard_map/pallas_call | solution.py:79
  2.7 0.0 copy-start
  2.7 0.0 copy-start.1
  2.7 0.0 copy-start.2
  2.7 0.0 copy-start.3
  2.7 0.0 copy-start.4
  2.7 19.3 %all-to-all-start = ((bf16[16,80,128]{2,1,0:T(8,128)(2,1)}), bf16[16,80,128]{2,1,0:T(8,128)(2,1)S(1)}, u32[]{:S(2)}, u32[]{:S(2)}) async-start(bf16[16,80,128]{2,1,0:T(8,128)(2,1)} %shard_map.87), calls=%async_computation | async-start | bytes 655360 | tf_op jit(solution)/shard_map/all_to_all | solution.py:92
  22.0 0.0 copy-done
  22.0 0.0 copy-done.1
  22.0 0.0 copy-done.2
  22.0 0.0 copy-done.3
  22.0 0.0 copy-done.4
  22.0 1.5 %shard_map.86 = (bf16[80,1536]{1,0:T(8,128)(2,1)S(1)}, bf16[5,128,128]{2,1,0:T(8,128)(2,1)S(1)}, f32[8,128]{1,0:T(8,128)S(1)}, f32[32,128]{1,0:T(8,128)S(1)}, f3...) custom-call(s32[33]{0:T(128)S(1)} %copy-done.4, bf16[64,1536]{1,0:T(8,128)(2,1)S(1)} %copy-done.2, ...), custom_call_target="tpu_custom_call" | custom-call | flops 1000000000 | tf_op jit(solution)/shard_map/pallas_call | solution.py:79
  23.6 13.7 %all-to-all-done = bf16[16,80,128]{2,1,0:T(8,128)(2,1)S(1)} async-done(((bf16[16,80,128]{2,1,0:T(8,128)(2,1)}), bf16[16,80,128]{2,1,0:T(8,128)(2,1)S(1)}, u32[]{:S(2)}, u32[]{:S(2)}) %all-to-all-start) | async-done | bytes 327712 | tf_op jit(solution)/shard_map/all_to_all | solution.py:92
  37.3 2.8 %all-gather = bf16[32,80,128]{2,1,0:T(8,128)(2,1)S(1)} all-gather(bf16[16,80,128]{2,1,0:T(8,128)(2,1)S(1)} %all-to-all-done), channel_id=2, replica_groups=mesh['z'=16,'core'=2,'y'=4,'x'=4] {'core'}, dimensions={0}, use_global_device_ids=true | all-gather | bytes 983040 | tf_op jit(solution)/shard_map/all_gather | solution.py:391
  40.1 0.7 shard_map.88
  40.8 13.4 %all_to_all.30 = bf16[16,96,128]{2,1,0:T(8,128)(2,1)S(1)} all-to-all(bf16[16,96,128]{2,1,0:T(8,128)(2,1)S(1)} %shard_map.88), channel_id=1, replica_groups={{10,11,12,13,14,15,0,1,2,3,4,5,6,7,8,9},{26,27,28,29,30,31,16,17,18,19,..., dimensions={0} | all-to-all | bytes 786432 | tf_op jit(solution)/shard_map/all_to_all | solution.py:92
  54.2 3.0 %all-gather.1 = bf16[32,96,128]{2,1,0:T(8,128)(2,1)S(1)} all-gather(bf16[16,96,128]{2,1,0:T(8,128)(2,1)S(1)} %all_to_all.30), channel_id=3, replica_groups=mesh['z'=16,'core'=2,'y'=4,'x'=4] {'core'}, dimensions={0}, use_global_device_ids=true | all-gather | bytes 1179648 | tf_op jit(solution)/shard_map/all_gather | solution.py:394
  57.2 1.3 %shard_map.89 = (bf16[16,128,128]{2,1,0:T(8,128)(2,1)S(1)}, f32[16,128]{1,0:T(8,128)S(1)}, bf16[16,16,128]{2,1,0:T(8,128)(2,1)S(1)}) custom-call(f32[8,128]{1,0:T(8,128)S(1)} %get-tuple-element.18.coef, bf16[2,16,96,128]{3,2,1,0:T(8,128)(2,1)S(1)} %bitcast.5, f32[32,128]{1,0:T(8,128)S(1)} %get-tuple-element.21.mine, f32[16,128]{1,0:T(8,128)S(1)} %get-tuple-element.22.direct), custom_call_target="tpu_custom_call" | custom-call | tf_op jit(solution)/shard_map/pallas_call | solution.py:79
  58.5 15.4 %all_to_all.31.got = bf16[16,16,128]{2,1,0:T(8,128)(2,1)S(1)} all-to-all(bf16[16,16,128]{2,1,0:T(8,128)(2,1)S(1)} %get-tuple-element.23), channel_id=1, replica_groups={{256,288,320,352,384,416,448,480,0,32,64,96,128,160,192,224},{257,289,3..., dimensions={0} | all-to-all | bytes 131072 | tf_op jit(solution)/shard_map/all_to_all | solution.py:92
  73.9 0.5 shard_map.90
  74.3 12.2 %all_to_all.32.got = bf16[32,32,128]{2,1,0:T(8,128)(2,1)S(1)} all-to-all(bf16[32,32,128]{2,1,0:T(8,128)(2,1)S(1)} %get-tuple-element.26), channel_id=1, replica_groups={{10,11,12,13,14,15,0,1,2,3,4,5,6,7,8,9,26,27,28,29,30,31,16,17,18,19,20..., dimensions={0} | all-to-all | bytes 524288 | tf_op jit(solution)/shard_map/all_to_all | solution.py:92
  86.5 1.4 %shard_map.91 = (f32[16,128]{1,0:T(8,128)S(1)}, bf16[16,16,128]{2,1,0:T(8,128)(2,1)S(1)}) custom-call(f32[8,128]{1,0:T(8,128)S(1)} %get-tuple-element.18.coef, bf16[32,32,128]{2,1,0:T(8,128)(2,1)S(1)} %all_to_all.32.got, f32[2,16,128]{2,1,0:T(8,128)S(1)} %get-tuple-element.27.latents, f32[2,32,128]{2,1,0:T(8,128)S(1)} %get-tuple-element.28.mine, ...), custom_call_target="tpu_custom_call" | custom-call | tf_op jit(solution)/shard_map/pallas_call | solution.py:79
  87.9 15.3 %all_to_all.33.got = bf16[16,16,128]{2,1,0:T(8,128)(2,1)S(1)} all-to-all(bf16[16,16,128]{2,1,0:T(8,128)(2,1)S(1)} %get-tuple-element.30), channel_id=1, replica_groups={{256,288,320,352,384,416,448,480,0,32,64,96,128,160,192,224},{257,289,3..., dimensions={0} | all-to-all | bytes 131072 | tf_op jit(solution)/shard_map/all_to_all | solution.py:92
  103.2 0.1 shard_map.92
  103.3 2.4 %all-gather.2 = f32[4,24,128]{2,1,0:T(8,128)S(1)} all-gather(f32[2,24,128]{2,1,0:T(8,128)S(1)} %shard_map.92), channel_id=4, replica_groups=mesh['z'=16,'core'=2,'y'=4,'x'=4] {'core'}, dimensions={0}, use_global_device_ids=true | all-gather | bytes 73728 | tf_op jit(solution)/shard_map/all_gather | solution.py:416
  105.7 9.5 %all_to_all.34.got = f32[16,8,128]{2,1,0:T(8,128)S(1)} all-to-all(f32[16,8,128]{2,1,0:T(8,128)S(1)} %shard_map.93), channel_id=1, replica_groups={{10,11,12,13,14,15,0,1,2,3,4,5,6,7,8,9},{26,27,28,29,30,31,16,17,18,19,..., dimensions={0} | all-to-all | bytes 131072 | tf_op jit(solution)/shard_map/all_to_all | solution.py:92
  115.2 0.7 shard_map.94
  (1 shorter events, 0.0 us)
Async XLA Ops:
  2.7 19.3 %copy-start = (bf16[1536,64]{0,1:T(8,128)(2,1)S(1)}, bf16[1536,64]{0,1:T(8,128)(2,1)}, u32[]{:S(2)}) copy-start(bf16[1536,64]{0,1:T(8,128)(2,1)} %param.13) | copy-start | bytes 589828
  2.7 19.3 %copy-start.1 = (f32[64,64]{1,0:T(8,128)S(1)}, f32[64,64]{1,0:T(8,128)}, u32[]{:S(2)}) copy-start(f32[64,64]{1,0:T(8,128)} %start.5) | copy-start | bytes 49156
  2.7 19.3 %copy-start.2 = (bf16[64,1536]{1,0:T(8,128)(2,1)S(1)}, bf16[64,1536]{1,0:T(8,128)(2,1)}, u32[]{:S(2)}) copy-start(bf16[64,1536]{1,0:T(8,128)(2,1)} %w_in.1) | copy-start | bytes 589828
  2.7 19.3 %copy-start.3 = (bf16[1,3072]{1,0:T(2,128)(2,1)S(1)}, bf16[1,3072]{1,0:T(2,128)(2,1)}, u32[]{:S(2)}) copy-start(bf16[1,3072]{1,0:T(2,128)(2,1)} %modulation.1) | copy-start | bytes 18436
  2.7 19.3 %copy-start.4 = (s32[33]{0:T(128)S(1)}, s32[33]{0:T(128)}, u32[]{:S(2)}) copy-start(s32[33]{0:T(128)} %timesteps.1) | copy-start | bytes 400
  2.7 34.5 %all-to-all-start = ((bf16[16,80,128]{2,1,0:T(8,128)(2,1)}), bf16[16,80,128]{2,1,0:T(8,128)(2,1)S(1)}, u32[]{:S(2)}, u32[]{:S(2)}) async-start(bf16[16,80,128]{2,1,0:T(8,128)(2,1)} %shard_map.87), calls=%async_computation | async-start | bytes 655360 | tf_op jit(solution)/shard_map/all_to_all | solution.py:92

commit v10 on v9

--- a/solution.py
+++ b/solution.py
@@ -22,6 +22,7 @@
 FIRST_Z = 8
 FIRST_SEQ = 10
 Z_ORDER = [(at + FIRST_Z) % Z for at in range(Z)]
+Z_FIRST = [(at + 11) % Z for at in range(Z)]
 SEQ_ORDER = [(at + FIRST_SEQ) % 16 for at in range(16)]
 FLAT_ORDER = SEQ_ORDER + [16 + at for at in SEQ_ORDER]
 BF = jnp.bfloat16
@@ -72,6 +73,13 @@
         pieces.append(piece)
         values = values - piece.astype(F32)
     return pieces
+
+
+def fine_dot(a, b, dims):
+    a_high, a_low = split_of(a, 2)
+    b_high, b_low = split_of(b, 2)
+    parts = [lax.dot_general(x, y, dims, preferred_element_type=F32) for x, y in ((a_high, b_low), (a_low, b_high), (a_high, b_high))]
+    return parts[0] + parts[1] + parts[2]
 
 
 def call(kernel, outs, args, scratch=(), smem=(), far=(), flops=0, grant=40, out_far=False):
@@ -185,7 +193,7 @@
 
 def make_heads(both, left, own, out, qk, vw):
     _, _, seq = place()
-    for rank, z in enumerate(Z_ORDER):
+    for rank, z in enumerate(Z_FIRST):
         for parity in range(2):
             at = (z * 2 + parity) * ROWS
             qk[at : at + 48, :] = both[parity, rank, 0:48, :]
@@ -196,12 +204,12 @@
     first = dot(left[...], qk[...])
     value = dot(left[...], vw[...])[:, :C]
     query, key = first[:, :C], first[:, C:]
-    ranks = [sum(jnp.where(seq // 2 == z // 2, Z_ORDER.index(z), 0) for z in range(late, Z, 2)) for late in range(2)]
+    ranks = [sum(jnp.where(seq // 2 == z // 2, Z_FIRST.index(z), 0) for z in range(late, Z, 2)) for late in range(2)]
     head = [both[group % 2, ranks[group // 2], 64:80, C:].astype(F32) for group in range(4)]
     head = jnp.concatenate(head, axis=0)
-    a = lax.dot_general(query, key, NT, precision=BEST, preferred_element_type=F32) * SCALE
-    b = jnp.dot(value, head, precision=BEST, preferred_element_type=F32)
-    bias = lax.dot_general(key[C : C + 8], query, NT, precision=BEST, preferred_element_type=F32) * SCALE
+    a = fine_dot(query, key, NT) * SCALE
+    b = fine_dot(value, head, (((1,), (0,)), ((), ())))
+    bias = fine_dot(key[C : C + 8], query, NT) * SCALE
     bias = jnp.concatenate([bias, jnp.zeros((8, 128 - bias.shape[1]), F32)], axis=1)[0:1]
     main = jnp.concatenate([a[:, :C], b], axis=1)
     main = jnp.where(rows(main.shape) == C + 1, bias, main).astype(BF)
@@ -370,7 +378,7 @@
         grant=62,
         out_far=True,
     )
-    got = exchange(sent, "z")
+    got = lax.all_to_all(sent, "z", 0, 0, axis_index_groups=[Z_FIRST], tiled=True)
     left, table, coef, mine, direct, own = call(
         make_tables,
         (

time: 116 us -> 116 us (level)
  starting transfers between devices: 19.3 us -> 16.6 us
  waiting for transfers between devices: 13.7 us -> 16 us
    all_to_all x1, starting transfers between devices: 19.3 us -> 16.6 us  [body(): lax.all_to_all(sent, 'z', 0, 0, axis_index_groups=[Z_FIRST], tiled=True)]
    all_to_all x1, waiting for transfers between devices: 13.7 us -> 16 us  [body(): lax.all_to_all(sent, 'z', 0, 0, axis_index_groups=[Z_FIRST], tiled=True)]
where the time goes in v10:
time: 116 us
  blocking collectives  74 us (64%)
  starting transfers between devices  16.6 us (14%)
  waiting for transfers between devices  16 us (14%)
  Pallas kernels  8.22 us (7%)
    all_to_all x5, blocking collectives, exchange(): lax.all_to_all(values, axis, 0, 0, axis_index_groups=[order], tiled=True)  65.7 us
    all_to_all x1, starting transfers between devices, body(): lax.all_to_all(sent, 'z', 0, 0, axis_index_groups=[Z_FIRST], tiled=True)  16.6 us
    all_to_all x1, waiting for transfers between devices, body(): lax.all_to_all(sent, 'z', 0, 0, axis_index_groups=[Z_FIRST], tiled=True)  16 us
    pallas_call x9, Pallas kernels, call(): pl.pallas_call(kernel, out_shape=outs, in_specs=[pl.BlockSpec(memory_spac...  8.22 us
    all_gather x1, blocking collectives, body(): got = lax.all_gather(exchange(sent, ('y', 'x')), 'core')  2.97 us
    all_gather x1, blocking collectives, body(): lax.all_gather(got, 'core')  2.87 us
    all_gather x1, blocking collectives, body(): halves = lax.all_gather(fresh, 'core')  2.44 us
  transfers between devices with their start and end apart: 1, of which 1 were waited for; matrix products, arithmetic and copies ran while one was open for 0% of the time, Pallas kernels for 1%

profile of v10, /device:TPU:1, one launch (start us, length us, event | category | flops | bytes accessed | tf_op | source)
XLA Modules:
  0.0 115.6 jit_solution(8323367129404747538)
XLA Ops:
  0.6 2.0 %shard_map.87 = bf16[16,80,128]{2,1,0:T(8,128)(2,1)} custom-call(bf16[48,3072]{1,0:T(8,128)(2,1)} %w_qkv.1, bf16[32,1536]{1,0:T(8,128)(2,1)} %w_o.1, bf16[64,1536]{1,0:T(8,128)(2,1)} %bitcast.9), custom_call_target="tpu_custom_call" | custom-call | tf_op jit(solution)/shard_map/pallas_call | solution.py:87
  2.7 0.0 copy-start
  2.7 0.0 copy-start.1
  2.7 0.0 copy-start.2
  2.7 0.0 copy-start.3
  2.7 0.0 copy-start.4
  2.7 16.6 %all-to-all-start = ((bf16[16,80,128]{2,1,0:T(8,128)(2,1)}), bf16[16,80,128]{2,1,0:T(8,128)(2,1)S(1)}, u32[]{:S(2)}, u32[]{:S(2)}) async-start(bf16[16,80,128]{2,1,0:T(8,128)(2,1)} %shard_map.87), calls=%async_computation | async-start | bytes 655360 | tf_op jit(solution)/shard_map/all_to_all | solution.py:381
  19.3 0.0 copy-done
  19.3 0.0 copy-done.1
  19.3 0.0 copy-done.2
  19.3 0.0 copy-done.3
  19.3 0.0 copy-done.4
  19.3 1.5 %shard_map.86 = (bf16[80,1536]{1,0:T(8,128)(2,1)S(1)}, bf16[5,128,128]{2,1,0:T(8,128)(2,1)S(1)}, f32[8,128]{1,0:T(8,128)S(1)}, f32[32,128]{1,0:T(8,128)S(1)}, f3...) custom-call(s32[33]{0:T(128)S(1)} %copy-done.4, bf16[64,1536]{1,0:T(8,128)(2,1)S(1)} %copy-done.2, ...), custom_call_target="tpu_custom_call" | custom-call | flops 1000000000 | tf_op jit(solution)/shard_map/pallas_call | solution.py:87
  20.9 16.0 %all-to-all-done = bf16[16,80,128]{2,1,0:T(8,128)(2,1)S(1)} async-done(((bf16[16,80,128]{2,1,0:T(8,128)(2,1)}), bf16[16,80,128]{2,1,0:T(8,128)(2,1)S(1)}, u32[]{:S(2)}, u32[]{:S(2)}) %all-to-all-start) | async-done | bytes 327712 | tf_op jit(solution)/shard_map/all_to_all | solution.py:381
  36.9 2.9 %all-gather = bf16[32,80,128]{2,1,0:T(8,128)(2,1)S(1)} all-gather(bf16[16,80,128]{2,1,0:T(8,128)(2,1)S(1)} %all-to-all-done), channel_id=2, replica_groups=mesh['z'=16,'core'=2,'y'=4,'x'=4] {'core'}, dimensions={0}, use_global_device_ids=true | all-gather | bytes 983040 | tf_op jit(solution)/shard_map/all_gather | solution.py:399
  39.8 0.6 shard_map.88
  40.4 13.4 %all_to_all.30 = bf16[16,96,128]{2,1,0:T(8,128)(2,1)S(1)} all-to-all(bf16[16,96,128]{2,1,0:T(8,128)(2,1)S(1)} %shard_map.88), channel_id=1, replica_groups={{10,11,12,13,14,15,0,1,2,3,4,5,6,7,8,9},{26,27,28,29,30,31,16,17,18,19,..., dimensions={0} | all-to-all | bytes 786432 | tf_op jit(solution)/shard_map/all_to_all | solution.py:100
  53.9 3.0 %all-gather.1 = bf16[32,96,128]{2,1,0:T(8,128)(2,1)S(1)} all-gather(bf16[16,96,128]{2,1,0:T(8,128)(2,1)S(1)} %all_to_all.30), channel_id=3, replica_groups=mesh['z'=16,'core'=2,'y'=4,'x'=4] {'core'}, dimensions={0}, use_global_device_ids=true | all-gather | bytes 1179648 | tf_op jit(solution)/shard_map/all_gather | solution.py:402
  56.8 1.3 %shard_map.89 = (bf16[16,128,128]{2,1,0:T(8,128)(2,1)S(1)}, f32[16,128]{1,0:T(8,128)S(1)}, bf16[16,16,128]{2,1,0:T(8,128)(2,1)S(1)}) custom-call(f32[8,128]{1,0:T(8,128)S(1)} %get-tuple-element.18.coef, bf16[2,16,96,128]{3,2,1,0:T(8,128)(2,1)S(1)} %bitcast.5, f32[32,128]{1,0:T(8,128)S(1)} %get-tuple-element.21.mine, f32[16,128]{1,0:T(8,128)S(1)} %get-tuple-element.22.direct), custom_call_target="tpu_custom_call" | custom-call | tf_op jit(solution)/shard_map/pallas_call | solution.py:87
  58.2 15.4 %all_to_all.31.got = bf16[16,16,128]{2,1,0:T(8,128)(2,1)S(1)} all-to-all(bf16[16,16,128]{2,1,0:T(8,128)(2,1)S(1)} %get-tuple-element.23), channel_id=1, replica_groups={{256,288,320,352,384,416,448,480,0,32,64,96,128,160,192,224},{257,289,3..., dimensions={0} | all-to-all | bytes 131072 | tf_op jit(solution)/shard_map/all_to_all | solution.py:100
  73.5 0.5 shard_map.90
  74.0 12.2 %all_to_all.32.got = bf16[32,32,128]{2,1,0:T(8,128)(2,1)S(1)} all-to-all(bf16[32,32,128]{2,1,0:T(8,128)(2,1)S(1)} %get-tuple-element.26), channel_id=1, replica_groups={{10,11,12,13,14,15,0,1,2,3,4,5,6,7,8,9,26,27,28,29,30,31,16,17,18,19,20..., dimensions={0} | all-to-all | bytes 524288 | tf_op jit(solution)/shard_map/all_to_all | solution.py:100
  86.2 1.4 %shard_map.91 = (f32[16,128]{1,0:T(8,128)S(1)}, bf16[16,16,128]{2,1,0:T(8,128)(2,1)S(1)}) custom-call(f32[8,128]{1,0:T(8,128)S(1)} %get-tuple-element.18.coef, bf16[32,32,128]{2,1,0:T(8,128)(2,1)S(1)} %all_to_all.32.got, f32[2,16,128]{2,1,0:T(8,128)S(1)} %get-tuple-element.27.latents, f32[2,32,128]{2,1,0:T(8,128)S(1)} %get-tuple-element.28.mine, ...), custom_call_target="tpu_custom_call" | custom-call | tf_op jit(solution)/shard_map/pallas_call | solution.py:87
  87.6 15.3 %all_to_all.33.got = bf16[16,16,128]{2,1,0:T(8,128)(2,1)S(1)} all-to-all(bf16[16,16,128]{2,1,0:T(8,128)(2,1)S(1)} %get-tuple-element.30), channel_id=1, replica_groups={{256,288,320,352,384,416,448,480,0,32,64,96,128,160,192,224},{257,289,3..., dimensions={0} | all-to-all | bytes 131072 | tf_op jit(solution)/shard_map/all_to_all | solution.py:100
  102.9 0.1 shard_map.92
  102.9 2.4 %all-gather.2 = f32[4,24,128]{2,1,0:T(8,128)S(1)} all-gather(f32[2,24,128]{2,1,0:T(8,128)S(1)} %shard_map.92), channel_id=4, replica_groups=mesh['z'=16,'core'=2,'y'=4,'x'=4] {'core'}, dimensions={0}, use_global_device_ids=true | all-gather | bytes 73728 | tf_op jit(solution)/shard_map/all_gather | solution.py:424
  105.4 9.5 %all_to_all.34.got = f32[16,8,128]{2,1,0:T(8,128)S(1)} all-to-all(f32[16,8,128]{2,1,0:T(8,128)S(1)} %shard_map.93), channel_id=1, replica_groups={{10,11,12,13,14,15,0,1,2,3,4,5,6,7,8,9},{26,27,28,29,30,31,16,17,18,19,..., dimensions={0} | all-to-all | bytes 131072 | tf_op jit(solution)/shard_map/all_to_all | solution.py:100
  114.9 0.7 shard_map.94
  (1 shorter events, 0.0 us)
Async XLA Ops:
  2.7 16.6 %copy-start = (bf16[1536,64]{0,1:T(8,128)(2,1)S(1)}, bf16[1536,64]{0,1:T(8,128)(2,1)}, u32[]{:S(2)}) copy-start(bf16[1536,64]{0,1:T(8,128)(2,1)} %param.13) | copy-start | bytes 589828
  2.7 16.6 %copy-start.1 = (f32[64,64]{1,0:T(8,128)S(1)}, f32[64,64]{1,0:T(8,128)}, u32[]{:S(2)}) copy-start(f32[64,64]{1,0:T(8,128)} %start.5) | copy-start | bytes 49156
  2.7 16.6 %copy-start.2 = (bf16[64,1536]{1,0:T(8,128)(2,1)S(1)}, bf16[64,1536]{1,0:T(8,128)(2,1)}, u32[]{:S(2)}) copy-start(bf16[64,1536]{1,0:T(8,128)(2,1)} %w_in.1) | copy-start | bytes 589828
  2.7 16.6 %copy-start.3 = (bf16[1,3072]{1,0:T(2,128)(2,1)S(1)}, bf16[1,3072]{1,0:T(2,128)(2,1)}, u32[]{:S(2)}) copy-start(bf16[1,3072]{1,0:T(2,128)(2,1)} %modulation.1) | copy-start | bytes 18436
  2.7 16.6 %copy-start.4 = (s32[33]{0:T(128)S(1)}, s32[33]{0:T(128)}, u32[]{:S(2)}) copy-start(s32[33]{0:T(128)} %timesteps.1) | copy-start | bytes 400
  2.7 34.2 %all-to-all-start = ((bf16[16,80,128]{2,1,0:T(8,128)(2,1)}), bf16[16,80,128]{2,1,0:T(8,128)(2,1)S(1)}, u32[]{:S(2)}, u32[]{:S(2)}) async-start(bf16[16,80,128]{2,1,0:T(8,128)(2,1)} %shard_map.87), calls=%async_computation | async-start | bytes 655360 | tf_op jit(solution)/shard_map/all_to_all | solution.py:381

commit v11 on v10

--- a/solution.py
+++ b/solution.py
@@ -250,7 +250,7 @@
         weight[step] = jnp.exp2(scores[step] - tops[step]).astype(BF)
     mixed = [dot(weight[step], keys[step][...]) for step in both]
     for step in both:
-        shares = (mixed[step] / mixed[step][:, C : C + 1]).astype(BF)
+        shares = (mixed[step] * (1.0 / mixed[step][:, C : C + 1])).astype(BF)
         for head in range(HEADS):
             mix[step, :, head * 128 : (head + 1) * 128] = shares[head * 32 : (head + 1) * 32]
     eps = []

time: 116 us -> 116 us (level)
  no operation moved by 1% of the time
where the time goes in v11:
time: 116 us
  blocking collectives  74 us (64%)
  starting transfers between devices  16.6 us (14%)
  waiting for transfers between devices  16 us (14%)
  Pallas kernels  8.21 us (7%)
    all_to_all x5, blocking collectives, exchange(): lax.all_to_all(values, axis, 0, 0, axis_index_groups=[order], tiled=True)  65.7 us
    all_to_all x1, starting transfers between devices, body(): lax.all_to_all(sent, 'z', 0, 0, axis_index_groups=[Z_FIRST], tiled=True)  16.6 us
    all_to_all x1, waiting for transfers between devices, body(): lax.all_to_all(sent, 'z', 0, 0, axis_index_groups=[Z_FIRST], tiled=True)  16 us
    pallas_call x9, Pallas kernels, call(): pl.pallas_call(kernel, out_shape=outs, in_specs=[pl.BlockSpec(memory_spac...  8.21 us
    all_gather x1, blocking collectives, body(): got = lax.all_gather(exchange(sent, ('y', 'x')), 'core')  2.97 us
    all_gather x1, blocking collectives, body(): lax.all_gather(got, 'core')  2.87 us
    all_gather x1, blocking collectives, body(): halves = lax.all_gather(fresh, 'core')  2.45 us
  transfers between devices with their start and end apart: 1, of which 1 were waited for; matrix products, arithmetic and copies ran while one was open for 0% of the time, Pallas kernels for 1%

profile of v11, /device:TPU:1, one launch (start us, length us, event | category | flops | bytes accessed | tf_op | source)
XLA Modules:
  0.0 115.6 jit_solution(2291258017152640354)
XLA Ops:
  0.6 2.0 %shard_map.87 = bf16[16,80,128]{2,1,0:T(8,128)(2,1)} custom-call(bf16[48,3072]{1,0:T(8,128)(2,1)} %w_qkv.1, bf16[32,1536]{1,0:T(8,128)(2,1)} %w_o.1, bf16[64,1536]{1,0:T(8,128)(2,1)} %bitcast.9), custom_call_target="tpu_custom_call" | custom-call | tf_op jit(solution)/shard_map/pallas_call | solution.py:87
  2.7 0.0 copy-start
  2.7 0.0 copy-start.1
  2.7 0.0 copy-start.2
  2.7 0.0 copy-start.3
  2.7 0.0 copy-start.4
  2.7 16.6 %all-to-all-start = ((bf16[16,80,128]{2,1,0:T(8,128)(2,1)}), bf16[16,80,128]{2,1,0:T(8,128)(2,1)S(1)}, u32[]{:S(2)}, u32[]{:S(2)}) async-start(bf16[16,80,128]{2,1,0:T(8,128)(2,1)} %shard_map.87), calls=%async_computation | async-start | bytes 655360 | tf_op jit(solution)/shard_map/all_to_all | solution.py:381
  19.3 0.0 copy-done
  19.3 0.0 copy-done.1
  19.3 0.0 copy-done.2
  19.3 0.0 copy-done.3
  19.3 0.0 copy-done.4
  19.3 1.5 %shard_map.86 = (bf16[80,1536]{1,0:T(8,128)(2,1)S(1)}, bf16[5,128,128]{2,1,0:T(8,128)(2,1)S(1)}, f32[8,128]{1,0:T(8,128)S(1)}, f32[32,128]{1,0:T(8,128)S(1)}, f3...) custom-call(s32[33]{0:T(128)S(1)} %copy-done.4, bf16[64,1536]{1,0:T(8,128)(2,1)S(1)} %copy-done.2, ...), custom_call_target="tpu_custom_call" | custom-call | flops 1000000000 | tf_op jit(solution)/shard_map/pallas_call | solution.py:87
  20.9 16.0 %all-to-all-done = bf16[16,80,128]{2,1,0:T(8,128)(2,1)S(1)} async-done(((bf16[16,80,128]{2,1,0:T(8,128)(2,1)}), bf16[16,80,128]{2,1,0:T(8,128)(2,1)S(1)}, u32[]{:S(2)}, u32[]{:S(2)}) %all-to-all-start) | async-done | bytes 327712 | tf_op jit(solution)/shard_map/all_to_all | solution.py:381
  36.9 2.9 %all-gather = bf16[32,80,128]{2,1,0:T(8,128)(2,1)S(1)} all-gather(bf16[16,80,128]{2,1,0:T(8,128)(2,1)S(1)} %all-to-all-done), channel_id=2, replica_groups=mesh['z'=16,'core'=2,'y'=4,'x'=4] {'core'}, dimensions={0}, use_global_device_ids=true | all-gather | bytes 983040 | tf_op jit(solution)/shard_map/all_gather | solution.py:399
  39.8 0.6 shard_map.88
  40.4 13.4 %all_to_all.30 = bf16[16,96,128]{2,1,0:T(8,128)(2,1)S(1)} all-to-all(bf16[16,96,128]{2,1,0:T(8,128)(2,1)S(1)} %shard_map.88), channel_id=1, replica_groups={{10,11,12,13,14,15,0,1,2,3,4,5,6,7,8,9},{26,27,28,29,30,31,16,17,18,19,..., dimensions={0} | all-to-all | bytes 786432 | tf_op jit(solution)/shard_map/all_to_all | solution.py:100
  53.9 3.0 %all-gather.1 = bf16[32,96,128]{2,1,0:T(8,128)(2,1)S(1)} all-gather(bf16[16,96,128]{2,1,0:T(8,128)(2,1)S(1)} %all_to_all.30), channel_id=3, replica_groups=mesh['z'=16,'core'=2,'y'=4,'x'=4] {'core'}, dimensions={0}, use_global_device_ids=true | all-gather | bytes 1179648 | tf_op jit(solution)/shard_map/all_gather | solution.py:402
  56.8 1.3 %shard_map.89 = (bf16[16,128,128]{2,1,0:T(8,128)(2,1)S(1)}, f32[16,128]{1,0:T(8,128)S(1)}, bf16[16,16,128]{2,1,0:T(8,128)(2,1)S(1)}) custom-call(f32[8,128]{1,0:T(8,128)S(1)} %get-tuple-element.18.coef, bf16[2,16,96,128]{3,2,1,0:T(8,128)(2,1)S(1)} %bitcast.5, f32[32,128]{1,0:T(8,128)S(1)} %get-tuple-element.21.mine, f32[16,128]{1,0:T(8,128)S(1)} %get-tuple-element.22.direct), custom_call_target="tpu_custom_call" | custom-call | tf_op jit(solution)/shard_map/pallas_call | solution.py:87
  58.2 15.4 %all_to_all.31.got = bf16[16,16,128]{2,1,0:T(8,128)(2,1)S(1)} all-to-all(bf16[16,16,128]{2,1,0:T(8,128)(2,1)S(1)} %get-tuple-element.23), channel_id=1, replica_groups={{256,288,320,352,384,416,448,480,0,32,64,96,128,160,192,224},{257,289,3..., dimensions={0} | all-to-all | bytes 131072 | tf_op jit(solution)/shard_map/all_to_all | solution.py:100
  73.5 0.5 shard_map.90
  74.0 12.2 %all_to_all.32.got = bf16[32,32,128]{2,1,0:T(8,128)(2,1)S(1)} all-to-all(bf16[32,32,128]{2,1,0:T(8,128)(2,1)S(1)} %get-tuple-element.26), channel_id=1, replica_groups={{10,11,12,13,14,15,0,1,2,3,4,5,6,7,8,9,26,27,28,29,30,31,16,17,18,19,20..., dimensions={0} | all-to-all | bytes 524288 | tf_op jit(solution)/shard_map/all_to_all | solution.py:100
  86.2 1.4 %shard_map.91 = (f32[16,128]{1,0:T(8,128)S(1)}, bf16[16,16,128]{2,1,0:T(8,128)(2,1)S(1)}) custom-call(f32[8,128]{1,0:T(8,128)S(1)} %get-tuple-element.18.coef, bf16[32,32,128]{2,1,0:T(8,128)(2,1)S(1)} %all_to_all.32.got, f32[2,16,128]{2,1,0:T(8,128)S(1)} %get-tuple-element.27.latents, f32[2,32,128]{2,1,0:T(8,128)S(1)} %get-tuple-element.28.mine, ...), custom_call_target="tpu_custom_call" | custom-call | tf_op jit(solution)/shard_map/pallas_call | solution.py:87
  87.6 15.3 %all_to_all.33.got = bf16[16,16,128]{2,1,0:T(8,128)(2,1)S(1)} all-to-all(bf16[16,16,128]{2,1,0:T(8,128)(2,1)S(1)} %get-tuple-element.30), channel_id=1, replica_groups={{256,288,320,352,384,416,448,480,0,32,64,96,128,160,192,224},{257,289,3..., dimensions={0} | all-to-all | bytes 131072 | tf_op jit(solution)/shard_map/all_to_all | solution.py:100
  102.9 0.1 shard_map.92
  102.9 2.5 %all-gather.2 = f32[4,24,128]{2,1,0:T(8,128)S(1)} all-gather(f32[2,24,128]{2,1,0:T(8,128)S(1)} %shard_map.92), channel_id=4, replica_groups=mesh['z'=16,'core'=2,'y'=4,'x'=4] {'core'}, dimensions={0}, use_global_device_ids=true | all-gather | bytes 73728 | tf_op jit(solution)/shard_map/all_gather | solution.py:424
  105.4 9.5 %all_to_all.34.got = f32[16,8,128]{2,1,0:T(8,128)S(1)} all-to-all(f32[16,8,128]{2,1,0:T(8,128)S(1)} %shard_map.93), channel_id=1, replica_groups={{10,11,12,13,14,15,0,1,2,3,4,5,6,7,8,9},{26,27,28,29,30,31,16,17,18,19,..., dimensions={0} | all-to-all | bytes 131072 | tf_op jit(solution)/shard_map/all_to_all | solution.py:100
  114.8 0.7 shard_map.94
  (1 shorter events, 0.0 us)
Async XLA Ops:
  2.7 16.6 %copy-start = (bf16[1536,64]{0,1:T(8,128)(2,1)S(1)}, bf16[1536,64]{0,1:T(8,128)(2,1)}, u32[]{:S(2)}) copy-start(bf16[1536,64]{0,1:T(8,128)(2,1)} %param.13) | copy-start | bytes 589828
  2.7 16.6 %copy-start.1 = (f32[64,64]{1,0:T(8,128)S(1)}, f32[64,64]{1,0:T(8,128)}, u32[]{:S(2)}) copy-start(f32[64,64]{1,0:T(8,128)} %start.5) | copy-start | bytes 49156
  2.7 16.6 %copy-start.2 = (bf16[64,1536]{1,0:T(8,128)(2,1)S(1)}, bf16[64,1536]{1,0:T(8,128)(2,1)}, u32[]{:S(2)}) copy-start(bf16[64,1536]{1,0:T(8,128)(2,1)} %w_in.1) | copy-start | bytes 589828
  2.7 16.6 %copy-start.3 = (bf16[1,3072]{1,0:T(2,128)(2,1)S(1)}, bf16[1,3072]{1,0:T(2,128)(2,1)}, u32[]{:S(2)}) copy-start(bf16[1,3072]{1,0:T(2,128)(2,1)} %modulation.1) | copy-start | bytes 18436
  2.7 16.6 %copy-start.4 = (s32[33]{0:T(128)S(1)}, s32[33]{0:T(128)}, u32[]{:S(2)}) copy-start(s32[33]{0:T(128)} %timesteps.1) | copy-start | bytes 400
  2.7 34.2 %all-to-all-start = ((bf16[16,80,128]{2,1,0:T(8,128)(2,1)}), bf16[16,80,128]{2,1,0:T(8,128)(2,1)S(1)}, u32[]{:S(2)}, u32[]{:S(2)}) async-start(bf16[16,80,128]{2,1,0:T(8,128)(2,1)} %shard_map.87), calls=%async_computation | async-start | bytes 655360 | tf_op jit(solution)/shard_map/all_to_all | solution.py:381

commit v12 on v11

--- a/solution.py
+++ b/solution.py
@@ -22,7 +22,7 @@
 FIRST_Z = 8
 FIRST_SEQ = 10
 Z_ORDER = [(at + FIRST_Z) % Z for at in range(Z)]
-Z_FIRST = [(at + 11) % Z for at in range(Z)]
+Z_FIRST = [(at + 10) % Z for at in range(Z)]
 SEQ_ORDER = [(at + FIRST_SEQ) % 16 for at in range(16)]
 FLAT_ORDER = SEQ_ORDER + [16 + at for at in SEQ_ORDER]
 BF = jnp.bfloat16

time: 116 us -> 116 us (level)
  waiting for transfers between devices: 16 us -> 14 us
  blocking collectives: 74 us -> 75.2 us
    all_to_all x1, waiting for transfers between devices: 16 us -> 14 us  [body(): lax.all_to_all(sent, 'z', 0, 0, axis_index_groups=[Z_FIRST], tiled=True)]
    all_gather x1, blocking collectives: 2.87 us -> 4.04 us  [body(): lax.all_gather(got, 'core')]
where the time goes in v12:
time: 116 us
  blocking collectives  75.2 us (65%)
  starting transfers between devices  17.5 us (15%)
  waiting for transfers between devices  14 us (12%)
  Pallas kernels  8.22 us (7%)
    all_to_all x5, blocking collectives, exchange(): lax.all_to_all(values, axis, 0, 0, axis_index_groups=[order], tiled=True)  65.7 us
    all_to_all x1, starting transfers between devices, body(): lax.all_to_all(sent, 'z', 0, 0, axis_index_groups=[Z_FIRST], tiled=True)  17.5 us
    all_to_all x1, waiting for transfers between devices, body(): lax.all_to_all(sent, 'z', 0, 0, axis_index_groups=[Z_FIRST], tiled=True)  14 us
    pallas_call x9, Pallas kernels, call(): pl.pallas_call(kernel, out_shape=outs, in_specs=[pl.BlockSpec(memory_spac...  8.22 us
    all_gather x1, blocking collectives, body(): lax.all_gather(got, 'core')  4.04 us
    all_gather x1, blocking collectives, body(): got = lax.all_gather(exchange(sent, ('y', 'x')), 'core')  2.97 us
    all_gather x1, blocking collectives, body(): halves = lax.all_gather(fresh, 'core')  2.45 us
  transfers between devices with their start and end apart: 1, of which 1 were waited for; matrix products, arithmetic and copies ran while one was open for 0% of the time, Pallas kernels for 1%

profile of v12, /device:TPU:1, one launch (start us, length us, event | category | flops | bytes accessed | tf_op | source)
XLA Modules:
  0.0 115.6 jit_solution(4421557004144924339)
XLA Ops:
  0.6 2.0 %shard_map.87 = bf16[16,80,128]{2,1,0:T(8,128)(2,1)} custom-call(bf16[48,3072]{1,0:T(8,128)(2,1)} %w_qkv.1, bf16[32,1536]{1,0:T(8,128)(2,1)} %w_o.1, bf16[64,1536]{1,0:T(8,128)(2,1)} %bitcast.9), custom_call_target="tpu_custom_call" | custom-call | tf_op jit(solution)/shard_map/pallas_call | solution.py:87
  2.7 0.0 copy-start
  2.7 0.0 copy-start.1
  2.7 0.0 copy-start.2
  2.7 0.0 copy-start.3
  2.7 0.0 copy-start.4
  2.7 17.5 %all-to-all-start = ((bf16[16,80,128]{2,1,0:T(8,128)(2,1)}), bf16[16,80,128]{2,1,0:T(8,128)(2,1)S(1)}, u32[]{:S(2)}, u32[]{:S(2)}) async-start(bf16[16,80,128]{2,1,0:T(8,128)(2,1)} %shard_map.87), calls=%async_computation | async-start | bytes 655360 | tf_op jit(solution)/shard_map/all_to_all | solution.py:381
  20.2 0.0 copy-done
  20.2 0.0 copy-done.1
  20.2 0.0 copy-done.2
  20.2 0.0 copy-done.3
  20.2 0.0 copy-done.4
  20.2 1.5 %shard_map.86 = (bf16[80,1536]{1,0:T(8,128)(2,1)S(1)}, bf16[5,128,128]{2,1,0:T(8,128)(2,1)S(1)}, f32[8,128]{1,0:T(8,128)S(1)}, f32[32,128]{1,0:T(8,128)S(1)}, f3...) custom-call(s32[33]{0:T(128)S(1)} %copy-done.4, bf16[64,1536]{1,0:T(8,128)(2,1)S(1)} %copy-done.2, ...), custom_call_target="tpu_custom_call" | custom-call | flops 1000000000 | tf_op jit(solution)/shard_map/pallas_call | solution.py:87
  21.8 14.0 %all-to-all-done = bf16[16,80,128]{2,1,0:T(8,128)(2,1)S(1)} async-done(((bf16[16,80,128]{2,1,0:T(8,128)(2,1)}), bf16[16,80,128]{2,1,0:T(8,128)(2,1)S(1)}, u32[]{:S(2)}, u32[]{:S(2)}) %all-to-all-start) | async-done | bytes 327712 | tf_op jit(solution)/shard_map/all_to_all | solution.py:381
  35.8 4.0 %all-gather = bf16[32,80,128]{2,1,0:T(8,128)(2,1)S(1)} all-gather(bf16[16,80,128]{2,1,0:T(8,128)(2,1)S(1)} %all-to-all-done), channel_id=2, replica_groups=mesh['z'=16,'core'=2,'y'=4,'x'=4] {'core'}, dimensions={0}, use_global_device_ids=true | all-gather | bytes 983040 | tf_op jit(solution)/shard_map/all_gather | solution.py:399
  39.9 0.6 shard_map.88
  40.5 13.4 %all_to_all.30 = bf16[16,96,128]{2,1,0:T(8,128)(2,1)S(1)} all-to-all(bf16[16,96,128]{2,1,0:T(8,128)(2,1)S(1)} %shard_map.88), channel_id=1, replica_groups={{10,11,12,13,14,15,0,1,2,3,4,5,6,7,8,9},{26,27,28,29,30,31,16,17,18,19,..., dimensions={0} | all-to-all | bytes 786432 | tf_op jit(solution)/shard_map/all_to_all | solution.py:100
  54.0 3.0 %all-gather.1 = bf16[32,96,128]{2,1,0:T(8,128)(2,1)S(1)} all-gather(bf16[16,96,128]{2,1,0:T(8,128)(2,1)S(1)} %all_to_all.30), channel_id=3, replica_groups=mesh['z'=16,'core'=2,'y'=4,'x'=4] {'core'}, dimensions={0}, use_global_device_ids=true | all-gather | bytes 1179648 | tf_op jit(solution)/shard_map/all_gather | solution.py:402
  56.9 1.3 %shard_map.89 = (bf16[16,128,128]{2,1,0:T(8,128)(2,1)S(1)}, f32[16,128]{1,0:T(8,128)S(1)}, bf16[16,16,128]{2,1,0:T(8,128)(2,1)S(1)}) custom-call(f32[8,128]{1,0:T(8,128)S(1)} %get-tuple-element.18.coef, bf16[2,16,96,128]{3,2,1,0:T(8,128)(2,1)S(1)} %bitcast.5, f32[32,128]{1,0:T(8,128)S(1)} %get-tuple-element.21.mine, f32[16,128]{1,0:T(8,128)S(1)} %get-tuple-element.22.direct), custom_call_target="tpu_custom_call" | custom-call | tf_op jit(solution)/shard_map/pallas_call | solution.py:87
  58.2 15.4 %all_to_all.31.got = bf16[16,16,128]{2,1,0:T(8,128)(2,1)S(1)} all-to-all(bf16[16,16,128]{2,1,0:T(8,128)(2,1)S(1)} %get-tuple-element.23), channel_id=1, replica_groups={{256,288,320,352,384,416,448,480,0,32,64,96,128,160,192,224},{257,289,3..., dimensions={0} | all-to-all | bytes 131072 | tf_op jit(solution)/shard_map/all_to_all | solution.py:100
  73.6 0.5 shard_map.90
  74.1 12.2 %all_to_all.32.got = bf16[32,32,128]{2,1,0:T(8,128)(2,1)S(1)} all-to-all(bf16[32,32,128]{2,1,0:T(8,128)(2,1)S(1)} %get-tuple-element.26), channel_id=1, replica_groups={{10,11,12,13,14,15,0,1,2,3,4,5,6,7,8,9,26,27,28,29,30,31,16,17,18,19,20..., dimensions={0} | all-to-all | bytes 524288 | tf_op jit(solution)/shard_map/all_to_all | solution.py:100
  86.2 1.4 %shard_map.91 = (f32[16,128]{1,0:T(8,128)S(1)}, bf16[16,16,128]{2,1,0:T(8,128)(2,1)S(1)}) custom-call(f32[8,128]{1,0:T(8,128)S(1)} %get-tuple-element.18.coef, bf16[32,32,128]{2,1,0:T(8,128)(2,1)S(1)} %all_to_all.32.got, f32[2,16,128]{2,1,0:T(8,128)S(1)} %get-tuple-element.27.latents, f32[2,32,128]{2,1,0:T(8,128)S(1)} %get-tuple-element.28.mine, ...), custom_call_target="tpu_custom_call" | custom-call | tf_op jit(solution)/shard_map/pallas_call | solution.py:87
  87.7 15.3 %all_to_all.33.got = bf16[16,16,128]{2,1,0:T(8,128)(2,1)S(1)} all-to-all(bf16[16,16,128]{2,1,0:T(8,128)(2,1)S(1)} %get-tuple-element.30), channel_id=1, replica_groups={{256,288,320,352,384,416,448,480,0,32,64,96,128,160,192,224},{257,289,3..., dimensions={0} | all-to-all | bytes 131072 | tf_op jit(solution)/shard_map/all_to_all | solution.py:100
  102.9 0.1 shard_map.92
  103.0 2.5 %all-gather.2 = f32[4,24,128]{2,1,0:T(8,128)S(1)} all-gather(f32[2,24,128]{2,1,0:T(8,128)S(1)} %shard_map.92), channel_id=4, replica_groups=mesh['z'=16,'core'=2,'y'=4,'x'=4] {'core'}, dimensions={0}, use_global_device_ids=true | all-gather | bytes 73728 | tf_op jit(solution)/shard_map/all_gather | solution.py:424
  105.5 9.5 %all_to_all.34.got = f32[16,8,128]{2,1,0:T(8,128)S(1)} all-to-all(f32[16,8,128]{2,1,0:T(8,128)S(1)} %shard_map.93), channel_id=1, replica_groups={{10,11,12,13,14,15,0,1,2,3,4,5,6,7,8,9},{26,27,28,29,30,31,16,17,18,19,..., dimensions={0} | all-to-all | bytes 131072 | tf_op jit(solution)/shard_map/all_to_all | solution.py:100
  114.9 0.7 shard_map.94
  (1 shorter events, 0.0 us)
Async XLA Ops:
  2.7 17.5 %copy-start = (bf16[1536,64]{0,1:T(8,128)(2,1)S(1)}, bf16[1536,64]{0,1:T(8,128)(2,1)}, u32[]{:S(2)}) copy-start(bf16[1536,64]{0,1:T(8,128)(2,1)} %param.13) | copy-start | bytes 589828
  2.7 17.5 %copy-start.1 = (f32[64,64]{1,0:T(8,128)S(1)}, f32[64,64]{1,0:T(8,128)}, u32[]{:S(2)}) copy-start(f32[64,64]{1,0:T(8,128)} %start.5) | copy-start | bytes 49156
  2.7 17.5 %copy-start.2 = (bf16[64,1536]{1,0:T(8,128)(2,1)S(1)}, bf16[64,1536]{1,0:T(8,128)(2,1)}, u32[]{:S(2)}) copy-start(bf16[64,1536]{1,0:T(8,128)(2,1)} %w_in.1) | copy-start | bytes 589828
  2.7 17.5 %copy-start.3 = (bf16[1,3072]{1,0:T(2,128)(2,1)S(1)}, bf16[1,3072]{1,0:T(2,128)(2,1)}, u32[]{:S(2)}) copy-start(bf16[1,3072]{1,0:T(2,128)(2,1)} %modulation.1) | copy-start | bytes 18436
  2.7 17.5 %copy-start.4 = (s32[33]{0:T(128)S(1)}, s32[33]{0:T(128)}, u32[]{:S(2)}) copy-start(s32[33]{0:T(128)} %timesteps.1) | copy-start | bytes 400
  2.7 33.1 %all-to-all-start = ((bf16[16,80,128]{2,1,0:T(8,128)(2,1)}), bf16[16,80,128]{2,1,0:T(8,128)(2,1)S(1)}, u32[]{:S(2)}, u32[]{:S(2)}) async-start(bf16[16,80,128]{2,1,0:T(8,128)(2,1)} %shard_map.87), calls=%async_computation | async-start | bytes 655360 | tf_op jit(solution)/shard_map/all_to_all | solution.py:381
